TPU v7x, 128 devices: a whole 4x4x4 slice. The times are simulated.
128 devices in a mesh: sample: 8 (over z_hi, y), span: 16 (over x, z_lo, core).
Axes of the slice: x: 4, y: 4, z: 4 (z_hi: 2, z_lo: 2; z = z_hi * 2 + z_lo), core: 2. Of those that a mesh axis runs over, the one named last changes fastest.
Arguments:
- fields: float32 [3, 8, 128, 128, 193], P(None, 'sample', None, 'span'), may hold values from -1.5 to 1.5
- wiener: float32 [3, 8, 128, 128, 193], P(None, 'sample', None, 'span'), may hold values from -6 to 6
- velocity: float32 [3, 128, 128, 193], P(None, None, 'span'), may hold values from -6 to 6
- gradient: float32 [9, 128, 128, 193], P(None, None, 'span'), may hold values from -30 to 30
- wall_derivative: float32 [193, 193], replicated, may hold values from -4.2 to 4.2
- to_modes: float32 [193, 193], replicated, may hold values from -0.4375 to 0.4375
- from_modes: float32 [193, 193], replicated, may hold values from -0.4375 to 0.4375
- mode_rates: float32 [193], replicated, may hold values from 1 to 400
Outputs:
- new_fields: float32 [3, 8, 128, 128, 193], P(None, 'sample', None, 'span')
- new_velocity: float32 [3, 128, 128, 193], P(None, None, 'span')
- new_gradient: float32 [9, 128, 128, 193], P(None, None, 'span')
All inputs are finite; a program needn't handle non-finite values.
Results may differ from a plain program's by a relative error of at most 0.0001.
Values sent between devices are 32-bit elements; how exact they have to be, the bound alone decides.
No kernel may reach another device: no remote copies, remote signals or barrier semaphores. Data moves between devices by JAX's collectives and lax.ppermute only.
A program may use at most 192 MiB of HBM per device.

v0:
```python
import math

import jax
import jax.numpy as jnp
from jax import lax
from jax.sharding import PartitionSpec as P

TIME_STEP = 0.01
WEISSENBERG = 0.05
EXTENSIBILITY = 10.0
POLYMER_WEIGHT = 5.0
VISCOSITY = 0.5
DIFFUSIVITY = 0.003
LENGTH_X = math.pi
LENGTH_Z = 2.0 * math.pi / 3.0
PRECISE = lax.Precision.HIGHEST
FIRST_INDEX = (0, 0, 0, 1, 1, 2)
SECOND_INDEX = (0, 1, 2, 1, 2, 2)
IDENTITY_PAIRS = (1.0, 0.0, 0.0, 1.0, 0.0, 1.0)


def padded_2(cells, sides, width):
    for axis, dim in sides:
        count = lax.axis_size(axis)
        head = lax.slice_in_dim(cells, 0, width, axis=dim)
        tail = lax.slice_in_dim(cells, cells.shape[dim] - width, cells.shape[dim], axis=dim)
        cells = jnp.concatenate(
            [
                lax.ppermute(tail, axis, [(i, (i + 1) % count) for i in range(count)]),
                cells,
                lax.ppermute(head, axis, [((i + 1) % count, i) for i in range(count)]),
            ],
            axis=dim,
        )
    return cells


def phase_tables(wanted, places, period):
    product = wanted[:, None] * places[None, :] % period
    angles = product.astype(jnp.float32) * (2.0 * math.pi / period)
    return (jnp.cos(angles), jnp.sin(angles))


def wave_numbers(indices, period, extent, derivative):
    shifted = jnp.where(indices < period // 2, indices, indices - period)
    if derivative:
        shifted = jnp.where(indices == period // 2, 0, shifted)
    return shifted.astype(jnp.float32) * (2.0 * math.pi / extent)


def forward_x(stacked):
    period = stacked.shape[1]
    places = jnp.arange(period, dtype=jnp.int32)
    cosine_table, sine_table = phase_tables(places, places, period)
    weights_table = jnp.stack([cosine_table, -sine_table])
    return jnp.einsum("rkj,cjzy->rckzy", weights_table, stacked, precision=PRECISE)


def inverse_x(spectral):
    kept = spectral.shape[2]
    places = jnp.arange(kept, dtype=jnp.int32)
    wanted = jnp.arange(kept, dtype=jnp.int32)
    cosine_table, sine_table = phase_tables(wanted, places, kept)
    weights_table = jnp.stack([cosine_table, -sine_table])
    return jnp.einsum("rkj,rckzy->cjzy", weights_table, spectral, precision=PRECISE)


def forward_z(values, wanted, places, period, scaling):
    cosine_table, sine_table = phase_tables(wanted, places, period)
    weights_table = (
        jnp.stack([jnp.stack([cosine_table, -sine_table]), jnp.stack([sine_table, cosine_table])])
        * scaling
    )
    return jnp.einsum("rckzy,rswz->wscky", values, weights_table, precision=PRECISE)


def inverse_z(spectra, wanted, places, period):
    cosine_table, sine_table = phase_tables(wanted, places, period)
    weights_table = jnp.stack(
        [jnp.stack([cosine_table, sine_table]), jnp.stack([-sine_table, cosine_table])]
    )
    return jnp.einsum("wscky,srwz->rckzy", spectra, weights_table, precision=PRECISE)


def stress_from(moments, spring):
    identity = jnp.array(IDENTITY_PAIRS, jnp.float32)[:, None, None, None]
    return spring * moments - identity


def rotate(values, factor):
    return jnp.stack([-factor * values[:, 1], factor * values[:, 0]], axis=1)


def solve_modes(
    spectra,
    kx_index,
    kz_index,
    period_x,
    period_z,
    wall_derivative,
    to_modes,
    from_modes,
    mode_rates,
):
    kappa_x = wave_numbers(kx_index, period_x, LENGTH_X, False)
    kappa_z = wave_numbers(kz_index, period_z, LENGTH_Z, False)
    factor_x = wave_numbers(kx_index, period_x, LENGTH_X, True)[None, None, :, None]
    factor_z = wave_numbers(kz_index, period_z, LENGTH_Z, True)[:, None, None, None]

    def along_wall(values):
        return jnp.einsum("nrckw,yw->nrcky", values, wall_derivative, precision=PRECISE)

    stress = spectra[:, :, 0:6]
    velocity_hat = spectra[:, :, 6:9]
    column_x = stress[:, :, 0:3]
    column_y = jnp.stack([stress[:, :, 1], stress[:, :, 3], stress[:, :, 4]], axis=2)
    column_z = jnp.stack([stress[:, :, 2], stress[:, :, 4], stress[:, :, 5]], axis=2)
    divergence = rotate(column_x, factor_x) + along_wall(column_y) + rotate(column_z, factor_z)
    forcing = velocity_hat + TIME_STEP * POLYMER_WEIGHT * divergence
    modes = jnp.einsum("nrckw,mw->nrckm", forcing, to_modes, precision=PRECISE)
    damping = 1.0 + TIME_STEP * VISCOSITY * (
        (kappa_x * kappa_x)[None, None, None, :, None]
        + (kappa_z * kappa_z)[:, None, None, None, None]
        + mode_rates[None, None, None, None, :]
    )
    updated = jnp.einsum("nrckm,ym->nrcky", modes / damping, from_modes, precision=PRECISE)
    gradients = jnp.stack(
        [rotate(updated, factor_x), along_wall(updated), rotate(updated, factor_z)], axis=3
    )
    shape_now = updated.shape
    gradients = gradients.reshape(shape_now[0], 2, 9, shape_now[3], shape_now[4])
    return jnp.concatenate([updated, gradients], axis=2)


def on_device(
    fields, wiener, velocity, gradient, wall_derivative, to_modes, from_modes, mode_rates
):
    samples_here = fields.shape[1]
    size_x = fields.shape[2]
    slab_cells = fields.shape[3]
    size_y = fields.shape[4]
    sample_count = lax.axis_size("sample")
    span_count = lax.axis_size("span")
    size_z = slab_cells * span_count
    total_fields = samples_here * sample_count
    step_x = LENGTH_X / size_x
    step_z = LENGTH_Z / size_z
    local_square = jnp.sum(fields * fields, axis=(0, 1))
    mean_square = lax.psum(local_square, "sample") / total_fields
    spring = 1.0 / (1.0 - mean_square / EXTENSIBILITY)
    padded = padded_2(fields, (("span", 3),), 1)
    upper_cells = padded[:, :, :, 2:]
    lower_cells = padded[:, :, :, :-2]
    slope_z = (upper_cells - lower_cells) / (2.0 * step_z)
    curve_z = upper_cells - 2.0 * fields + lower_cells
    slope_x = (jnp.roll(fields, -1, axis=2) - jnp.roll(fields, 1, axis=2)) / (2.0 * step_x)
    slope_y = jnp.einsum("cfxzy,wy->cfxzw", fields, wall_derivative, precision=PRECISE)
    advect = velocity[0] * slope_x + velocity[1] * slope_y + velocity[2] * slope_z
    tensor = gradient.reshape(3, 3, size_x, slab_cells, size_y)
    stretch = (
        tensor[:, 0][:, None] * fields[0][None]
        + tensor[:, 1][:, None] * fields[1][None]
        + tensor[:, 2][:, None] * fields[2][None]
    )
    new_fields = fields + TIME_STEP * (stretch - advect - spring * fields / (2.0 * WEISSENBERG))
    new_fields = new_fields + DIFFUSIVITY * TIME_STEP / (step_z * step_z) * curve_z
    new_fields = new_fields + math.sqrt(TIME_STEP / WEISSENBERG) * wiener
    moments = jnp.stack(
        [
            jnp.sum(new_fields[FIRST_INDEX[p]] * new_fields[SECOND_INDEX[p]], axis=0)
            for p in range(6)
        ]
    )
    span_index = lax.axis_index("span")
    mode_count = size_x // span_count
    kx_index = span_index * mode_count + jnp.arange(mode_count, dtype=jnp.int32)
    scaling = 1.0 / (size_x * size_z)
    moments = lax.psum(moments, "sample") / total_fields
    stacked = jnp.concatenate([stress_from(moments, spring), velocity], axis=0)
    spectral_x = forward_x(stacked)
    swapped = lax.all_to_all(spectral_x, "span", split_axis=2, concat_axis=3, tiled=True)
    positions = jnp.arange(size_z, dtype=jnp.int32)
    spectra = forward_z(swapped, positions, positions, size_z, scaling)
    solved = solve_modes(
        spectra,
        kx_index,
        positions,
        size_x,
        size_z,
        wall_derivative,
        to_modes,
        from_modes,
        mode_rates,
    )
    physical_z = inverse_z(solved, positions, positions, size_z)
    returned = lax.all_to_all(physical_z, "span", split_axis=3, concat_axis=2, tiled=True)
    result = inverse_x(returned)
    return (new_fields, result[0:3], result[3:12])


def solution(mesh):
    in_specs = (
        P(None, "sample", None, "span", None),
        P(None, "sample", None, "span", None),
        P(None, None, "span", None),
        P(None, None, "span", None),
        P(),
        P(),
        P(),
        P(),
    )
    out_specs = (
        P(None, "sample", None, "span", None),
        P(None, None, "span", None),
        P(None, None, "span", None),
    )
    return jax.shard_map(
        on_device, mesh=mesh, in_specs=in_specs, out_specs=out_specs, check_vma=False
    )
```

profile of v0, /device:TPU:37, one launch (start us, length us, event | category | flops | bytes accessed | tf_op | source)
XLA Modules:
  0.0 1283.5 jit_solution(7870628112952978746)
XLA Ops:
  18.8 3.2 fusion.89
  37.2 56.6 %all-reduce.3.cloned.1.call-done = f32[128,8,193]{0,1,2:T(8,128)} async-done(((f32[128,8,193]{0,1,2:T(8,128)}), f32[128,8,193]{0,1,2:T(8,128)}) %all-reduce.3.cloned.1.call-update) | async-done | bytes 790544 | tf_op jit(solution)/shard_map/psum | solution.py:149
  96.3 14.5 %fusion.43 = f32[3,1,128,8,193]{2,4,3,0,1:T(8,128)S(1)} fusion(f32[3,1,128,8,193]{2,4,3,0,1:T(8,128)S(1)} %copy-done.7, f32[3,1,8,193]{1,3,2,0:T(8,128)} %copy.95, f32[3,127,8,193]{1,3,2,0:T(8,128)} %get-tuple-element.30, f32[3,127,8,193]{1,3,2,0:T(8,128)} %get-tuple-element.29, f32[3,1,8,193]{1,3,2,0:T(8,128)} %copy.98, ...), kind=kOutput, calls=%fused_computation.58 | convolution fusion | flops 1390341120 | bytes 27619844 | tf_op jit(solution)/shard_map/cfxzy,wy->cfxzw/dot_general | solution.py:157
  119.9 120.7 %all-reduce.5.cloned.1.call-done = f32[6,128,8,193]{1,3,2,0:T(8,128)} async-done(((f32[6,128,8,193]{1,3,2,0:T(8,128)}), f32[6,128,8,193]{1,3,2,0:T(8,128)}) %all-reduce.5.cloned.1.call-update) | async-done | bytes 4743184 | tf_op jit(solution)/shard_map/psum | solution.py:178
  243.5 14.1 %convolution_bitcast_fusion = f32[2,9,128,8,193]{2,4,0,3,1:T(8,128)} fusion(f32[3,128,8,193]{1,3,2,0:T(8,128)S(1)} %copy.117, f32[6,128,8,193]{1,3,2,0:T(8,128)S(1)} %multiply_add_fusion, f32[1,128,128]{2,1,0:T(8,128)S(1)} %get-tuple-element.47, f32[1,128,128]{2,1,0:T(8,128)S(1)} %copy-done.13), kind=kOutput, calls=%fused_computation.10 | convolution fusion | flops 5465940992 | bytes 21475328 | tf_op jit(solution)/shard_map/rkj,cjzy->rckzy/dot_general | solution.py:56
  257.7 27.0 %copy.118 = f32[2,9,128,8,193]{4,0,3,1,2:T(2,128)} copy(f32[2,9,128,8,193]{2,4,0,3,1:T(8,128)} %convolution_bitcast_fusion) | data formatting | bytes 28459008 | tf_op jit(solution)/shard_map/rkj,cjzy->rckzy/transpose | solution.py:56
  284.7 7.4 all-to-all-start
  293.9 305.4 %all-to-all-done = f32[2,9,128,8,193]{4,0,3,1,2:T(2,128)} async-done(((f32[2,9,128,8,193]{4,0,3,1,2:T(2,128)}), f32[2,9,128,8,193]{4,0,3,1,2:T(2,128)}, u32[]{:S(2)}, u32[]{:S(2)}) %all-to-all-start) | async-done | bytes 14229536 | tf_op jit(solution)/shard_map/all_to_all | solution.py:181
  599.2 16.2 %copy.119 = f32[2,9,128,8,193]{4,3,2,1,0:T(8,128)} copy(f32[2,9,128,8,193]{4,0,3,1,2:T(2,128)} %all-to-all-done) | data formatting | bytes 28459008 | tf_op jit(solution)/shard_map/all_to_all | solution.py:181
  615.4 34.5 %fusion.10 = f32[128,2,9,8,193]{0,4,3,2,1:T(8,128)S(1)} fusion(f32[2,9,8,16,8,193]{5,4,2,3,1,0:T(8,128)} %bitcast.153, f32[1,2,128,128]{3,2,1,0:T(8,128)S(1)} %get-tuple-element.42, f32[1,2,128,128]{3,2,1,0:T(8,128)S(1)} %get-tuple-element.45), kind=kOutput, calls=%fused_computation.15 | convolution fusion | flops 10928390144 | bytes 28721152 | tf_op jit(solution)/shard_map/rckzy,rswz->wscky/dot_general | solution.py:74
  654.5 5.2 fusion.19
  662.5 11.1 fusion.13
  673.6 6.9 fusion.26
  680.6 6.6 convolution_bitcast_fusion.1
  693.2 11.7 pad_maximum_fusion
  705.0 12.6 copy.124
  717.5 12.7 copy.126
  730.2 20.9 %fusion.9 = f32[2,12,8,128,193]{3,4,2,1,0:T(8,128)} fusion(f32[128,2,9,8,193]{0,4,1,3,2:T(8,128)} %copy.126, f32[128,2,3,8,193]{0,4,3,2,1:T(8,128)} %copy-done.3, f32[1,2,128,128]{3,2,1,0:T(8,128)S(1)} %get-tuple-element.46, f32[1,2,128,128]{3,2,1,0:T(8,128)S(1)} %get-tuple-element.41), kind=kOutput, calls=%fused_computation.14 | convolution fusion | flops 14575820800 | bytes 38207488 | tf_op jit(solution)/shard_map/wscky,srwz->rckzy/dot_general | solution.py:82
  751.2 24.8 %copy.128 = f32[2,12,8,128,193]{4,2,1,0,3:T(8,128)} copy(f32[2,12,8,128,193]{3,4,2,1,0:T(8,128)} %fusion.9) | data formatting | bytes 37945344 | tf_op jit(solution)/shard_map/wscky,srwz->rckzy/transpose | solution.py:82
  776.0 6.2 all-to-all-start.1
  784.0 410.2 %all-to-all-done.1 = f32[2,12,8,128,193]{4,2,1,0,3:T(8,128)} async-done(((f32[2,12,8,128,193]{4,2,1,0,3:T(8,128)}), f32[2,12,8,128,193]{4,2,1,0,3:T(8,128)}, u32[]{:S(2)}, u32[]{:S(2)}) %all-to-all-start.1) | async-done | bytes 18972704 | tf_op jit(solution)/shard_map/all_to_all | solution.py:196
  1194.2 24.8 %copy.130 = f32[2,12,16,8,8,193]{5,4,3,2,1,0:T(8,128)} copy(f32[2,12,16,8,8,193]{5,3,1,0,4,2:T(8,128)} %bitcast.61) | data formatting | bytes 37945344 | tf_op jit(solution)/shard_map/all_to_all | solution.py:196
  1219.0 50.7 %fusion.28 = f32[12,128,8,193]{1,3,2,0:T(8,128)S(1)} fusion(f32[2,12,128,8,193]{4,3,2,1,0:T(8,128)} %bitcast.151, f32[1,128,128]{2,1,0:T(8,128)S(1)} %get-tuple-element.47, f32[1,128,128]{2,1,0:T(8,128)S(1)} %copy-done.14), kind=kOutput, calls=%fused_computation.37 | convolution fusion | flops 7285538816 | bytes 28590080 | tf_op jit(solution)/shard_map/rkj,rckzy->cjzy/dot_general | solution.py:65
  1270.5 4.2 copy.134
  (102 shorter events, 60.5 us)
Async XLA Ops:
  7.2 89.1 %copy-start = (f32[193,193]{1,0:T(8,128)S(1)}, f32[193,193]{1,0:T(8,128)}, u32[]{:S(2)}) copy-start(f32[193,193]{1,0:T(8,128)} %param.13) | copy-start | bytes 446992
  7.2 3.1 copy-start.2
  7.2 86.6 %all-reduce.3.cloned.1.call-start = ((), (), s32[]{:S(2)}) async-start(), calls=%async_computation.2 | async-start | bytes 1581056 | tf_op jit(solution)/shard_map/psum | solution.py:149
  10.2 230.4 %all-reduce.5.cloned.1.call-start = ((), (), s32[]{:S(2)}) async-start(), calls=%async_computation.3 | async-start | bytes 9830400 | tf_op jit(solution)/shard_map/psum | solution.py:178
  10.7 5.0 copy-start.6
  11.7 84.5 %collective-permute-start.1 = (f32[3,1,128,1,193]{2,4,3,0,1:T(8,128)}, f32[3,1,128,1,193]{2,4,3,0,1:T(8,128)}, u32[]{:S(2)}, u32[]{:S(2)}) collective-permute-start(f32[3,1,128,1,193]{2,4,3,0,1:T(8,128)} %get-tuple-element.27), channel_id=1, source_target_pairs={{0,1},{1,2},{2,3},{3,4},{4,5},{5,6},{6,7},{7,8},{8,9},{9,10},{10,1... | collective-permute-start | bytes 889352 | tf_op jit(solution)/shard_map/ppermute | solution.py:29
  12.7 83.5 %collective-permute-start = (f32[3,1,128,1,193]{2,4,3,0,1:T(8,128)}, f32[3,1,128,1,193]{2,4,3,0,1:T(8,128)}, u32[]{:S(2)}, u32[]{:S(2)}) collective-permute-start(f32[3,1,128,1,193]{2,4,3,0,1:T(8,128)} %get-tuple-element.28), channel_id=1, source_target_pairs={{1,0},{2,1},{3,2},{4,3},{5,4},{6,5},{7,6},{8,7},{9,8},{10,9},{11,1... | collective-permute-start | bytes 889352 | tf_op jit(solution)/shard_map/ppermute | solution.py:31
  12.7 6.1 slice-start
  15.7 3.1 slice-start.1
  18.8 3.2 copy-start.10
  110.8 4.9 copy-start.4
  116.7 3.1 copy-start.12
  116.7 123.9 %copy-start.18 = (f32[6]{0:T(128)S(1)}, f32[6]{0:T(128)}, u32[]{:S(2)}) copy-start(f32[6]{0:T(128)} %constant.88) | copy-start | bytes 76
  240.6 2.9 copy-start.13
  284.7 7.5 copy-start.17
  284.7 314.5 %all-to-all-start = ((f32[2,9,128,8,193]{4,0,3,1,2:T(2,128)}), f32[2,9,128,8,193]{4,0,3,1,2:T(2,128)}, u32[]{:S(2)}, u32[]{:S(2)}) async-start(f32[2,9,128,8,193]{4,0,3,1,2:T(2,128)} %copy.118), calls=%async_computation | async-start | bytes 37748736 | tf_op jit(solution)/shard_map/all_to_all | solution.py:181
  651.7 2.7 copy-start.11
  659.7 2.7 copy-start.16
  662.5 11.1 copy-start.15
  662.5 11.1 copy-start.19
  680.6 6.7 copy-start.3
  776.0 6.2 copy-start.5
  776.0 418.2 %all-to-all-start.1 = ((f32[2,12,8,128,193]{4,2,1,0,3:T(8,128)}), f32[2,12,8,128,193]{4,2,1,0,3:T(8,128)}, u32[]{:S(2)}, u32[]{:S(2)}) async-start(f32[2,12,8,128,193]{4,2,1,0,3:T(8,128)} %copy.128), calls=%async_computation.1 | async-start | bytes 50331648 | tf_op jit(solution)/shard_map/all_to_all | solution.py:196
  1270.5 6.0 copy-start.1
  (4 other events, 9.3 us)
Sparse Core Ops, SparseCore 0:
  10.5 83.1 all-reduce.2
  116.8 123.7 all-reduce.4
where the time goes:
time: 1290 us; the launch traced here: 1280 us
  waiting for transfers between devices  893 us (69%)
  matrix products  165 us (13%)
  local copies, waits for them, and re-layouts  158 us (12%)
  other arithmetic  38.7 us (3%)
  starting transfers between devices  14.7 us (1%)
  between operations  14.7 us (1%)
    all_to_all x1, waiting for transfers between devices, on_device(): lax.all_to_all(physical_z, 'span', split_axis=3, concat_axis=2, tiled=True)  410 us
    all_to_all x1, waiting for transfers between devices, on_device(): lax.all_to_all(spectral_x, 'span', split_axis=2, concat_axis=3, tiled=True)  305 us
    psum x1, waiting for transfers between devices, on_device(): moments = lax.psum(moments, 'sample') / total_fields  121 us
    psum x1, waiting for transfers between devices, on_device(): mean_square = lax.psum(local_square, 'sample') / total_fields  56.6 us
    dot_general x1, matrix products, inverse_x(): jnp.einsum('rkj,rckzy->cjzy', weights_table, spectral, precision=PRECISE)  50.7 us
    dot_general x1, matrix products, forward_z(): jnp.einsum('rckzy,rswz->wscky', values, weights_table, precision=PRECISE)  34.5 us
    transpose x1, local copies, waits for them, and re-layouts, forward_x(): jnp.einsum('rkj,cjzy->rckzy', weights_table, stacked, precision=PRECISE)  27 us
  transfers between devices with their start and end apart: 6, of which 4 were waited for; matrix products, arithmetic and copies ran while one was open for 3% of the time, Pallas kernels for 0%

commit v1 on v0

v1 whole, which is shorter than its diff:
```python
import math

import jax
import jax.numpy as jnp
import numpy as np
from jax import lax
from jax.sharding import PartitionSpec as P

TIME_STEP = 0.01
WEISSENBERG = 0.05
EXTENSIBILITY = 10.0
POLYMER_WEIGHT = 5.0
VISCOSITY = 0.5
DIFFUSIVITY = 0.003
LENGTH_X = math.pi
LENGTH_Z = 2.0 * math.pi / 3.0
FULL = lax.Precision.HIGHEST
HIGH = lax.Precision.HIGH
BOTH = ("sample", "span")


def real_basis(count, extent):
    half = count // 2
    place = np.arange(count)
    rows = np.zeros((count, count))
    kappa = np.zeros(count)
    slope = np.zeros((count, count))
    unit = 2.0 * math.pi / extent
    rows[0] = math.sqrt(1.0 / count)
    for k in range(1, half):
        angle = 2.0 * math.pi * ((k * place) % count) / count
        rows[k] = math.sqrt(2.0 / count) * np.cos(angle)
        rows[half + k] = math.sqrt(2.0 / count) * np.sin(angle)
        kappa[k] = kappa[half + k] = unit * k
        slope[k, half + k] = unit * k
        slope[half + k, k] = -unit * k
    rows[half] = math.sqrt(1.0 / count) * (1.0 - 2.0 * (place % 2))
    kappa[half] = unit * half
    return rows, slope, kappa * kappa


def f32(values):
    return jnp.asarray(np.asarray(values, np.float32))


def spring_free(fields, wiener, velocity, gradient, wall_derivative, step_x, step_z):
    span_count = lax.axis_size("span")
    ahead = [(i, (i + 1) % span_count) for i in range(span_count)]
    back = [((i + 1) % span_count, i) for i in range(span_count)]
    below = lax.ppermute(fields[:, :, -1:], "span", ahead)
    above = lax.ppermute(fields[:, :, :1], "span", back)
    upper = jnp.concatenate([fields[:, :, 1:], above], axis=2)
    lower = jnp.concatenate([below, fields[:, :, :-1]], axis=2)
    slope_z = (upper - lower) / (2.0 * step_z)
    curve_z = upper - 2.0 * fields + lower
    slope_x = (jnp.roll(fields, -1, axis=1) - jnp.roll(fields, 1, axis=1)) / (2.0 * step_x)
    slope_y = jnp.einsum("cxzy,wy->cxzw", fields, wall_derivative, precision=HIGH)
    advect = velocity[0] * slope_x + velocity[1] * slope_y + velocity[2] * slope_z
    tensor = gradient.reshape((3, 3) + gradient.shape[1:])
    stretch = tensor[:, 0] * fields[0] + tensor[:, 1] * fields[1] + tensor[:, 2] * fields[2]
    result = fields + TIME_STEP * (stretch - advect)
    result = result + DIFFUSIVITY * TIME_STEP / (step_z * step_z) * curve_z
    return result + math.sqrt(TIME_STEP / WEISSENBERG) * wiener


def gathered(plane, count):
    parts = [
        lax.ppermute(plane, "sample", [(i, (i + k) % count) for i in range(count)])
        for k in range(count - 1, 0, -1)
    ] + [plane]
    twice = jnp.stack(parts + parts)
    start = (count - 1 - lax.axis_index("sample")) % count
    return lax.dynamic_slice_in_dim(twice, start, count, axis=0)


def on_device(
    fields, wiener, velocity, gradient, wall_derivative, to_modes, from_modes, mode_rates
):
    size_x, slab, size_y = fields.shape[2:]
    samples = lax.axis_size("sample")
    spans = lax.axis_size("span")
    size_z = slab * spans
    step_x = LENGTH_X / size_x
    step_z = LENGTH_Z / size_z
    coupling = TIME_STEP * POLYMER_WEIGHT
    relax = TIME_STEP / (2.0 * WEISSENBERG)

    rows_x, slope_rows_x, square_x = real_basis(size_x, LENGTH_X)
    rows_z, slope_rows_z, square_z = real_basis(size_z, LENGTH_Z)
    order = np.array([slab * (d % spans) + d // spans for d in range(samples * spans)])

    field = fields[:, 0]
    field_planes = lax.all_to_all(
        jnp.transpose(field, (2, 0, 3, 1)), "sample", 0, 0, tiled=True
    )
    free = spring_free(
        field, wiener[:, 0], velocity, gradient, wall_derivative, step_x, step_z
    )
    free_planes = lax.all_to_all(
        jnp.transpose(free, (2, 0, 3, 1)), "sample", 0, 0, tiled=True
    )

    plane_square = jnp.sum(field_planes * field_planes, axis=(0, 1)) / samples
    spring = 1.0 / (1.0 - plane_square / EXTENSIBILITY)
    moved = free_planes - relax * spring * field_planes

    def stress(a, b):
        product = jnp.sum(moved[:, a] * moved[:, b], axis=0) / samples
        value = spring * product
        return value - 1.0 if a == b else value

    t00, t01, t02 = stress(0, 0), stress(0, 1), stress(0, 2)
    t11, t12, t22 = stress(1, 1), stress(1, 2), stress(2, 2)
    own_velocity = lax.dynamic_index_in_dim(
        velocity, lax.axis_index("sample"), 2, keepdims=False
    )
    modes_slope = coupling * jnp.dot(to_modes, wall_derivative, precision=FULL)
    modes_scaled = coupling * to_modes
    column_x = jnp.stack([t00, t01, t02])
    column_y = jnp.stack([t01, t11, t12])
    column_z = jnp.stack([t02, t12, t22])
    direct = jnp.einsum("my,cxy->cmx", to_modes, own_velocity, precision=FULL) + jnp.einsum(
        "my,cyx->cmx", modes_slope, column_y, precision=FULL
    )
    along_x = jnp.einsum("my,cyx->cmx", modes_scaled, column_x, precision=FULL)
    along_z = jnp.einsum("my,cyx->cmx", modes_scaled, column_z, precision=FULL)
    table_x = f32(np.concatenate([rows_x, slope_rows_x @ rows_x], axis=1))
    force = jnp.einsum(
        "rx,cmx->rcm", table_x, jnp.concatenate([direct, along_x], axis=2), precision=FULL
    )
    force_z = jnp.einsum("rx,cmx->rcm", f32(rows_x), along_z, precision=FULL)
    message = jnp.concatenate([force, force_z], axis=1)
    spectra = lax.all_to_all(message, BOTH, 0, 0, tiled=True)

    row = lax.axis_index("sample") * spans + lax.axis_index("span")
    square_row = lax.dynamic_index_in_dim(f32(square_x), row, 0, keepdims=False)
    table_f = f32(rows_z[:, order])
    table_g = f32((slope_rows_z @ rows_z)[:, order])
    solved = jnp.einsum("kz,zcm->kcm", table_f, spectra[:, :3], precision=FULL) + jnp.einsum(
        "kz,zcm->kcm", table_g, spectra[:, 3:], precision=FULL
    )
    damping = 1.0 + TIME_STEP * VISCOSITY * (
        square_row + f32(square_z)[:, None] + mode_rates[None, :]
    )
    solved = solved / damping[:, None, :]
    back_table = np.stack([rows_z.T, rows_z.T @ slope_rows_z]).reshape(2, spans, slab, size_z)
    back = jnp.einsum("dpzk,kcm->pdczm", f32(back_table), solved, precision=FULL)
    back, late_spring = lax.optimization_barrier((back, spring))
    slab_spring = gathered(late_spring, samples)
    back = jnp.broadcast_to(back[None], (samples,) + back.shape)
    back = back.reshape((samples * spans, 6, slab, size_y))
    rows = lax.all_to_all(back, BOTH, 0, 0, tiled=True)

    modes_wall = jnp.dot(wall_derivative, from_modes, precision=FULL)
    value = jnp.einsum("rczm,ym->rczy", rows, from_modes, precision=HIGH)
    value_y = jnp.einsum("rczm,ym->rczy", rows[:, :3], modes_wall, precision=HIGH)
    inverse = f32(rows_x.T)
    inverse_slope = f32(rows_x.T @ slope_rows_x)
    values = jnp.einsum("xr,rczy->cxzy", inverse, value, precision=HIGH)
    slope_x = jnp.einsum("xr,rczy->cxzy", inverse_slope, value[:, :3], precision=HIGH)
    slope_y = jnp.einsum("xr,rczy->cxzy", inverse, value_y, precision=HIGH)
    new_velocity = values[:3]
    new_gradient = jnp.stack([slope_x, slope_y, values[3:]], axis=1)
    new_gradient = new_gradient.reshape((9,) + new_gradient.shape[2:])

    new_fields = free - relax * jnp.transpose(slab_spring, (2, 0, 1)) * field
    return (new_fields[:, None], new_velocity, new_gradient)


def solution(mesh):
    in_specs = (
        P(None, "sample", None, "span", None),
        P(None, "sample", None, "span", None),
        P(None, None, "span", None),
        P(None, None, "span", None),
        P(),
        P(),
        P(),
        P(),
    )
    out_specs = (
        P(None, "sample", None, "span", None),
        P(None, None, "span", None),
        P(None, None, "span", None),
    )
    return jax.shard_map(
        on_device, mesh=mesh, in_specs=in_specs, out_specs=out_specs, check_vma=False
    )
```

time: 1290 us -> 266 us (0.21)
  the two profiles are of different devices: /device:TPU:37 before, /device:TPU:5 now
where the time goes in v1:
time: 266 us; the launch traced here: 265 us
  waiting for transfers between devices  116 us (44%)
  starting transfers between devices  61.2 us (23%)
  local copies, waits for them, and re-layouts  47.4 us (18%)
  matrix products  30.1 us (11%)
  other arithmetic  9.49 us (4%)
    ppermute x7, waiting for transfers between devices, gathered(): lax.ppermute(plane, 'sample', [(i, (i + k) % count) for i in range(count)])  70.2 us
    all_to_all x1, waiting for transfers between devices, on_device(): lax.all_to_all(jnp.transpose(free, (2, 0, 3, 1)), 'sample', 0, 0, tiled=T...  25.8 us
    ppermute x7, starting transfers between devices, gathered(): lax.ppermute(plane, 'sample', [(i, (i + k) % count) for i in range(count)])  20.7 us
    all_to_all x1, waiting for transfers between devices, on_device(): spectra = lax.all_to_all(message, BOTH, 0, 0, tiled=True)  14.7 us
    all_to_all x1, starting transfers between devices, on_device(): spectra = lax.all_to_all(message, BOTH, 0, 0, tiled=True)  14.2 us
    dot_general x1, matrix products, spring_free(): jnp.einsum('cxzy,wy->cxzw', fields, wall_derivative, precision=HIGH)  10.3 us
    all_to_all x1, starting transfers between devices, on_device(): lax.all_to_all(jnp.transpose(free, (2, 0, 3, 1)), 'sample', 0, 0, tiled=T...  10.2 us
    unnamed x66, local copies, waits for them, and re-layouts  10.1 us
  transfers between devices with their start and end apart: 13, of which 7 were waited for; matrix products, arithmetic and copies ran while one was open for 14% of the time, Pallas kernels for 0%

profile of v1, /device:TPU:5, one launch (start us, length us, event | category | flops | bytes accessed | tf_op | source)
XLA Modules:
  0.0 265.3 jit_solution(2929129293725694031)
XLA Ops:
  0.7 2.2 copy.119
  7.9 7.2 %all-to-all-start = ((f32[8,3,193,128]{3,2,1,0:T(8,128)}), f32[8,3,193,128]{3,2,1,0:T(8,128)}, u32[]{:S(2)}, u32[]{:S(2)}) async-start(f32[8,3,193,128]{3,2,1,0:T(8,128)} %copy.60), calls=%async_computation | async-start | bytes 4915200 | tf_op jit(solution)/shard_map/all_to_all | solution.py:93
  15.1 3.0 %fusion.60 = (f32[3,1,8,193]{1,3,2,0:T(8,128)}, f32[3,1,8,193]{1,3,2,0:T(8,128)}) fusion(f32[3,128,8,193]{1,3,2,0:T(8,128)S(1)} %bitcast.182), kind=kLoop, calls=%fused_computation.125 | loop fusion | bytes 74112 | tf_op jit(solution)/shard_map/jit(_roll_static)/slice | solution.py:56
  18.1 3.0 %fusion.61 = (f32[3,127,8,193]{1,3,2,0:T(8,128)}, f32[3,127,8,193]{1,3,2,0:T(8,128)}) fusion(f32[3,128,8,193]{1,3,2,0:T(8,128)S(1)} %bitcast.183), kind=kLoop, calls=%fused_computation.126 | loop fusion | bytes 9412224 | tf_op jit(solution)/shard_map/jit(_roll_static)/slice | solution.py:56
  26.0 3.1 %fusion.57 = (f32[3,1,128,8,193]{2,3,4,1,0:T(8,128)}, f32[3,1,128,8,193]{2,3,4,1,0:T(8,128)}, f32[3,1,128,8,193]{2,3,4,1,0:T(8,128)}) fusion(f32[3,3,128,8,193]{2,3,4,1,0:T(8,128)S(1)} %bitcast.192), kind=kLoop, calls=%fused_computation.122 | loop fusion | bytes 14229504 | tf_op jit(solution)/shard_map/slice | solution.py:60
  30.7 10.3 %fusion.7 = f32[3,128,8,193]{1,3,2,0:T(8,128)S(1)} fusion(f32[3,1,8,193]{1,3,2,0:T(8,128)} %get-tuple-element.32, f32[3,127,8,193]{1,3,2,0:T(8,128)} %get-tuple-element.34, f32[3,127,8,193]{1,3,2,0:T(8,128)} %get-tuple-element.33, f32[3,1,8,193]{1,3,2,0:T(8,128)} %get-tuple-element.31, f32[3,1,128,8,193]{2,3,4,1,0:T(8,128)} %get-tuple-element.24, ...), kind=kOutput, calls=%fused_computation.10 | convolution fusion | flops 701988864 | bytes 28608004 | tf_op jit(solution)/shard_map/cxzy,wy->cxzw/dot_general | solution.py:57
  42.6 5.2 %all-to-all-done = f32[8,3,193,128]{3,2,1,0:T(8,128)} async-done(((f32[8,3,193,128]{3,2,1,0:T(8,128)}), f32[8,3,193,128]{3,2,1,0:T(8,128)}, u32[]{:S(2)}, u32[]{:S(2)}) %all-to-all-start) | async-done | bytes 2371616 | tf_op jit(solution)/shard_map/all_to_all | solution.py:93
  47.8 10.2 %all-to-all-start.1 = ((f32[8,3,193,128]{3,2,1,0:T(8,128)}), f32[8,3,193,128]{3,2,1,0:T(8,128)}, u32[]{:S(2)}, u32[]{:S(2)}) async-start(f32[8,3,193,128]{3,2,1,0:T(8,128)} %copy.61), calls=%async_computation.1 | async-start | bytes 4915200 | tf_op jit(solution)/shard_map/all_to_all | solution.py:99
  64.7 25.8 %all-to-all-done.1 = f32[8,3,193,128]{3,2,1,0:T(8,128)} async-done(((f32[8,3,193,128]{3,2,1,0:T(8,128)}), f32[8,3,193,128]{3,2,1,0:T(8,128)}, u32[]{:S(2)}, u32[]{:S(2)}) %all-to-all-start.1) | async-done | bytes 2371616 | tf_op jit(solution)/shard_map/all_to_all | solution.py:99
  90.5 2.7 %multiply_subtract_fusion = f32[8,3,193,128]{3,2,1,0:T(8,128)S(1)} fusion(f32[8,3,193,128]{3,2,1,0:T(8,128)} %all-to-all-done.1, f32[8,3,193,128]{3,2,1,0:T(8,128)} %all-to-all-done, f32[193,128]{1,0:T(8,128)S(1)} %get-tuple-element.44), kind=kLoop, calls=%fused_computation.24 | loop fusion | flops 1185792 | bytes 7213568 | tf_op jit(solution)/shard_map/sub | solution.py:105
  99.1 14.2 %all-to-all-start.2 = ((f32[128,6,193]{2,1,0:T(8,128)}), f32[128,6,193]{2,1,0:T(8,128)}, u32[]{:S(2)}, u32[]{:S(2)}) async-start(f32[128,6,193]{2,1,0:T(8,128)} %copy.62), calls=%async_computation.2 | async-start | bytes 2097152 | tf_op jit(solution)/shard_map/all_to_all | solution.py:133
  115.9 14.7 %all-to-all-done.2 = f32[128,6,193]{2,1,0:T(8,128)} async-done(((f32[128,6,193]{2,1,0:T(8,128)}), f32[128,6,193]{2,1,0:T(8,128)}, u32[]{:S(2)}, u32[]{:S(2)}) %all-to-all-start.2) | async-done | bytes 592928 | tf_op jit(solution)/shard_map/all_to_all | solution.py:133
  136.6 3.5 %broadcast_in_dim.5 = f32[8,16,2,3,8,193]{5,4,3,2,1,0:T(8,128)} broadcast(f32[16,2,3,8,193]{4,3,2,1,0:T(8,128)S(1)} %copy.65), dimensions={1,2,3,4,5} | broadcast | bytes 5336064 | tf_op jit(solution)/shard_map/broadcast_in_dim | solution.py:150
  140.1 6.7 %all-to-all-start.3 = ((f32[128,6,8,193]{3,2,1,0:T(8,128)}), f32[128,6,8,193]{3,2,1,0:T(8,128)}, u32[]{:S(2)}, u32[]{:S(2)}) async-start(f32[128,6,8,193]{3,2,1,0:T(8,128)} %bitcast.188), calls=%async_computation.3 | async-start | bytes 12582912 | tf_op jit(solution)/shard_map/all_to_all | solution.py:152
  146.8 5.6 %collective-permute-start.2 = (f32[193,128]{1,0:T(8,128)S(1)}, f32[193,128]{1,0:T(8,128)S(1)}, u32[]{:S(2)}, u32[]{:S(2)}) collective-permute-start(f32[193,128]{1,0:T(8,128)S(1)} %copy-done.8), channel_id=1, source_target_pairs={{0,112},{16,0},{32,16},{48,32},{64,48},{80,64},{96,80},{112,96},{1... | collective-permute-start | bytes 296456 | tf_op jit(solution)/shard_map/ppermute | solution.py:68
  153.4 3.2 %collective-permute-start.5 = (f32[193,128]{1,0:T(8,128)S(1)}, f32[193,128]{1,0:T(8,128)S(1)}, u32[]{:S(2)}, u32[]{:S(2)}) collective-permute-start(f32[193,128]{1,0:T(8,128)S(1)} %copy-done.8), channel_id=1, source_target_pairs={{0,64},{16,80},{32,96},{48,112},{64,0},{80,16},{96,32},{112,48},{1... | collective-permute-start | bytes 296456 | tf_op jit(solution)/shard_map/ppermute | solution.py:68
  156.6 60.3 %collective-permute-done.2 = f32[193,128]{1,0:T(8,128)S(1)} collective-permute-done((f32[193,128]{1,0:T(8,128)S(1)}, f32[193,128]{1,0:T(8,128)S(1)}, u32[]{:S(2)}, u32[]{:S(2)}) %collective-permute-start.2) | collective-permute-done | bytes 98848 | tf_op jit(solution)/shard_map/ppermute | solution.py:68
  217.0 9.5 %collective-permute-start.7 = (f32[193,128]{1,0:T(8,128)S(1)}, f32[193,128]{1,0:T(8,128)S(1)}, u32[]{:S(2)}, u32[]{:S(2)}) collective-permute-start(f32[193,128]{1,0:T(8,128)S(1)} %copy-done.8), channel_id=1, source_target_pairs={{0,32},{16,48},{32,64},{48,80},{64,96},{80,112},{96,0},{112,16},{1... | collective-permute-start | bytes 296456 | tf_op jit(solution)/shard_map/ppermute | solution.py:68
  228.3 6.3 %collective-permute-done.6 = f32[193,128]{1,0:T(8,128)S(1)} collective-permute-done((f32[193,128]{1,0:T(8,128)S(1)}, f32[193,128]{1,0:T(8,128)S(1)}, u32[]{:S(2)}, u32[]{:S(2)}) %collective-permute-start.6) | collective-permute-done | bytes 98848 | tf_op jit(solution)/shard_map/ppermute | solution.py:68
  235.8 2.4 collective-permute-done.8
  240.9 6.2 %copy.66 = f32[128,6,8,193]{0,3,2,1:T(8,128)} copy(f32[128,6,8,193]{3,2,1,0:T(8,128)} %all-to-all-done.3) | data formatting | bytes 9486336 | tf_op jit(solution)/shard_map/all_to_all | solution.py:152
  247.1 4.9 %fusion.41 = f32[128,6,8,193]{0,3,2,1:T(8,128)S(1)} fusion(f32[128,6,8,193]{0,3,2,1:T(8,128)} %copy.66, f32[193,193]{1,0:T(8,128)S(1)} %copy-done), kind=kOutput, calls=%fused_computation.79 | convolution fusion | flops 1373147136 | bytes 9635332 | tf_op jit(solution)/shard_map/rczm,ym->rczy/dot_general | solution.py:155
  252.0 2.2 convolution_bitcast_fusion
  259.3 4.2 %copy.68 = f32[3,3,128,8,193]{2,3,4,1,0:T(8,128)} copy(f32[3,3,128,8,193]{2,4,3,0,1:T(8,128)S(1)} %pad_maximum_fusion) | data formatting | bytes 14229504 | tf_op jit(solution)/shard_map/stack | solution.py:163
  (123 shorter events, 47.2 us)
Async XLA Ops:
  0.6 151.8 %copy-start = (f32[193,193]{1,0:T(8,128)S(1)}, f32[193,193]{1,0:T(8,128)}, u32[]{:S(2)}) copy-start(f32[193,193]{1,0:T(8,128)} %param.23) | copy-start | bytes 446992
  0.6 5.4 %copy-start.1 = (f32[3,1,128,8,193]{2,3,4,1,0:T(8,128)S(1)}, f32[3,1,128,8,193]{2,3,4,1,0:T(8,128)}, u32[]{:S(2)}) copy-start(f32[3,1,128,8,193]{2,3,4,1,0:T(8,128)} %param.17) | copy-start | bytes 7114756
  3.8 26.9 %collective-permute-start = (f32[3,128,1,193]{1,3,2,0:T(8,128)}, f32[3,128,1,193]{1,3,2,0:T(8,128)S(1)}, u32[]{:S(2)}, u32[]{:S(2)}) collective-permute-start(f32[3,128,1,193]{1,3,2,0:T(8,128)} %get-tuple-element.29), channel_id=1, source_target_pairs={{1,0},{2,1},{3,2},{4,3},{5,4},{6,5},{7,6},{8,7},{9,8},{10,9},{11,1... | collective-permute-start | bytes 889352 | tf_op jit(solution)/shard_map/ppermute | solution.py:51
  4.5 26.2 %collective-permute-start.1 = (f32[3,128,1,193]{1,3,2,0:T(8,128)}, f32[3,128,1,193]{1,3,2,0:T(8,128)S(1)}, u32[]{:S(2)}, u32[]{:S(2)}) collective-permute-start(f32[3,128,1,193]{1,3,2,0:T(8,128)} %get-tuple-element.30), channel_id=1, source_target_pairs={{0,1},{1,2},{2,3},{3,4},{4,5},{5,6},{6,7},{7,8},{8,9},{9,10},{10,1... | collective-permute-start | bytes 889352 | tf_op jit(solution)/shard_map/ppermute | solution.py:50
  7.9 39.9 %all-to-all-start = ((f32[8,3,193,128]{3,2,1,0:T(8,128)}), f32[8,3,193,128]{3,2,1,0:T(8,128)}, u32[]{:S(2)}, u32[]{:S(2)}) async-start(f32[8,3,193,128]{3,2,1,0:T(8,128)} %copy.60), calls=%async_computation | async-start | bytes 4915200 | tf_op jit(solution)/shard_map/all_to_all | solution.py:93
  42.6 17.3 %copy-start.4 = (f32[193,193]{1,0:T(8,128)S(1)}, f32[193,193]{1,0:T(8,128)}, u32[]{:S(2)}) copy-start(f32[193,193]{1,0:T(8,128)} %param.22) | copy-start | bytes 446992
  47.8 42.7 %all-to-all-start.1 = ((f32[8,3,193,128]{3,2,1,0:T(8,128)}), f32[8,3,193,128]{3,2,1,0:T(8,128)}, u32[]{:S(2)}, u32[]{:S(2)}) async-start(f32[8,3,193,128]{3,2,1,0:T(8,128)} %copy.61), calls=%async_computation.1 | async-start | bytes 4915200 | tf_op jit(solution)/shard_map/all_to_all | solution.py:99
  64.0 29.2 %copy-start.9 = (f32[193,128]{1,0:T(8,128)}, f32[193,128]{1,0:T(8,128)S(1)}, u32[]{:S(2)}) copy-start(f32[193,128]{1,0:T(8,128)S(1)} %multiply_reduce_fusion) | copy-start | bytes 296452
  97.6 16.9 %copy-start.19 = (f32[128]{0:T(128)S(1)}, f32[128]{0:T(128)}, u32[]{:S(2)}) copy-start(f32[128]{0:T(128)} %constant.108.clone) | copy-start | bytes 1540
  97.6 17.5 %copy-start.17 = (f32[193]{0:T(256)S(1)}, f32[193]{0:T(256)}, u32[]{:S(2)}) copy-start(f32[193]{0:T(256)} %param.24) | copy-start | bytes 2320
  99.1 33.4 %copy-start.15 = (f32[128,128,1]{1,0,2:T(8,128)S(1)}, f32[128,128,1]{1,0,2:T(8,128)}, u32[]{:S(2)}) copy-start(f32[128,128,1]{1,0,2:T(8,128)} %constant.118) | copy-start | bytes 196612
  99.1 34.4 %copy-start.18 = (f32[128,128,1]{1,0,2:T(8,128)S(1)}, f32[128,128,1]{1,0,2:T(8,128)}, u32[]{:S(2)}) copy-start(f32[128,128,1]{1,0,2:T(8,128)} %constant.119) | copy-start | bytes 196612
  99.1 31.5 %all-to-all-start.2 = ((f32[128,6,193]{2,1,0:T(8,128)}), f32[128,6,193]{2,1,0:T(8,128)}, u32[]{:S(2)}, u32[]{:S(2)}) async-start(f32[128,6,193]{2,1,0:T(8,128)} %copy.62), calls=%async_computation.2 | async-start | bytes 2097152 | tf_op jit(solution)/shard_map/all_to_all | solution.py:133
  140.1 6.8 %copy-start.8 = (f32[193,128]{1,0:T(8,128)S(1)}, f32[193,128]{1,0:T(8,128)}, u32[]{:S(2)}) copy-start(f32[193,128]{1,0:T(8,128)} %get-tuple-element.5) | copy-start | bytes 296452
  140.1 100.8 %all-to-all-start.3 = ((f32[128,6,8,193]{3,2,1,0:T(8,128)}), f32[128,6,8,193]{3,2,1,0:T(8,128)}, u32[]{:S(2)}, u32[]{:S(2)}) async-start(f32[128,6,8,193]{3,2,1,0:T(8,128)} %bitcast.188), calls=%async_computation.3 | async-start | bytes 12582912 | tf_op jit(solution)/shard_map/all_to_all | solution.py:152
  146.8 70.1 %collective-permute-start.2 = (f32[193,128]{1,0:T(8,128)S(1)}, f32[193,128]{1,0:T(8,128)S(1)}, u32[]{:S(2)}, u32[]{:S(2)}) collective-permute-start(f32[193,128]{1,0:T(8,128)S(1)} %copy-done.8), channel_id=1, source_target_pairs={{0,112},{16,0},{32,16},{48,32},{64,48},{80,64},{96,80},{112,96},{1... | collective-permute-start | bytes 296456 | tf_op jit(solution)/shard_map/ppermute | solution.py:68
  152.8 85.6 %copy-start.3 = (f32[3,1,128,8,193]{2,3,4,1,0:T(8,128)S(1)}, f32[3,1,128,8,193]{2,3,4,1,0:T(8,128)}, u32[]{:S(2)}) copy-start(f32[3,1,128,8,193]{2,3,4,1,0:T(8,128)} %param.17) | copy-start | bytes 7114756
  152.8 73.7 %collective-permute-start.3 = (f32[193,128]{1,0:T(8,128)S(1)}, f32[193,128]{1,0:T(8,128)S(1)}, u32[]{:S(2)}, u32[]{:S(2)}) collective-permute-start(f32[193,128]{1,0:T(8,128)S(1)} %copy-done.8), channel_id=1, source_target_pairs={{0,96},{16,112},{32,0},{48,16},{64,32},{80,48},{96,64},{112,80},{1... | collective-permute-start | bytes 296456 | tf_op jit(solution)/shard_map/ppermute | solution.py:68
  153.3 74.9 %collective-permute-start.4 = (f32[193,128]{1,0:T(8,128)S(1)}, f32[193,128]{1,0:T(8,128)S(1)}, u32[]{:S(2)}, u32[]{:S(2)}) collective-permute-start(f32[193,128]{1,0:T(8,128)S(1)} %copy-done.8), channel_id=1, source_target_pairs={{0,80},{16,96},{32,112},{48,0},{64,16},{80,32},{96,48},{112,64},{1... | collective-permute-start | bytes 296456 | tf_op jit(solution)/shard_map/ppermute | solution.py:68
  153.4 74.8 %collective-permute-start.5 = (f32[193,128]{1,0:T(8,128)S(1)}, f32[193,128]{1,0:T(8,128)S(1)}, u32[]{:S(2)}, u32[]{:S(2)}) collective-permute-start(f32[193,128]{1,0:T(8,128)S(1)} %copy-done.8), channel_id=1, source_target_pairs={{0,64},{16,80},{32,96},{48,112},{64,0},{80,16},{96,32},{112,48},{1... | collective-permute-start | bytes 296456 | tf_op jit(solution)/shard_map/ppermute | solution.py:68
  156.6 78.0 %collective-permute-start.6 = (f32[193,128]{1,0:T(8,128)S(1)}, f32[193,128]{1,0:T(8,128)S(1)}, u32[]{:S(2)}, u32[]{:S(2)}) collective-permute-start(f32[193,128]{1,0:T(8,128)S(1)} %copy-done.8), channel_id=1, source_target_pairs={{0,48},{16,64},{32,80},{48,96},{64,112},{80,0},{96,16},{112,32},{1... | collective-permute-start | bytes 296456 | tf_op jit(solution)/shard_map/ppermute | solution.py:68
  217.0 18.8 %collective-permute-start.7 = (f32[193,128]{1,0:T(8,128)S(1)}, f32[193,128]{1,0:T(8,128)S(1)}, u32[]{:S(2)}, u32[]{:S(2)}) collective-permute-start(f32[193,128]{1,0:T(8,128)S(1)} %copy-done.8), channel_id=1, source_target_pairs={{0,32},{16,48},{32,64},{48,80},{64,96},{80,112},{96,0},{112,16},{1... | collective-permute-start | bytes 296456 | tf_op jit(solution)/shard_map/ppermute | solution.py:68
  226.5 11.6 %collective-permute-start.8 = (f32[193,128]{1,0:T(8,128)S(1)}, f32[193,128]{1,0:T(8,128)S(1)}, u32[]{:S(2)}, u32[]{:S(2)}) collective-permute-start(f32[193,128]{1,0:T(8,128)S(1)} %copy-done.8), channel_id=1, source_target_pairs={{0,16},{16,32},{32,48},{48,64},{64,80},{80,96},{96,112},{112,0},{1... | collective-permute-start | bytes 296456 | tf_op jit(solution)/shard_map/ppermute | solution.py:68
  247.1 5.0 %copy-start.11 = (f32[128,128,1,1]{1,0,3,2:T(8,128)S(1)}, f32[128,128,1,1]{1,0,3,2:T(8,128)}, u32[]{:S(2)}) copy-start(f32[128,128,1,1]{1,0,3,2:T(8,128)} %constant.121) | copy-start | bytes 196612
  (13 other events, 32.8 us)

commit v2 on v1

v2 whole, which is shorter than its diff:
```python
import functools
import math

import jax
import jax.numpy as jnp
import numpy as np
from jax import lax
from jax.experimental import pallas as pl
from jax.experimental.pallas import tpu as pltpu
from jax.sharding import PartitionSpec as P

TIME_STEP = 0.01
WEISSENBERG = 0.05
EXTENSIBILITY = 10.0
POLYMER_WEIGHT = 5.0
VISCOSITY = 0.5
DIFFUSIVITY = 0.003
LENGTH_X = math.pi
LENGTH_Z = 2.0 * math.pi / 3.0
FULL = lax.Precision.HIGHEST
HIGH = lax.Precision.HIGH
BOTH = ("sample", "span")
LANES = 256
PAIRS = ((0, 0), (0, 1), (0, 2), (1, 1), (1, 2), (2, 2))
COLUMN = ((0, 1, 2), (1, 3, 4), (2, 4, 5))


def real_basis(count, extent):
    half = count // 2
    place = np.arange(count)
    rows = np.zeros((count, count))
    kappa = np.zeros(count)
    slope = np.zeros((count, count))
    unit = 2.0 * math.pi / extent
    rows[0] = math.sqrt(1.0 / count)
    for k in range(1, half):
        angle = 2.0 * math.pi * ((k * place) % count) / count
        rows[k] = math.sqrt(2.0 / count) * np.cos(angle)
        rows[half + k] = math.sqrt(2.0 / count) * np.sin(angle)
        kappa[k] = kappa[half + k] = unit * k
        slope[k, half + k] = unit * k
        slope[half + k, k] = -unit * k
    rows[half] = math.sqrt(1.0 / count) * (1.0 - 2.0 * (place % 2))
    kappa[half] = unit * half
    return rows, slope, kappa * kappa


def f32(values):
    return jnp.asarray(np.asarray(values, np.float32))


def free_kernel(scales, f_ref, w_ref, v_ref, g_ref, lo_ref, hi_ref, d_ref, o_ref):
    scale_x, scale_z, scale_c, scale_w = scales
    i = pl.program_id(0)
    slab, _, size_y, size_x = f_ref.shape
    noise, speed, tensor = [
        r.reshape(r.shape[0], size_y * slab, size_x) for r in (w_ref, v_ref, g_ref)
    ]
    for z in range(slab):
        plane = pl.ds(z, size_y, stride=slab)
        own = f_ref[z, i]
        upper = hi_ref[i] if z == slab - 1 else f_ref[z + 1, i]
        lower = lo_ref[i] if z == 0 else f_ref[z - 1, i]
        slope_x = pltpu.roll(own, size_x - 1, 1) - pltpu.roll(own, 1, 1)
        slope_y = full_dot(d_ref[...], own)
        advect = (
            speed[0, plane, :] * (scale_x * slope_x)
            + speed[1, plane, :] * slope_y
            + speed[2, plane, :] * (scale_z * (upper - lower))
        )
        stretch = (
            tensor[0, plane, :] * f_ref[z, 0]
            + tensor[1, plane, :] * f_ref[z, 1]
            + tensor[2, plane, :] * f_ref[z, 2]
        )
        result = own + TIME_STEP * (stretch - advect)
        result = result + scale_c * (upper - 2.0 * own + lower)
        o_ref[z, 0] = result + scale_w * noise[0, plane, :]


def spring_free(planes, wiener, velocity, gradient, below, above, wall_derivative, step_x, step_z):
    slab, _, size_y, size_x = planes.shape
    whole = pl.BlockSpec(memory_space=pltpu.VMEM)
    scales = (
        1.0 / (2.0 * step_x),
        1.0 / (2.0 * step_z),
        DIFFUSIVITY * TIME_STEP / (step_z * step_z),
        math.sqrt(TIME_STEP / WEISSENBERG),
    )
    return pl.pallas_call(
        functools.partial(free_kernel, scales),
        grid=(3,),
        in_specs=[
            whole,
            pl.BlockSpec((1, size_y, slab, size_x), lambda i: (i, 0, 0, 0)),
            whole,
            pl.BlockSpec((3, size_y, slab, size_x), lambda i: (i, 0, 0, 0)),
            whole,
            whole,
            whole,
        ],
        out_specs=pl.BlockSpec((slab, 1, size_y, size_x), lambda i: (0, i, 0, 0)),
        out_shape=pltpu.HBM(planes.shape, jnp.float32),
        compiler_params=pltpu.CompilerParams(vmem_limit_bytes=32 * 1024 * 1024),
        cost_estimate=pl.CostEstimate(flops=3 * 10**9, bytes_accessed=18 * 10**6, transcendentals=0),
    )(planes, wiener, velocity, gradient, below, above, wall_derivative)


def padded(values, rows, columns):
    return jnp.pad(
        values, ((0, rows - values.shape[0]), (0, columns - values.shape[1]))
    )


def stacked_three(table):
    table = np.asarray(table, np.float32)
    high = table.astype(jnp.bfloat16)
    low = (table - high.astype(np.float32)).astype(jnp.bfloat16)
    return jnp.asarray(np.concatenate([high, high, low], axis=0))


def split_three(table, axis):
    high = lax.reduce_precision(table, 8, 7)
    low = (table - high).astype(jnp.bfloat16)
    high = high.astype(jnp.bfloat16)
    return jnp.concatenate([high, high, low], axis=axis)


def three_of(values, axis):
    high = values.astype(jnp.bfloat16)
    low = (values - high.astype(jnp.float32)).astype(jnp.bfloat16)
    return jnp.concatenate([high, low, high], axis=axis)


def full_dot(a, b, side=0):
    return lax.dot_general(
        a,
        b,
        (((1,), (side,)), ((), ())),
        precision=FULL,
        preferred_element_type=jnp.float32,
    )


def plane_kernel(coupling, relax, f_ref, a_ref, s_ref, v_ref, m_ref, x_ref, o_ref, t_ref):
    count, _, size_y, size_x = f_ref.shape
    for start in range(0, size_y, 32):
        part = pl.ds(start, min(32, size_y - start))
        spring = s_ref[part, :]
        scale = relax * spring
        sums = [None] * 6
        for k in range(count):
            moved = [a_ref[k, c, part, :] - scale * f_ref[k, c, part, :] for c in range(3)]
            for p, (i, j) in enumerate(PAIRS):
                value = moved[i] * moved[j]
                sums[p] = value if sums[p] is None else sums[p] + value
        for p, (i, j) in enumerate(PAIRS):
            value = spring * (sums[p] / count)
            t_ref[p, part, :] = value - 1.0 if i == j else value
    modes, slope = m_ref[:LANES, :], m_ref[LANES:, :]
    scaled = coupling * modes
    rows, slope_rows = x_ref[:size_x, :], x_ref[size_x:, :]
    for i in range(3):
        direct = full_dot(modes, v_ref[i]) + full_dot(slope, t_ref[COLUMN[i][1]])
        along_x = full_dot(scaled, t_ref[COLUMN[i][0]])
        along_z = full_dot(scaled, t_ref[COLUMN[i][2]])
        force = full_dot(rows, direct, 1) + full_dot(slope_rows, along_x, 1)
        force_z = full_dot(rows, along_z, 1)
        for half in range(2):
            lanes = slice(half * 128, half * 128 + 128)
            o_ref[pl.ds(8 * half + i, 128, stride=16), :] = force[:, lanes]
            o_ref[pl.ds(8 * half + 3 + i, 128, stride=16), :] = force_z[:, lanes]


def own_plane(field_planes, free_planes, spring, own_velocity, modes, rows, coupling, relax):
    _, _, size_y, size_x = field_planes.shape
    message = pl.pallas_call(
        functools.partial(plane_kernel, coupling, relax),
        out_shape=jax.ShapeDtypeStruct((size_x * 16, 128), jnp.float32),
        scratch_shapes=[pltpu.VMEM((6, size_y, size_x), jnp.float32)],
        compiler_params=pltpu.CompilerParams(vmem_limit_bytes=60 * 1024 * 1024),
    )(field_planes, free_planes, spring, own_velocity, modes, rows)
    return message.reshape(size_x, 2, 8, 128)


def row_kernel(spans, in_ref, d_ref, f_ref, g_ref, b_ref, o_ref, t_ref, sem):
    flat = in_ref.reshape(in_ref.shape[0] * 16, 128)
    lane = lax.broadcasted_iota(jnp.int32, (128, 128), 1)
    last = jnp.zeros((128, 128), jnp.float32)

    def loaded(c):
        return jnp.concatenate(
            [flat[pl.ds(8 * half + c, 128, stride=16), :] for half in range(2)], axis=1
        )

    for i in range(3):
        solved = full_dot(f_ref[...], loaded(i)) + full_dot(g_ref[...], loaded(3 + i))
        both = full_dot(b_ref[...], solved / d_ref[...])
        value, slope = both[:128], both[128:]
        t_ref[:, i] = value[:, :128].reshape(spans, 8, 128)
        t_ref[:, 3 + i] = slope[:, :128].reshape(spans, 8, 128)
        value, slope = value[:, 128:], slope[:, 128:]
        mixed = jnp.where(lane < 64, value, pltpu.roll(slope, 64, 1))
        t_ref[:, 6 + i] = mixed.reshape(spans, 8, 128)
        last = jnp.where(lane == i, pltpu.roll(value, 64 + i, 1), last)
        last = jnp.where(lane == 3 + i, pltpu.roll(slope, 67 + i, 1), last)
    t_ref[:, 9] = last.reshape(spans, 8, 128)
    copies = [
        pltpu.make_async_copy(t_ref, o_ref.at[pl.ds(k * spans, spans)], sem.at[k])
        for k in range(o_ref.shape[0] // spans)
    ]
    for copy in copies:
        copy.start()
    for copy in copies:
        copy.wait()


def own_row(spectra, damping, forward, forward_slope, inverse, samples, spans):
    whole = pl.BlockSpec(memory_space=pltpu.VMEM)
    return pl.pallas_call(
        functools.partial(row_kernel, spans),
        in_specs=[whole] * 5,
        out_specs=pl.BlockSpec(memory_space=pltpu.HBM),
        out_shape=pltpu.HBM((samples * spans, 10, 8, 128), jnp.float32),
        scratch_shapes=[
            pltpu.VMEM((spans, 10, 8, 128), jnp.float32),
            pltpu.SemaphoreType.DMA((samples,)),
        ],
        compiler_params=pltpu.CompilerParams(vmem_limit_bytes=32 * 1024 * 1024),
    )(spectra, damping, forward, forward_slope, inverse)


def slab_kernel(u_ref, w_ref, h_ref, l_ref, t_ref, x_ref, v_ref, g_ref):
    i = pl.program_id(0)
    rows = u_ref.shape[0]
    _, size_y, slab, size_x = v_ref.shape
    flat = [r.reshape(rows * slab, 128) for r in (u_ref, w_ref, h_ref, l_ref)]
    out_v = v_ref.reshape(size_y * slab, size_x)
    out_g = g_ref.reshape(3, size_y * slab, size_x)
    lane = lax.broadcasted_iota(jnp.int32, (rows, 128), 1)
    half = t_ref.shape[0] // 2
    for first in range(0, slab, 2):
        values, slopes = [], []
        for z in (first, first + 1):
            value, slope, high, last = [r[pl.ds(z, rows, stride=slab), :] for r in flat]
            value_high = jnp.where(lane < 64, high, pltpu.roll(last, 64 - i, 1))
            slope_high = jnp.where(
                lane < 64, pltpu.roll(high, 64, 1), pltpu.roll(last, 61 - i, 1)
            )
            value_high = jnp.where(lane <= 64, value_high, 0.0)
            slope_high = jnp.where(lane <= 64, slope_high, 0.0)
            values.append(jnp.concatenate([value, value_high], axis=1))
            slopes.append(jnp.concatenate([slope, slope_high], axis=1))
        across = (((1,), (1,)), ((), ()))
        value = lax.dot_general(
            t_ref[...],
            three_of(jnp.concatenate(values, axis=0), 1),
            across,
            preferred_element_type=jnp.float32,
        )
        slope = lax.dot_general(
            t_ref[:half],
            three_of(jnp.concatenate(slopes, axis=0), 1),
            across,
            preferred_element_type=jnp.float32,
        )
        for k, z in enumerate((first, first + 1)):
            place = pl.ds(z, size_y, stride=slab)
            lanes = slice(k * rows, k * rows + rows)
            both = jnp.dot(
                three_of(value[:half, lanes], 1), x_ref[...], preferred_element_type=jnp.float32
            )
            out_v[place, :] = both[:size_y, :size_x]
            out_g[0, place, :] = both[:size_y, size_x:]
            both = jnp.dot(
                three_of(jnp.concatenate([value[half:, lanes], slope[:, lanes]], axis=0), 1),
                x_ref[:, :size_x],
                preferred_element_type=jnp.float32,
            )
            out_g[1, place, :] = both[:size_y]
            out_g[2, place, :] = both[half : half + size_y]


def slab_values(rows, wall_table, table_x, size_y):
    count = rows.shape[0]
    slab, size_x = rows.shape[2], table_x.shape[1] // 2
    whole = pl.BlockSpec(memory_space=pltpu.VMEM)

    def piece(place):
        return pl.BlockSpec((count, 1, slab, 128), lambda i: (0, place(i), 0, 0))

    return pl.pallas_call(
        slab_kernel,
        grid=(3,),
        in_specs=[
            piece(lambda i: i),
            piece(lambda i: i + 3),
            piece(lambda i: i + 6),
            piece(lambda i: 9),
            whole,
            whole,
        ],
        out_specs=(
            pl.BlockSpec((1, size_y, slab, size_x), lambda i: (i, 0, 0, 0)),
            pl.BlockSpec((3, size_y, slab, size_x), lambda i: (i, 0, 0, 0)),
        ),
        out_shape=(
            jax.ShapeDtypeStruct((3, size_y, slab, size_x), jnp.float32),
            jax.ShapeDtypeStruct((9, size_y, slab, size_x), jnp.float32),
        ),
        compiler_params=pltpu.CompilerParams(vmem_limit_bytes=60 * 1024 * 1024),
    )(rows, rows, rows, rows, wall_table, table_x)


def gathered(plane, count):
    index = lax.axis_index("sample")
    ring = count // 2
    parts = [
        lax.ppermute(
            plane,
            "sample",
            [(i, i - i % ring + (i + k) % ring) for i in range(count)],
        )
        for k in range(ring - 1, 0, -1)
    ] + [plane]
    start = (ring - 1 - index % ring) % ring
    planes = lax.dynamic_slice_in_dim(jnp.stack(parts + parts), start, ring, axis=0)
    other = lax.ppermute(planes, "sample", [(i, (i + ring) % count) for i in range(count)])
    return jnp.where(
        index < ring,
        jnp.concatenate([planes, other]),
        jnp.concatenate([other, planes]),
    )


def on_device(
    fields, wiener, velocity, gradient, wall_derivative, to_modes, from_modes, mode_rates
):
    size_x, slab, size_y = fields.shape[2:]
    samples = lax.axis_size("sample")
    spans = lax.axis_size("span")
    size_z = slab * spans
    step_x = LENGTH_X / size_x
    step_z = LENGTH_Z / size_z
    coupling = TIME_STEP * POLYMER_WEIGHT
    relax = TIME_STEP / (2.0 * WEISSENBERG)

    rows_x, slope_rows_x, square_x = real_basis(size_x, LENGTH_X)
    rows_z, slope_rows_z, square_z = real_basis(size_z, LENGTH_Z)
    order = np.array([slab * (d % spans) + d // spans for d in range(samples * spans)])

    field = jnp.transpose(fields[:, 0], (2, 0, 3, 1))
    ahead = [(i, (i + 1) % spans) for i in range(spans)]
    back = [((i + 1) % spans, i) for i in range(spans)]
    below = lax.ppermute(field[-1], "span", ahead)
    above = lax.ppermute(field[0], "span", back)
    field_planes = lax.all_to_all(field, "sample", 0, 0, tiled=True)
    speed = jnp.transpose(velocity, (0, 3, 2, 1))
    free = spring_free(
        field,
        jnp.transpose(wiener[:, 0], (0, 3, 2, 1)),
        speed,
        jnp.transpose(gradient, (0, 3, 2, 1)),
        below,
        above,
        wall_derivative,
        step_x,
        step_z,
    )
    free_planes = lax.all_to_all(free, "sample", 0, 0, tiled=True)

    own_velocity = lax.dynamic_index_in_dim(
        speed, lax.axis_index("sample"), 2, keepdims=False
    )
    modes = padded(to_modes, LANES, size_y)
    modes_slope = coupling * jnp.dot(modes, wall_derivative, precision=FULL)
    plane_square = jnp.sum(field_planes * field_planes, axis=(0, 1)) / samples
    spring = 1.0 / (1.0 - plane_square / EXTENSIBILITY)
    slab_spring = gathered(spring, samples)
    message = own_plane(
        field_planes,
        free_planes,
        spring,
        own_velocity,
        jnp.concatenate([modes, modes_slope]),
        f32(np.concatenate([rows_x, slope_rows_x @ rows_x])),
        coupling,
        relax,
    )
    message, slab_spring = lax.optimization_barrier((message, slab_spring))
    spectra = lax.all_to_all(message, BOTH, 0, 0, tiled=True)

    row = lax.axis_index("sample") * spans + lax.axis_index("span")
    square_row = lax.dynamic_index_in_dim(f32(square_x), row, 0, keepdims=False)
    rates = padded(mode_rates[None, :], 1, LANES)
    damping = 1.0 + TIME_STEP * VISCOSITY * (
        square_row + f32(square_z)[:, None] + rates
    )
    back = own_row(
        spectra,
        damping,
        f32(rows_z[:, order]),
        f32((slope_rows_z @ rows_z)[:, order]),
        f32(np.concatenate([rows_z.T, rows_z.T @ slope_rows_z])),
        samples,
        spans,
    )
    rows = lax.all_to_all(back, BOTH, 0, 0, tiled=True)

    modes_wall = jnp.dot(wall_derivative, from_modes, precision=FULL)
    wall_table = jnp.concatenate(
        [padded(from_modes, 208, LANES), padded(modes_wall, 208, LANES)]
    )
    new_velocity, new_gradient = slab_values(
        rows,
        split_three(wall_table, 1),
        stacked_three(np.concatenate([rows_x, (rows_x.T @ slope_rows_x).T], axis=1)),
        size_y,
    )
    new_fields = free - relax * slab_spring[:, None] * field
    return (
        jnp.transpose(new_fields, (1, 3, 0, 2))[:, None],
        jnp.transpose(new_velocity, (0, 3, 2, 1)),
        jnp.transpose(new_gradient, (0, 3, 2, 1)),
    )


def solution(mesh):
    in_specs = (
        P(None, "sample", None, "span", None),
        P(None, "sample", None, "span", None),
        P(None, None, "span", None),
        P(None, None, "span", None),
        P(),
        P(),
        P(),
        P(),
    )
    out_specs = (
        P(None, "sample", None, "span", None),
        P(None, None, "span", None),
        P(None, None, "span", None),
    )
    return jax.shard_map(
        on_device, mesh=mesh, in_specs=in_specs, out_specs=out_specs, check_vma=False
    )
```

time: 266 us -> 239 us (0.90)
  Pallas kernels: 0 us -> 35 us
  local copies, waits for them, and re-layouts: 47.4 us -> 15.6 us
  matrix products: 30.1 us -> 1.78 us
  starting transfers between devices: 61.2 us -> 40.5 us
  waiting for transfers between devices: 116 us -> 135 us
    all_to_all x1, waiting for transfers between devices: 0.01 us -> 61.1 us  [on_device(): rows = lax.all_to_all(back, BOTH, 0, 0, tiled=True)]
    ppermute x9 -> x6, waiting for transfers between devices: 70.2 us -> 28.6 us  [the longest x3 28.6 us: gathered(): lax.ppermute(plane, 'sample', [(i, i - i % ring + (i + k) % ring) for i i...]
    pallas_call x0 -> x4, Pallas kernels: none -> 35 us  [the longest x1 13 us: slab_values(): pl.pallas_call(slab_kernel, grid=(3,), in_specs=[piece(lambda i: i), piec...]
    dot_general x16 -> x1, matrix products: 29.7 us -> 0.37 us  [on_device(): modes_slope = coupling * jnp.dot(modes, wall_derivative, precision=FULL)]
    slice x6 -> x0, local copies, waits for them, and re-layouts: 13.5 us -> none  [the longest x2 6.02 us: spring_free(): jnp.roll(fields, 1, axis=1)]
    ppermute x9 -> x6, starting transfers between devices: 22.9 us -> 12.3 us  [the longest x3 7.91 us: gathered(): lax.ppermute(plane, 'sample', [(i, i - i % ring + (i + k) % ring) for i i...]
    all_to_all x1 -> x0, local copies, waits for them, and re-layouts: 6.19 us -> none  [on_device(): rows = lax.all_to_all(back, BOTH, 0, 0, tiled=True)]
    all_to_all x1, starting transfers between devices: 14.2 us -> 8.82 us  [on_device(): spectra = lax.all_to_all(message, BOTH, 0, 0, tiled=True)]
  transfers between devices with their start and end apart: 13 -> 10, of which waited for: 7 -> 5; matrix products, arithmetic and copies ran while one was open for 14% -> 7% of each run, Pallas kernels for 0% -> 7%
where the time goes in v2:
time: 239 us; the launch traced here: 237 us
  waiting for transfers between devices  135 us (56%)
  starting transfers between devices  40.5 us (17%)
  Pallas kernels  35 us (15%)
  local copies, waits for them, and re-layouts  15.6 us (7%)
  other arithmetic  8.03 us (3%)
    all_to_all x1, waiting for transfers between devices, on_device(): rows = lax.all_to_all(back, BOTH, 0, 0, tiled=True)  61.1 us
    all_to_all x1, waiting for transfers between devices, on_device(): field_planes = lax.all_to_all(field, 'sample', 0, 0, tiled=True)  28.7 us
    ppermute x3, waiting for transfers between devices, gathered(): lax.ppermute(plane, 'sample', [(i, i - i % ring + (i + k) % ring) for i i...  28.6 us
    all_to_all x1, waiting for transfers between devices, on_device(): spectra = lax.all_to_all(message, BOTH, 0, 0, tiled=True)  16.3 us
    pallas_call x1, Pallas kernels, slab_values(): pl.pallas_call(slab_kernel, grid=(3,), in_specs=[piece(lambda i: i), piec...  13 us
    unnamed x35, local copies, waits for them, and re-layouts  12.7 us
    pallas_call x1, Pallas kernels, spring_free(): pl.pallas_call(functools.partial(free_kernel, scales), grid=(3,), in_spec...  9.82 us
    all_to_all x1, starting transfers between devices, on_device(): spectra = lax.all_to_all(message, BOTH, 0, 0, tiled=True)  8.82 us
  transfers between devices with their start and end apart: 10, of which 5 were waited for; matrix products, arithmetic and copies ran while one was open for 7% of the time, Pallas kernels for 7%

profile of v2, /device:TPU:5, one launch (start us, length us, event | category | flops | bytes accessed | tf_op | source)
XLA Modules:
  0.0 236.6 jit_solution(12525097053141285549)
XLA Ops:
  0.6 3.6 %copy.33 = f32[3,1,128,8,193]{2,4,0,3,1:T(8,128)} copy(f32[3,1,128,8,193]{2,3,4,1,0:T(8,128)} %param.15) | data formatting | bytes 4743168 | tf_op args[0]
  4.2 7.5 %all-to-all-start = ((f32[8,3,193,128]{3,2,1,0:T(8,128)}), f32[8,3,193,128]{3,2,1,0:T(8,128)}, u32[]{:S(2)}, u32[]{:S(2)}) async-start(f32[8,3,193,128]{3,2,1,0:T(8,128)} %bitcast.44.f_ref), calls=%async_computation | async-start | bytes 4915200 | tf_op jit(solution)/shard_map/all_to_all | solution.py:357
  11.7 2.1 slice_bitcast_fusion
  15.5 28.7 %all-to-all-done.f_ref = f32[8,3,193,128]{3,2,1,0:T(8,128)} async-done(((f32[8,3,193,128]{3,2,1,0:T(8,128)}), f32[8,3,193,128]{3,2,1,0:T(8,128)}, u32[]{:S(2)}, u32[]{:S(2)}) %all-to-all-start) | async-done | bytes 2371616 | tf_op jit(solution)/shard_map/all_to_all | solution.py:357
  44.2 1.9 multiply_reduce_fusion
  46.8 4.1 %collective-permute-start.2 = (f32[193,128]{1,0:T(8,128)}, f32[193,128]{1,0:T(8,128)}, u32[]{:S(2)}, u32[]{:S(2)}) collective-permute-start(f32[193,128]{1,0:T(8,128)} %subtract_divide_fusion.s_ref), channel_id=1, source_target_pairs={{0,48},{16,0},{32,16},{48,32},{64,112},{80,64},{96,80},{112,96},{1... | collective-permute-start | bytes 296456 | tf_op jit(solution)/shard_map/ppermute | solution.py:319
  50.9 3.0 %copy-done = f32[9,128,8,193]{1,2,3,0:T(8,128)S(1)} copy-done((f32[9,128,8,193]{1,2,3,0:T(8,128)S(1)}, f32[9,128,8,193]{1,2,3,0:T(8,128)}, u32[]{:S(2)}) %copy-start) | copy-done | bytes 7114776
  53.9 1.7 copy-done.2
  55.5 9.8 %shard_map.166 = f32[8,3,193,128]{3,2,1,0:T(8,128)} custom-call(f32[8,3,193,128]{3,2,1,0:T(8,128)} %bitcast.44.f_ref, f32[3,193,8,128]{3,2,1,0:T(8,128)S(1)} %bitcast.48, f32[3,193,8,128]{3,2,1,0:T(8,128)S(1)} %bitcast.47, f32[9,193,8,128]{3,2,1,0:T(8,128)S(1)} %bitcast.46, f32[3,193,128]{2,1,0:T(8,128)S(1)} %collective-permute-done.lo_ref, ...), custom_call_target="tpu_custom_call" | custom-call | flops 3000000000 | bytes 18000000 | tf_op jit(solution)/shard_map/pallas_call | solution.py:90
  65.4 5.1 %all-to-all-start.1 = ((f32[8,3,193,128]{3,2,1,0:T(8,128)}), f32[8,3,193,128]{3,2,1,0:T(8,128)}, u32[]{:S(2)}, u32[]{:S(2)}) async-start(f32[8,3,193,128]{3,2,1,0:T(8,128)} %shard_map.166), calls=%async_computation.1 | async-start | bytes 4915200 | tf_op jit(solution)/shard_map/all_to_all | solution.py:370
  70.5 1.5 collective-permute-start.4
  72.0 2.4 %collective-permute-start.3 = (f32[193,128]{1,0:T(8,128)}, f32[193,128]{1,0:T(8,128)S(1)}, u32[]{:S(2)}, u32[]{:S(2)}) collective-permute-start(f32[193,128]{1,0:T(8,128)} %subtract_divide_fusion.s_ref), channel_id=1, source_target_pairs={{0,32},{16,48},{32,0},{48,16},{64,96},{80,112},{96,64},{112,80},{1... | collective-permute-start | bytes 296456 | tf_op jit(solution)/shard_map/ppermute | solution.py:319
  75.3 27.6 %collective-permute-done.3 = f32[193,128]{1,0:T(8,128)S(1)} collective-permute-done((f32[193,128]{1,0:T(8,128)}, f32[193,128]{1,0:T(8,128)S(1)}, u32[]{:S(2)}, u32[]{:S(2)}) %collective-permute-start.3) | collective-permute-done | bytes 98848 | tf_op jit(solution)/shard_map/ppermute | solution.py:319
  104.9 2.7 %collective-permute-start.5 = (f32[4,193,128]{2,1,0:T(8,128)S(1)}, f32[4,193,128]{2,1,0:T(8,128)}, u32[]{:S(2)}, u32[]{:S(2)}) collective-permute-start(f32[4,193,128]{2,1,0:T(8,128)S(1)} %constant_dynamic-slice_fusion), channel_id=1, source_target_pairs={{0,64},{16,80},{32,96},{48,112},{64,0},{80,16},{96,32},{112,48},{1... | collective-permute-start | bytes 1185800 | tf_op jit(solution)/shard_map/ppermute | solution.py:328
  109.8 7.8 %shard_map.167 = f32[2048,128]{1,0:T(8,128)} custom-call(f32[8,3,193,128]{3,2,1,0:T(8,128)} %all-to-all-done.f_ref, f32[8,3,193,128]{3,2,1,0:T(8,128)} %all-to-all-done.1.a_ref, f32[193,128]{1,0:T(8,128)} %subtract_divide_fusion.s_ref, f32[3,193,128]{2,1,0:T(8,128)} %bitcast.50, f32[512,193]{1,0:T(8,128)} %pad_maximum_fusion.1.m_ref, ...), custom_call_target="tpu_custom_call" | custom-call | tf_op jit(solution)/shard_map/pallas_call | solution.py:177
  117.7 1.3 maximum_select_fusion
  119.0 8.8 %all-to-all-start.2 = ((f32[128,2,8,128]{3,2,1,0:T(8,128)}), f32[128,2,8,128]{3,2,1,0:T(8,128)S(1)}, u32[]{:S(2)}, u32[]{:S(2)}) async-start(f32[128,2,8,128]{3,2,1,0:T(8,128)} %bitcast.49), calls=%async_computation.2 | async-start | bytes 2097152 | tf_op jit(solution)/shard_map/all_to_all | solution.py:391
  129.2 16.3 %all-to-all-done.2.in_ref = f32[128,2,8,128]{3,2,1,0:T(8,128)S(1)} async-done(((f32[128,2,8,128]{3,2,1,0:T(8,128)}), f32[128,2,8,128]{3,2,1,0:T(8,128)S(1)}, u32[]{:S(2)}, u32[]{:S(2)}) %all-to-all-start.2) | async-done | bytes 1048608 | tf_op jit(solution)/shard_map/all_to_all | solution.py:391
  145.5 4.4 %shard_map.168 = f32[128,10,8,128]{3,2,1,0:T(8,128)} custom-call(f32[128,2,8,128]{3,2,1,0:T(8,128)S(1)} %all-to-all-done.2.in_ref, f32[128,256]{1,0:T(8,128)S(1)} %multiply_add_fusion.d_ref, f32[128,128]{1,0:T(8,128)S(1)} %copy-done.6, f32[128,128]{1,0:T(8,128)S(1)} %copy-done.5, f32[256,128]{1,0:T(8,128)S(1)} %copy-done.4), custom_call_target="tpu_custom_call" | custom-call | tf_op jit(solution)/shard_map/pallas_call | solution.py:220
  150.0 6.7 %all-to-all-start.3 = ((f32[128,10,8,128]{3,2,1,0:T(8,128)}), f32[128,10,8,128]{3,2,1,0:T(8,128)}, u32[]{:S(2)}, u32[]{:S(2)}) async-start(f32[128,10,8,128]{3,2,1,0:T(8,128)} %shard_map.168), calls=%async_computation.3 | async-start | bytes 10485760 | tf_op jit(solution)/shard_map/all_to_all | solution.py:408
  156.7 1.4 fusion.3
  160.7 1.8 copy.26
  162.5 61.1 %all-to-all-done.3.u_ref.w_ref.h_ref.l_ref = f32[128,10,8,128]{3,2,1,0:T(8,128)} async-done(((f32[128,10,8,128]{3,2,1,0:T(8,128)}), f32[128,10,8,128]{3,2,1,0:T(8,128)}, u32[]{:S(2)}, u32[]{:S(2)}) %all-to-all-start.3) | async-done | bytes 5242912 | tf_op jit(solution)/shard_map/all_to_all | solution.py:408
  223.6 13.0 %shard_map.169 = (f32[3,193,8,128]{3,2,1,0:T(8,128)}, f32[9,193,8,128]{3,2,1,0:T(8,128)}) custom-call(f32[128,10,8,128]{3,2,1,0:T(8,128)} %all-to-all-done.3.u_ref.w_ref.h_ref.l_ref, f32[128,10,8,128]{3,2,1,0:T(8,128)} %all-to-all-done.3.u_ref.w_ref.h_ref.l_ref, f32[128,10,8,128]{3,2,1,0:T(8,128)} %all-to-all-done.3.u_ref.w_ref.h_ref.l_ref, ...), custom_call_target="tpu_custom_call" | custom-call | tf_op jit(solution)/shard_map/pallas_call | solution.py:292
  (55 shorter events, 11.5 us)
Async XLA Ops:
  4.2 40.0 %all-to-all-start = ((f32[8,3,193,128]{3,2,1,0:T(8,128)}), f32[8,3,193,128]{3,2,1,0:T(8,128)}, u32[]{:S(2)}, u32[]{:S(2)}) async-start(f32[8,3,193,128]{3,2,1,0:T(8,128)} %bitcast.44.f_ref), calls=%async_computation | async-start | bytes 4915200 | tf_op jit(solution)/shard_map/all_to_all | solution.py:357
  11.7 39.1 %copy-start.1 = (f32[3,128,8,193]{1,2,3,0:T(8,128)S(1)}, f32[3,128,8,193]{1,2,3,0:T(8,128)}, u32[]{:S(2)}) copy-start(f32[3,128,8,193]{1,2,3,0:T(8,128)} %param.17) | copy-start | bytes 7114756
  11.7 39.1 %copy-start.3 = (f32[193,193]{1,0:T(8,128)S(1)}, f32[193,193]{1,0:T(8,128)}, u32[]{:S(2)}) copy-start(f32[193,193]{1,0:T(8,128)} %d_ref.1) | copy-start | bytes 446992
  13.8 37.0 %collective-permute-start.1 = (f32[3,193,128]{2,1,0:T(8,128)}, f32[3,193,128]{2,1,0:T(8,128)S(1)}, u32[]{:S(2)}, u32[]{:S(2)}) collective-permute-start(f32[3,193,128]{2,1,0:T(8,128)} %get-tuple-element.17), channel_id=1, source_target_pairs={{1,0},{2,1},{3,2},{4,3},{5,4},{6,5},{7,6},{8,7},{9,8},{10,9},{11,1... | collective-permute-start | bytes 889352 | tf_op jit(solution)/shard_map/ppermute | solution.py:356
  14.8 36.1 %collective-permute-start = (f32[3,193,128]{2,1,0:T(8,128)}, f32[3,193,128]{2,1,0:T(8,128)S(1)}, u32[]{:S(2)}, u32[]{:S(2)}) collective-permute-start(f32[3,193,128]{2,1,0:T(8,128)} %get-tuple-element.18), channel_id=1, source_target_pairs={{0,1},{1,2},{2,3},{3,4},{4,5},{5,6},{6,7},{7,8},{8,9},{9,10},{10,1... | collective-permute-start | bytes 889352 | tf_op jit(solution)/shard_map/ppermute | solution.py:355
  46.8 27.6 %collective-permute-start.2 = (f32[193,128]{1,0:T(8,128)}, f32[193,128]{1,0:T(8,128)}, u32[]{:S(2)}, u32[]{:S(2)}) collective-permute-start(f32[193,128]{1,0:T(8,128)} %subtract_divide_fusion.s_ref), channel_id=1, source_target_pairs={{0,48},{16,0},{32,16},{48,32},{64,112},{80,64},{96,80},{112,96},{1... | collective-permute-start | bytes 296456 | tf_op jit(solution)/shard_map/ppermute | solution.py:319
  50.8 3.0 %copy-start = (f32[9,128,8,193]{1,2,3,0:T(8,128)S(1)}, f32[9,128,8,193]{1,2,3,0:T(8,128)}, u32[]{:S(2)}) copy-start(f32[9,128,8,193]{1,2,3,0:T(8,128)} %param.18) | copy-start | bytes 21344260
  53.9 1.7 copy-start.2
  65.4 44.4 %all-to-all-start.1 = ((f32[8,3,193,128]{3,2,1,0:T(8,128)}), f32[8,3,193,128]{3,2,1,0:T(8,128)}, u32[]{:S(2)}, u32[]{:S(2)}) async-start(f32[8,3,193,128]{3,2,1,0:T(8,128)} %shard_map.166), calls=%async_computation.1 | async-start | bytes 4915200 | tf_op jit(solution)/shard_map/all_to_all | solution.py:370
  70.5 38.1 %copy-start.9 = (f32[193,193]{1,0:T(8,128)S(1)}, f32[193,193]{1,0:T(8,128)}, u32[]{:S(2)}) copy-start(f32[193,193]{1,0:T(8,128)} %param.20) | copy-start | bytes 446992
  70.5 33.4 %collective-permute-start.4 = (f32[193,128]{1,0:T(8,128)}, f32[193,128]{1,0:T(8,128)S(1)}, u32[]{:S(2)}, u32[]{:S(2)}) collective-permute-start(f32[193,128]{1,0:T(8,128)} %subtract_divide_fusion.s_ref), channel_id=1, source_target_pairs={{0,16},{16,32},{32,48},{48,0},{64,80},{80,96},{96,112},{112,64},{1... | collective-permute-start | bytes 296456 | tf_op jit(solution)/shard_map/ppermute | solution.py:319
  72.0 30.9 %collective-permute-start.3 = (f32[193,128]{1,0:T(8,128)}, f32[193,128]{1,0:T(8,128)S(1)}, u32[]{:S(2)}, u32[]{:S(2)}) collective-permute-start(f32[193,128]{1,0:T(8,128)} %subtract_divide_fusion.s_ref), channel_id=1, source_target_pairs={{0,32},{16,48},{32,0},{48,16},{64,96},{80,112},{96,64},{112,80},{1... | collective-permute-start | bytes 296456 | tf_op jit(solution)/shard_map/ppermute | solution.py:319
  104.9 12.7 %collective-permute-start.5 = (f32[4,193,128]{2,1,0:T(8,128)S(1)}, f32[4,193,128]{2,1,0:T(8,128)}, u32[]{:S(2)}, u32[]{:S(2)}) collective-permute-start(f32[4,193,128]{2,1,0:T(8,128)S(1)} %constant_dynamic-slice_fusion), channel_id=1, source_target_pairs={{0,64},{16,80},{32,96},{48,112},{64,0},{80,16},{96,32},{112,48},{1... | collective-permute-start | bytes 1185800 | tf_op jit(solution)/shard_map/ppermute | solution.py:328
  117.6 10.2 %copy-start.10 = (f32[193]{0:T(256)S(1)}, f32[193]{0:T(256)}, u32[]{:S(2)}) copy-start(f32[193]{0:T(256)} %param.22) | copy-start | bytes 2320
  117.6 10.3 %copy-start.12 = (f32[128]{0:T(128)S(1)}, f32[128]{0:T(128)}, u32[]{:S(2)}) copy-start(f32[128]{0:T(128)} %constant.75.clone) | copy-start | bytes 1540
  117.6 10.9 %copy-start.11 = (f32[128]{0:T(128)S(1)}, f32[128]{0:T(128)}, u32[]{:S(2)}) copy-start(f32[128]{0:T(128)} %constant.76.clone) | copy-start | bytes 1540
  117.6 27.9 %copy-start.4 = (f32[256,128]{1,0:T(8,128)S(1)}, f32[256,128]{1,0:T(8,128)}, u32[]{:S(2)}) copy-start(f32[256,128]{1,0:T(8,128)} %constant.79.clone.b_ref) | copy-start | bytes 393220
  117.6 27.9 %copy-start.5 = (f32[128,128]{1,0:T(8,128)S(1)}, f32[128,128]{1,0:T(8,128)}, u32[]{:S(2)}) copy-start(f32[128,128]{1,0:T(8,128)} %constant.78.clone.g_ref) | copy-start | bytes 196612
  117.6 27.9 %copy-start.6 = (f32[128,128]{1,0:T(8,128)S(1)}, f32[128,128]{1,0:T(8,128)}, u32[]{:S(2)}) copy-start(f32[128,128]{1,0:T(8,128)} %constant.77.clone.f_ref) | copy-start | bytes 196612
  119.0 26.5 %all-to-all-start.2 = ((f32[128,2,8,128]{3,2,1,0:T(8,128)}), f32[128,2,8,128]{3,2,1,0:T(8,128)S(1)}, u32[]{:S(2)}, u32[]{:S(2)}) async-start(f32[128,2,8,128]{3,2,1,0:T(8,128)} %bitcast.49), calls=%async_computation.2 | async-start | bytes 2097152 | tf_op jit(solution)/shard_map/all_to_all | solution.py:391
  150.0 10.2 %copy-start.8 = (f32[3,1,128,8,193]{2,3,4,1,0:T(8,128)S(1)}, f32[3,1,128,8,193]{2,3,4,1,0:T(8,128)}, u32[]{:S(2)}) copy-start(f32[3,1,128,8,193]{2,3,4,1,0:T(8,128)} %param.15) | copy-start | bytes 7114756
  150.0 73.6 %all-to-all-start.3 = ((f32[128,10,8,128]{3,2,1,0:T(8,128)}), f32[128,10,8,128]{3,2,1,0:T(8,128)}, u32[]{:S(2)}, u32[]{:S(2)}) async-start(f32[128,10,8,128]{3,2,1,0:T(8,128)} %shard_map.168), calls=%async_computation.3 | async-start | bytes 10485760 | tf_op jit(solution)/shard_map/all_to_all | solution.py:408
  156.7 3.4 %copy-start.7 = (f32[8,3,193,128]{3,2,1,0:T(8,128)S(1)}, f32[8,3,193,128]{3,2,1,0:T(8,128)}, u32[]{:S(2)}) copy-start(f32[8,3,193,128]{3,2,1,0:T(8,128)} %shard_map.166) | copy-start | bytes 7114756

commit v3 on v2

--- a/solution.py
+++ b/solution.py
@@ -101,7 +101,7 @@
         ],
         out_specs=pl.BlockSpec((slab, 1, size_y, size_x), lambda i: (0, i, 0, 0)),
         out_shape=pltpu.HBM(planes.shape, jnp.float32),
-        compiler_params=pltpu.CompilerParams(vmem_limit_bytes=32 * 1024 * 1024),
+        compiler_params=pltpu.CompilerParams(vmem_limit_bytes=60 * 1024 * 1024),
         cost_estimate=pl.CostEstimate(flops=3 * 10**9, bytes_accessed=18 * 10**6, transcendentals=0),
     )(planes, wiener, velocity, gradient, below, above, wall_derivative)
 
@@ -142,44 +142,68 @@
     )
 
 
-def plane_kernel(coupling, relax, f_ref, a_ref, s_ref, v_ref, m_ref, x_ref, o_ref, t_ref):
-    count, _, size_y, size_x = f_ref.shape
-    for start in range(0, size_y, 32):
-        part = pl.ds(start, min(32, size_y - start))
-        spring = s_ref[part, :]
-        scale = relax * spring
-        sums = [None] * 6
-        for k in range(count):
-            moved = [a_ref[k, c, part, :] - scale * f_ref[k, c, part, :] for c in range(3)]
+def plane_kernel(n_ref, s_ref, v_ref, m_ref, x_ref, o_ref, t_ref):
+    k = pl.program_id(0)
+    count = pl.num_programs(0)
+    size_y, size_x = s_ref.shape
+
+    @pl.when(k == 0)
+    def _():
+        t_ref[...] = jnp.zeros_like(t_ref)
+
+    for start in range(0, size_y, 64):
+        part = pl.ds(start, min(64, size_y - start))
+        moved = [n_ref[0, c, part, :] for c in range(3)]
+        for p, (i, j) in enumerate(PAIRS):
+            t_ref[p, part, :] += moved[i] * moved[j]
+
+    @pl.when(k == count - 1)
+    def _():
+        for start in range(0, size_y, 64):
+            part = pl.ds(start, min(64, size_y - start))
+            spring = s_ref[part, :]
             for p, (i, j) in enumerate(PAIRS):
-                value = moved[i] * moved[j]
-                sums[p] = value if sums[p] is None else sums[p] + value
-        for p, (i, j) in enumerate(PAIRS):
-            value = spring * (sums[p] / count)
-            t_ref[p, part, :] = value - 1.0 if i == j else value
-    modes, slope = m_ref[:LANES, :], m_ref[LANES:, :]
-    scaled = coupling * modes
-    rows, slope_rows = x_ref[:size_x, :], x_ref[size_x:, :]
-    for i in range(3):
-        direct = full_dot(modes, v_ref[i]) + full_dot(slope, t_ref[COLUMN[i][1]])
-        along_x = full_dot(scaled, t_ref[COLUMN[i][0]])
-        along_z = full_dot(scaled, t_ref[COLUMN[i][2]])
-        force = full_dot(rows, direct, 1) + full_dot(slope_rows, along_x, 1)
-        force_z = full_dot(rows, along_z, 1)
-        for half in range(2):
-            lanes = slice(half * 128, half * 128 + 128)
-            o_ref[pl.ds(8 * half + i, 128, stride=16), :] = force[:, lanes]
-            o_ref[pl.ds(8 * half + 3 + i, 128, stride=16), :] = force_z[:, lanes]
-
-
-def own_plane(field_planes, free_planes, spring, own_velocity, modes, rows, coupling, relax):
-    _, _, size_y, size_x = field_planes.shape
+                value = spring * (t_ref[p, part, :] / count)
+                t_ref[p, part, :] = value - 1.0 if i == j else value
+        scaled, slope = m_ref[:LANES, :], m_ref[LANES:, :]
+        for i in range(3):
+            column = [t_ref[p] for p in COLUMN[i]]
+            direct = v_ref[i] + jnp.dot(
+                slope, three_of(column[1], 0), preferred_element_type=jnp.float32
+            )
+            along = jnp.dot(
+                scaled,
+                three_of(jnp.concatenate([column[0], column[2]], axis=1), 0),
+                preferred_element_type=jnp.float32,
+            )
+            force = full_dot(
+                x_ref[...], jnp.concatenate([direct, along[:, :size_x]], axis=1), 1
+            )
+            force_z = full_dot(x_ref[:, :size_x], along[:, size_x:], 1)
+            for half in range(2):
+                lanes = slice(half * 128, half * 128 + 128)
+                o_ref[pl.ds(8 * half + i, 128, stride=16), :] = force[:, lanes]
+                o_ref[pl.ds(8 * half + 3 + i, 128, stride=16), :] = force_z[:, lanes]
+
+
+def own_plane(moved, spring, modes_velocity, modes, rows):
+    count, _, size_y, size_x = moved.shape
+    whole = pl.BlockSpec(memory_space=pltpu.VMEM)
     message = pl.pallas_call(
-        functools.partial(plane_kernel, coupling, relax),
+        plane_kernel,
+        grid=(count,),
+        in_specs=[
+            pl.BlockSpec((1, 3, size_y, size_x), lambda k: (k, 0, 0, 0)),
+            whole,
+            whole,
+            whole,
+            whole,
+        ],
+        out_specs=pl.BlockSpec((size_x * 16, 128), lambda k: (0, 0)),
         out_shape=jax.ShapeDtypeStruct((size_x * 16, 128), jnp.float32),
-        scratch_shapes=[pltpu.VMEM((6, size_y, size_x), jnp.float32)],
-        compiler_params=pltpu.CompilerParams(vmem_limit_bytes=60 * 1024 * 1024),
-    )(field_planes, free_planes, spring, own_velocity, modes, rows)
+        scratch_shapes=[pltpu.VMEM((6, LANES, size_x), jnp.float32)],
+        compiler_params=pltpu.CompilerParams(vmem_limit_bytes=24 * 1024 * 1024),
+    )(moved, spring, modes_velocity, modes, rows)
     return message.reshape(size_x, 2, 8, 128)
 
 
@@ -312,25 +336,29 @@
     )(rows, rows, rows, rows, wall_table, table_x)
 
 
-def gathered(plane, count):
+def summed(planes):
+    count = lax.axis_size("sample")
+    ring = count // 2
     index = lax.axis_index("sample")
-    ring = count // 2
-    parts = [
-        lax.ppermute(
-            plane,
-            "sample",
-            [(i, i - i % ring + (i + k) % ring) for i in range(count)],
-        )
-        for k in range(ring - 1, 0, -1)
-    ] + [plane]
-    start = (ring - 1 - index % ring) % ring
-    planes = lax.dynamic_slice_in_dim(jnp.stack(parts + parts), start, ring, axis=0)
-    other = lax.ppermute(planes, "sample", [(i, (i + ring) % count) for i in range(count)])
-    return jnp.where(
-        index < ring,
-        jnp.concatenate([planes, other]),
-        jnp.concatenate([other, planes]),
-    )
+    place = index % ring
+    quarters = planes.reshape((ring, planes.shape[0] // ring) + planes.shape[1:])
+
+    def shifted(values, k):
+        pairs = [(i, i - i % ring + (i + k) % ring) for i in range(count)]
+        return lax.ppermute(values, "sample", pairs)
+
+    ahead = lax.dynamic_slice_in_dim(
+        jnp.concatenate([quarters, quarters]), place, ring, axis=0
+    )
+    total = ahead[0]
+    for part in [shifted(ahead[k], k) for k in range(1, ring)]:
+        total = total + part
+    pairs = [(i, (i + ring) % count) for i in range(count)]
+    total = total + lax.ppermute(total, "sample", pairs)
+    parts = [shifted(total, k) for k in range(ring - 1, 0, -1)] + [total]
+    start = (ring - 1 - place) % ring
+    gathered = lax.dynamic_slice_in_dim(jnp.stack(parts + parts), start, ring, axis=0)
+    return gathered.reshape(planes.shape)
 
 
 def on_device(
@@ -354,7 +382,7 @@
     back = [((i + 1) % spans, i) for i in range(spans)]
     below = lax.ppermute(field[-1], "span", ahead)
     above = lax.ppermute(field[0], "span", back)
-    field_planes = lax.all_to_all(field, "sample", 0, 0, tiled=True)
+    total_square = summed(jnp.sum(field * field, axis=1))
     speed = jnp.transpose(velocity, (0, 3, 2, 1))
     free = spring_free(
         field,
@@ -367,27 +395,27 @@
         step_x,
         step_z,
     )
-    free_planes = lax.all_to_all(free, "sample", 0, 0, tiled=True)
+    slab_spring = 1.0 / (1.0 - total_square / samples / EXTENSIBILITY)
+    new_fields = free - relax * slab_spring[:, None] * field
+    moved = lax.all_to_all(new_fields, "sample", 0, 0, tiled=True)
 
     own_velocity = lax.dynamic_index_in_dim(
         speed, lax.axis_index("sample"), 2, keepdims=False
     )
     modes = padded(to_modes, LANES, size_y)
     modes_slope = coupling * jnp.dot(modes, wall_derivative, precision=FULL)
-    plane_square = jnp.sum(field_planes * field_planes, axis=(0, 1)) / samples
-    spring = 1.0 / (1.0 - plane_square / EXTENSIBILITY)
-    slab_spring = gathered(spring, samples)
+    modes_velocity = jnp.einsum("my,cyx->cmx", modes, own_velocity, precision=FULL)
+    modes_table = jnp.concatenate([coupling * modes, modes_slope])
+    spring = lax.dynamic_index_in_dim(
+        slab_spring, lax.axis_index("sample"), 0, keepdims=False
+    )
     message = own_plane(
-        field_planes,
-        free_planes,
+        moved,
         spring,
-        own_velocity,
-        jnp.concatenate([modes, modes_slope]),
-        f32(np.concatenate([rows_x, slope_rows_x @ rows_x])),
-        coupling,
-        relax,
-    )
-    message, slab_spring = lax.optimization_barrier((message, slab_spring))
+        modes_velocity,
+        split_three(padded(modes_table, 2 * LANES, LANES), 1),
+        f32(np.concatenate([rows_x, slope_rows_x @ rows_x], axis=1)),
+    )
     spectra = lax.all_to_all(message, BOTH, 0, 0, tiled=True)
 
     row = lax.axis_index("sample") * spans + lax.axis_index("span")
@@ -417,7 +445,6 @@
         stacked_three(np.concatenate([rows_x, (rows_x.T @ slope_rows_x).T], axis=1)),
         size_y,
     )
-    new_fields = free - relax * slab_spring[:, None] * field
     return (
         jnp.transpose(new_fields, (1, 3, 0, 2))[:, None],
         jnp.transpose(new_velocity, (0, 3, 2, 1)),

time: 239 us -> 220 us (0.921)
  waiting for transfers between devices: 135 us -> 128 us
  starting transfers between devices: 40.5 us -> 34 us
  local copies, waits for them, and re-layouts: 15.6 us -> 11.8 us
    all_to_all x2 -> x1, starting transfers between devices: 12.6 us -> 3.81 us  [on_device(): moved = lax.all_to_all(new_fields, 'sample', 0, 0, tiled=True)]
    ppermute x4 -> x7, waiting for transfers between devices: 28.6 us -> 20.9 us  [the longest x6 12 us: shifted(): return lax.ppermute(values, 'sample', pairs)]
    unnamed x35 -> x47, local copies, waits for them, and re-layouts: 12.7 us -> 8.29 us
    pallas_call x1, Pallas kernels: 7.82 us -> 4.2 us  [own_plane(): pl.pallas_call(plane_kernel, grid=(count,), in_specs=[pl.BlockSpec((1, 3,...]
    all_to_all x2 -> x1, waiting for transfers between devices: 28.7 us -> 27.3 us  [on_device(): moved = lax.all_to_all(new_fields, 'sample', 0, 0, tiled=True)]
    ppermute x4 -> x7, starting transfers between devices: 10.6 us -> 11 us  [the longest x6 7.29 us: shifted(): return lax.ppermute(values, 'sample', pairs)]
  transfers between devices with their start and end apart: 10 -> 12, of which waited for: 5 -> 6; matrix products, arithmetic and copies ran while one was open for 7% -> 5% of each run, Pallas kernels for 7% -> 5%
where the time goes in v3:
time: 220 us; the launch traced here: 217 us
  waiting for transfers between devices  128 us (58%)
  starting transfers between devices  34 us (15%)
  Pallas kernels  33.3 us (15%)
  local copies, waits for them, and re-layouts  11.8 us (5%)
  other arithmetic  7.41 us (3%)
    all_to_all x1, waiting for transfers between devices, on_device(): rows = lax.all_to_all(back, BOTH, 0, 0, tiled=True)  63.1 us
    all_to_all x1, waiting for transfers between devices, on_device(): moved = lax.all_to_all(new_fields, 'sample', 0, 0, tiled=True)  27.3 us
    all_to_all x1, waiting for transfers between devices, on_device(): spectra = lax.all_to_all(message, BOTH, 0, 0, tiled=True)  16.3 us
    pallas_call x1, Pallas kernels, slab_values(): pl.pallas_call(slab_kernel, grid=(3,), in_specs=[piece(lambda i: i), piec...  13 us
    ppermute x6, waiting for transfers between devices, shifted(): return lax.ppermute(values, 'sample', pairs)  12 us
    pallas_call x1, Pallas kernels, spring_free(): pl.pallas_call(functools.partial(free_kernel, scales), grid=(3,), in_spec...  11.7 us
    all_to_all x1, starting transfers between devices, on_device(): spectra = lax.all_to_all(message, BOTH, 0, 0, tiled=True)  9.34 us
    ppermute x1, waiting for transfers between devices, summed(): total = total + lax.ppermute(total, 'sample', pairs)  8.93 us
  transfers between devices with their start and end apart: 12, of which 6 were waited for; matrix products, arithmetic and copies ran while one was open for 5% of the time, Pallas kernels for 5%

profile of v3, /device:TPU:5, one launch (start us, length us, event | category | flops | bytes accessed | tf_op | source)
XLA Modules:
  0.0 217.2 jit_solution(13998402516863335185)
XLA Ops:
  0.6 2.2 multiply_reduce_fusion
  3.0 1.4 collective-permute-start.2
  4.4 2.6 %collective-permute-start.3 = (f32[2,193,128]{2,1,0:T(8,128)S(1)}, f32[2,193,128]{2,1,0:T(8,128)S(1)}, u32[]{:S(2)}, u32[]{:S(2)}) collective-permute-start(f32[2,193,128]{2,1,0:T(8,128)S(1)} %get-tuple-element.13), channel_id=1, source_target_pairs={{0,32},{16,48},{32,0},{48,16},{64,96},{80,112},{96,64},{112,80},{1... | collective-permute-start | bytes 592904 | tf_op jit(solution)/shard_map/ppermute | solution.py:348
  8.6 1.4 copy-done.7
  10.0 1.6 collective-permute-start.1
  11.6 1.6 collective-permute-start
  13.2 2.6 %collective-permute-done.3 = f32[2,193,128]{2,1,0:T(8,128)S(1)} collective-permute-done((f32[2,193,128]{2,1,0:T(8,128)S(1)}, f32[2,193,128]{2,1,0:T(8,128)S(1)}, u32[]{:S(2)}, u32[]{:S(2)}) %collective-permute-start.3) | collective-permute-done | bytes 197664 | tf_op jit(solution)/shard_map/ppermute | solution.py:348
  15.9 3.7 %collective-permute-start.5 = (f32[2,193,128]{2,1,0:T(8,128)S(1)}, f32[2,193,128]{2,1,0:T(8,128)}, u32[]{:S(2)}, u32[]{:S(2)}) collective-permute-start(f32[2,193,128]{2,1,0:T(8,128)S(1)} %fusion.6), channel_id=1, source_target_pairs={{0,64},{16,80},{32,96},{48,112},{64,0},{80,16},{96,32},{112,48},{1... | collective-permute-start | bytes 592904 | tf_op jit(solution)/shard_map/ppermute | solution.py:357
  19.6 8.9 %collective-permute-done.5 = f32[2,193,128]{2,1,0:T(8,128)} collective-permute-done((f32[2,193,128]{2,1,0:T(8,128)S(1)}, f32[2,193,128]{2,1,0:T(8,128)}, u32[]{:S(2)}, u32[]{:S(2)}) %collective-permute-start.5) | collective-permute-done | bytes 197664 | tf_op jit(solution)/shard_map/ppermute | solution.py:357
  30.3 11.7 %shard_map.166 = f32[8,3,193,128]{3,2,1,0:T(8,128)} custom-call(f32[8,3,193,128]{3,2,1,0:T(8,128)} %bitcast.73, f32[3,193,8,128]{3,2,1,0:T(8,128)} %bitcast.78, f32[3,193,8,128]{3,2,1,0:T(8,128)} %bitcast.77, f32[9,193,8,128]{3,2,1,0:T(8,128)} %bitcast.74, f32[3,193,128]{2,1,0:T(8,128)} %collective-permute-done.lo_ref, f32[3,193,128]{2,1,0:T(8,128)} %copy-done.15, ...), custom_call_target="tpu_custom_call" | custom-call | flops 3000000000 | bytes 18000000 | tf_op jit(solution)/shard_map/pallas_call | solution.py:90
  42.0 1.4 collective-permute-start.8
  44.2 9.3 %collective-permute-done.7 = f32[2,193,128]{2,1,0:T(8,128)S(1)} collective-permute-done((f32[2,193,128]{2,1,0:T(8,128)S(1)}, f32[2,193,128]{2,1,0:T(8,128)S(1)}, u32[]{:S(2)}, u32[]{:S(2)}) %collective-permute-start.7) | collective-permute-done | bytes 197664 | tf_op jit(solution)/shard_map/ppermute | solution.py:348
  55.7 2.0 multiply_subtract_fusion
  57.6 3.8 %all-to-all-start = ((f32[8,3,193,128]{3,2,1,0:T(8,128)}), f32[8,3,193,128]{3,2,1,0:T(8,128)S(1)}, u32[]{:S(2)}, u32[]{:S(2)}) async-start(f32[8,3,193,128]{3,2,1,0:T(8,128)} %multiply_subtract_fusion), calls=%async_computation | async-start | bytes 4915200 | tf_op jit(solution)/shard_map/all_to_all | solution.py:400
  61.5 1.9 constant_dynamic-slice_fusion
  66.6 27.3 %all-to-all-done.n_ref = f32[8,3,193,128]{3,2,1,0:T(8,128)S(1)} async-done(((f32[8,3,193,128]{3,2,1,0:T(8,128)}), f32[8,3,193,128]{3,2,1,0:T(8,128)S(1)}, u32[]{:S(2)}, u32[]{:S(2)}) %all-to-all-start) | async-done | bytes 2371616 | tf_op jit(solution)/shard_map/all_to_all | solution.py:400
  94.8 4.2 %shard_map.167 = f32[2048,128]{1,0:T(8,128)} custom-call(f32[8,3,193,128]{3,2,1,0:T(8,128)S(1)} %all-to-all-done.n_ref, f32[193,128]{1,0:T(8,128)S(1)} %dynamic-slice_bitcast_fusion.s_ref, f32[3,256,128]{2,1,0:T(8,128)S(1)} %copy-done, bf16[512,768]{1,0:T(8,128)(2,1)S(1)} %pad_maximum_fusion.m_ref, f32[128,256]{1,0:T(8,128)S(1)} %copy-done.2), custom_call_target="tpu_custom_call" | custom-call | tf_op jit(solution)/shard_map/pallas_call | solution.py:192
  99.1 9.3 %all-to-all-start.1 = ((f32[128,2,8,128]{3,2,1,0:T(8,128)}), f32[128,2,8,128]{3,2,1,0:T(8,128)S(1)}, u32[]{:S(2)}, u32[]{:S(2)}) async-start(f32[128,2,8,128]{3,2,1,0:T(8,128)} %bitcast.26), calls=%async_computation.1 | async-start | bytes 2097152 | tf_op jit(solution)/shard_map/all_to_all | solution.py:419
  109.8 16.3 %all-to-all-done.1.in_ref = f32[128,2,8,128]{3,2,1,0:T(8,128)S(1)} async-done(((f32[128,2,8,128]{3,2,1,0:T(8,128)}), f32[128,2,8,128]{3,2,1,0:T(8,128)S(1)}, u32[]{:S(2)}, u32[]{:S(2)}) %all-to-all-start.1) | async-done | bytes 1048608 | tf_op jit(solution)/shard_map/all_to_all | solution.py:419
  126.1 4.4 %shard_map.168 = f32[128,10,8,128]{3,2,1,0:T(8,128)} custom-call(f32[128,2,8,128]{3,2,1,0:T(8,128)S(1)} %all-to-all-done.1.in_ref, f32[128,256]{1,0:T(8,128)S(1)} %multiply_add_fusion.d_ref, f32[128,128]{1,0:T(8,128)S(1)} %copy-done.4, f32[128,128]{1,0:T(8,128)S(1)} %copy-done.3, f32[256,128]{1,0:T(8,128)S(1)} %copy-done.1), custom_call_target="tpu_custom_call" | custom-call | tf_op jit(solution)/shard_map/pallas_call | solution.py:244
  130.6 6.7 %all-to-all-start.2 = ((f32[128,10,8,128]{3,2,1,0:T(8,128)}), f32[128,10,8,128]{3,2,1,0:T(8,128)}, u32[]{:S(2)}, u32[]{:S(2)}) async-start(f32[128,10,8,128]{3,2,1,0:T(8,128)} %shard_map.168), calls=%async_computation.2 | async-start | bytes 10485760 | tf_op jit(solution)/shard_map/all_to_all | solution.py:436
  139.3 1.8 copy.23
  141.1 63.1 %all-to-all-done.2.u_ref.w_ref.h_ref.l_ref = f32[128,10,8,128]{3,2,1,0:T(8,128)} async-done(((f32[128,10,8,128]{3,2,1,0:T(8,128)}), f32[128,10,8,128]{3,2,1,0:T(8,128)}, u32[]{:S(2)}, u32[]{:S(2)}) %all-to-all-start.2) | async-done | bytes 5242912 | tf_op jit(solution)/shard_map/all_to_all | solution.py:436
  204.2 13.0 %shard_map.169 = (f32[3,193,8,128]{3,2,1,0:T(8,128)}, f32[9,193,8,128]{3,2,1,0:T(8,128)}) custom-call(f32[128,10,8,128]{3,2,1,0:T(8,128)} %all-to-all-done.2.u_ref.w_ref.h_ref.l_ref, f32[128,10,8,128]{3,2,1,0:T(8,128)} %all-to-all-done.2.u_ref.w_ref.h_ref.l_ref, f32[128,10,8,128]{3,2,1,0:T(8,128)} %all-to-all-done.2.u_ref.w_ref.h_ref.l_ref, ...), custom_call_target="tpu_custom_call" | custom-call | tf_op jit(solution)/shard_map/pallas_call | solution.py:316
  (75 shorter events, 13.9 us)
Async XLA Ops:
  2.8 5.3 %copy-start.6 = (f32[3,1,128,8,193]{2,3,4,1,0:T(8,128)S(1)}, f32[3,1,128,8,193]{2,3,4,1,0:T(8,128)}, u32[]{:S(2)}) copy-start(f32[3,1,128,8,193]{2,3,4,1,0:T(8,128)} %param.15) | copy-start | bytes 7114756
  3.0 10.2 %collective-permute-start.2 = (f32[2,193,128]{2,1,0:T(8,128)S(1)}, f32[2,193,128]{2,1,0:T(8,128)S(1)}, u32[]{:S(2)}, u32[]{:S(2)}) collective-permute-start(f32[2,193,128]{2,1,0:T(8,128)S(1)} %get-tuple-element.12), channel_id=1, source_target_pairs={{0,16},{16,32},{32,48},{48,0},{64,80},{80,96},{96,112},{112,64},{1... | collective-permute-start | bytes 592904 | tf_op jit(solution)/shard_map/ppermute | solution.py:348
  4.4 11.5 %collective-permute-start.3 = (f32[2,193,128]{2,1,0:T(8,128)S(1)}, f32[2,193,128]{2,1,0:T(8,128)S(1)}, u32[]{:S(2)}, u32[]{:S(2)}) collective-permute-start(f32[2,193,128]{2,1,0:T(8,128)S(1)} %get-tuple-element.13), channel_id=1, source_target_pairs={{0,32},{16,48},{32,0},{48,16},{64,96},{80,112},{96,64},{112,80},{1... | collective-permute-start | bytes 592904 | tf_op jit(solution)/shard_map/ppermute | solution.py:348
  7.0 8.9 %collective-permute-start.4 = (f32[2,193,128]{2,1,0:T(8,128)S(1)}, f32[2,193,128]{2,1,0:T(8,128)S(1)}, u32[]{:S(2)}, u32[]{:S(2)}) collective-permute-start(f32[2,193,128]{2,1,0:T(8,128)S(1)} %get-tuple-element.14), channel_id=1, source_target_pairs={{0,48},{16,0},{32,16},{48,32},{64,112},{80,64},{96,80},{112,96},{1... | collective-permute-start | bytes 592904 | tf_op jit(solution)/shard_map/ppermute | solution.py:348
  10.0 19.6 %collective-permute-start.1 = (f32[3,193,128]{2,1,0:T(8,128)S(1)}, f32[3,193,128]{2,1,0:T(8,128)S(1)}, u32[]{:S(2)}, u32[]{:S(2)}) collective-permute-start(f32[3,193,128]{2,1,0:T(8,128)S(1)} %get-tuple-element.10), channel_id=1, source_target_pairs={{1,0},{2,1},{3,2},{4,3},{5,4},{6,5},{7,6},{8,7},{9,8},{10,9},{11,1... | collective-permute-start | bytes 889352 | tf_op jit(solution)/shard_map/ppermute | solution.py:384
  11.6 18.0 %collective-permute-start = (f32[3,193,128]{2,1,0:T(8,128)S(1)}, f32[3,193,128]{2,1,0:T(8,128)}, u32[]{:S(2)}, u32[]{:S(2)}) collective-permute-start(f32[3,193,128]{2,1,0:T(8,128)S(1)} %get-tuple-element.11), channel_id=1, source_target_pairs={{0,1},{1,2},{2,3},{3,4},{4,5},{5,6},{6,7},{7,8},{8,9},{9,10},{10,1... | collective-permute-start | bytes 889352 | tf_op jit(solution)/shard_map/ppermute | solution.py:383
  15.9 12.6 %collective-permute-start.5 = (f32[2,193,128]{2,1,0:T(8,128)S(1)}, f32[2,193,128]{2,1,0:T(8,128)}, u32[]{:S(2)}, u32[]{:S(2)}) collective-permute-start(f32[2,193,128]{2,1,0:T(8,128)S(1)} %fusion.6), channel_id=1, source_target_pairs={{0,64},{16,80},{32,96},{48,112},{64,0},{80,16},{96,32},{112,48},{1... | collective-permute-start | bytes 592904 | tf_op jit(solution)/shard_map/ppermute | solution.py:357
  29.5 14.7 %collective-permute-start.6 = (f32[2,193,128]{2,1,0:T(8,128)S(1)}, f32[2,193,128]{2,1,0:T(8,128)S(1)}, u32[]{:S(2)}, u32[]{:S(2)}) collective-permute-start(f32[2,193,128]{2,1,0:T(8,128)S(1)} %add.81), channel_id=1, source_target_pairs={{0,48},{16,0},{32,16},{48,32},{64,112},{80,64},{96,80},{112,96},{1... | collective-permute-start | bytes 592904 | tf_op jit(solution)/shard_map/ppermute | solution.py:348
  42.0 11.5 %collective-permute-start.8 = (f32[2,193,128]{2,1,0:T(8,128)S(1)}, f32[2,193,128]{2,1,0:T(8,128)S(1)}, u32[]{:S(2)}, u32[]{:S(2)}) collective-permute-start(f32[2,193,128]{2,1,0:T(8,128)S(1)} %add.81), channel_id=1, source_target_pairs={{0,16},{16,32},{32,48},{48,0},{64,80},{80,96},{96,112},{112,64},{1... | collective-permute-start | bytes 592904 | tf_op jit(solution)/shard_map/ppermute | solution.py:348
  43.4 10.0 %collective-permute-start.7 = (f32[2,193,128]{2,1,0:T(8,128)S(1)}, f32[2,193,128]{2,1,0:T(8,128)S(1)}, u32[]{:S(2)}, u32[]{:S(2)}) collective-permute-start(f32[2,193,128]{2,1,0:T(8,128)S(1)} %add.81), channel_id=1, source_target_pairs={{0,32},{16,48},{32,0},{48,16},{64,96},{80,112},{96,64},{112,80},{1... | collective-permute-start | bytes 592904 | tf_op jit(solution)/shard_map/ppermute | solution.py:348
  57.6 3.8 %copy-start.10 = (f32[193,193]{1,0:T(8,128)S(1)}, f32[193,193]{1,0:T(8,128)}, u32[]{:S(2)}) copy-start(f32[193,193]{1,0:T(8,128)} %param.20) | copy-start | bytes 446992
  57.6 5.7 %copy-start.12 = (f32[193,193]{1,0:T(8,128)S(1)}, f32[193,193]{1,0:T(8,128)}, u32[]{:S(2)}) copy-start(f32[193,193]{1,0:T(8,128)} %d_ref.1) | copy-start | bytes 446992
  57.6 36.2 %all-to-all-start = ((f32[8,3,193,128]{3,2,1,0:T(8,128)}), f32[8,3,193,128]{3,2,1,0:T(8,128)S(1)}, u32[]{:S(2)}, u32[]{:S(2)}) async-start(f32[8,3,193,128]{3,2,1,0:T(8,128)} %multiply_subtract_fusion), calls=%async_computation | async-start | bytes 4915200 | tf_op jit(solution)/shard_map/all_to_all | solution.py:400
  63.8 30.1 %copy-start.2 = (f32[128,256]{1,0:T(8,128)S(1)}, f32[128,256]{1,0:T(8,128)}, u32[]{:S(2)}) copy-start(f32[128,256]{1,0:T(8,128)} %constant.78.clone.x_ref) | copy-start | bytes 393220
  99.1 9.4 %copy-start.18 = (f32[128]{0:T(128)S(1)}, f32[128]{0:T(128)}, u32[]{:S(2)}) copy-start(f32[128]{0:T(128)} %constant.79.clone) | copy-start | bytes 1540
  99.1 10.0 %copy-start.16 = (f32[193]{0:T(256)S(1)}, f32[193]{0:T(256)}, u32[]{:S(2)}) copy-start(f32[193]{0:T(256)} %param.22) | copy-start | bytes 2320
  99.1 10.0 %copy-start.17 = (f32[128]{0:T(128)S(1)}, f32[128]{0:T(128)}, u32[]{:S(2)}) copy-start(f32[128]{0:T(128)} %constant.80.clone) | copy-start | bytes 1540
  99.1 27.1 %copy-start.1 = (f32[256,128]{1,0:T(8,128)S(1)}, f32[256,128]{1,0:T(8,128)}, u32[]{:S(2)}) copy-start(f32[256,128]{1,0:T(8,128)} %constant.83.clone.b_ref) | copy-start | bytes 393220
  99.1 27.1 %copy-start.3 = (f32[128,128]{1,0:T(8,128)S(1)}, f32[128,128]{1,0:T(8,128)}, u32[]{:S(2)}) copy-start(f32[128,128]{1,0:T(8,128)} %constant.82.clone.g_ref) | copy-start | bytes 196612
  99.1 27.1 %copy-start.4 = (f32[128,128]{1,0:T(8,128)S(1)}, f32[128,128]{1,0:T(8,128)}, u32[]{:S(2)}) copy-start(f32[128,128]{1,0:T(8,128)} %constant.81.clone.f_ref) | copy-start | bytes 196612
  99.1 27.0 %all-to-all-start.1 = ((f32[128,2,8,128]{3,2,1,0:T(8,128)}), f32[128,2,8,128]{3,2,1,0:T(8,128)S(1)}, u32[]{:S(2)}, u32[]{:S(2)}) async-start(f32[128,2,8,128]{3,2,1,0:T(8,128)} %bitcast.26), calls=%async_computation.1 | async-start | bytes 2097152 | tf_op jit(solution)/shard_map/all_to_all | solution.py:419
  130.6 6.8 %copy-start.13 = (f32[193,193]{1,0:T(8,128)S(1)}, f32[193,193]{1,0:T(8,128)}, u32[]{:S(2)}) copy-start(f32[193,193]{1,0:T(8,128)} %d_ref.1) | copy-start | bytes 446992
  130.6 6.8 %copy-start.14 = (f32[193,193]{1,0:T(8,128)S(1)}, f32[193,193]{1,0:T(8,128)}, u32[]{:S(2)}) copy-start(f32[193,193]{1,0:T(8,128)} %param.21) | copy-start | bytes 446992
  130.6 73.6 %all-to-all-start.2 = ((f32[128,10,8,128]{3,2,1,0:T(8,128)}), f32[128,10,8,128]{3,2,1,0:T(8,128)}, u32[]{:S(2)}, u32[]{:S(2)}) async-start(f32[128,10,8,128]{3,2,1,0:T(8,128)} %shard_map.168), calls=%async_computation.2 | async-start | bytes 10485760 | tf_op jit(solution)/shard_map/all_to_all | solution.py:436
  (7 other events, 8.9 us)

commit v4 on v3

--- a/solution.py
+++ b/solution.py
@@ -49,20 +49,29 @@
     return jnp.asarray(np.asarray(values, np.float32))
 
 
-def free_kernel(scales, f_ref, w_ref, v_ref, g_ref, lo_ref, hi_ref, d_ref, o_ref):
+def free_kernel(scales, f_ref, w_ref, v_ref, g_ref, lo_ref, hi_ref, d_ref, e_ref, o_ref):
     scale_x, scale_z, scale_c, scale_w = scales
     i = pl.program_id(0)
     slab, _, size_y, size_x = f_ref.shape
     noise, speed, tensor = [
         r.reshape(r.shape[0], size_y * slab, size_x) for r in (w_ref, v_ref, g_ref)
     ]
+    slopes = []
     for z in range(slab):
         plane = pl.ds(z, size_y, stride=slab)
         own = f_ref[z, i]
+        if z % 2 == 0:
+            pair = jnp.concatenate([own, f_ref[z + 1, i]], axis=1)
+            high = pair.astype(jnp.bfloat16)
+            low = (pair - high.astype(jnp.float32)).astype(jnp.bfloat16)
+            slope = jnp.dot(d_ref[...], high, preferred_element_type=jnp.float32)
+            slope += jnp.dot(d_ref[...], low, preferred_element_type=jnp.float32)
+            slope += jnp.dot(e_ref[...], high, preferred_element_type=jnp.float32)
+            slopes = [slope[:, :size_x], slope[:, size_x:]]
+        slope_y = slopes[z % 2]
         upper = hi_ref[i] if z == slab - 1 else f_ref[z + 1, i]
         lower = lo_ref[i] if z == 0 else f_ref[z - 1, i]
         slope_x = pltpu.roll(own, size_x - 1, 1) - pltpu.roll(own, 1, 1)
-        slope_y = full_dot(d_ref[...], own)
         advect = (
             speed[0, plane, :] * (scale_x * slope_x)
             + speed[1, plane, :] * slope_y
@@ -81,6 +90,9 @@
 def spring_free(planes, wiener, velocity, gradient, below, above, wall_derivative, step_x, step_z):
     slab, _, size_y, size_x = planes.shape
     whole = pl.BlockSpec(memory_space=pltpu.VMEM)
+    high = lax.reduce_precision(wall_derivative, 8, 7)
+    low = (wall_derivative - high).astype(jnp.bfloat16)
+    high = high.astype(jnp.bfloat16)
     scales = (
         1.0 / (2.0 * step_x),
         1.0 / (2.0 * step_z),
@@ -98,12 +110,13 @@
             whole,
             whole,
             whole,
+            whole,
         ],
         out_specs=pl.BlockSpec((slab, 1, size_y, size_x), lambda i: (0, i, 0, 0)),
         out_shape=pltpu.HBM(planes.shape, jnp.float32),
         compiler_params=pltpu.CompilerParams(vmem_limit_bytes=60 * 1024 * 1024),
         cost_estimate=pl.CostEstimate(flops=3 * 10**9, bytes_accessed=18 * 10**6, transcendentals=0),
-    )(planes, wiener, velocity, gradient, below, above, wall_derivative)
+    )(planes, wiener, velocity, gradient, below, above, high, low)
 
 
 def padded(values, rows, columns):
@@ -166,6 +179,8 @@
                 value = spring * (t_ref[p, part, :] / count)
                 t_ref[p, part, :] = value - 1.0 if i == j else value
         scaled, slope = m_ref[:LANES, :], m_ref[LANES:, :]
+        last_mode = size_y - 1
+        rest = [None] * 6
         for i in range(3):
             column = [t_ref[p] for p in COLUMN[i]]
             direct = v_ref[i] + jnp.dot(
@@ -180,10 +195,24 @@
                 x_ref[...], jnp.concatenate([direct, along[:, :size_x]], axis=1), 1
             )
             force_z = full_dot(x_ref[:, :size_x], along[:, size_x:], 1)
+            top = slice(last_mode, last_mode + 8)
+            own = jnp.concatenate([direct[top], along[top, :size_x]], axis=1)
+            rest[i] = full_dot(own, x_ref[...], 1)[:1]
+            rest[3 + i] = full_dot(along[top, size_x:], x_ref[:, :size_x], 1)[:1]
             for half in range(2):
                 lanes = slice(half * 128, half * 128 + 128)
                 o_ref[pl.ds(8 * half + i, 128, stride=16), :] = force[:, lanes]
                 o_ref[pl.ds(8 * half + 3 + i, 128, stride=16), :] = force_z[:, lanes]
+        lane = lax.broadcasted_iota(jnp.int32, (128, 128), 1)
+        for c in range(2):
+            o_ref[pl.ds(6 + c, 128, stride=16), :] = jnp.broadcast_to(rest[c], (128, 128))
+        for c in range(4):
+            for part in range(2):
+                row = jnp.broadcast_to(rest[2 + c], (128, 128))
+                row = row if part else pltpu.roll(row, 64, 1)
+                place = pl.ds(8 + 2 * c + part, 128, stride=16)
+                kept = o_ref[place, :] if 2 * c + part < 6 else jnp.zeros_like(row)
+                o_ref[place, :] = jnp.where(lane < 64, kept, row)
 
 
 def own_plane(moved, spring, modes_velocity, modes, rows):
@@ -207,15 +236,15 @@
     return message.reshape(size_x, 2, 8, 128)
 
 
-def row_kernel(spans, in_ref, d_ref, f_ref, g_ref, b_ref, o_ref, t_ref, sem):
+def row_kernel(spans, in_ref, d_ref, e_ref, f_ref, g_ref, b_ref, w_ref, o_ref, l_ref, t_ref, sem):
     flat = in_ref.reshape(in_ref.shape[0] * 16, 128)
     lane = lax.broadcasted_iota(jnp.int32, (128, 128), 1)
-    last = jnp.zeros((128, 128), jnp.float32)
+
+    def taken(c):
+        return flat[pl.ds(c, 128, stride=16), :]
 
     def loaded(c):
-        return jnp.concatenate(
-            [flat[pl.ds(8 * half + c, 128, stride=16), :] for half in range(2)], axis=1
-        )
+        return jnp.concatenate([taken(c), taken(8 + c)], axis=1)
 
     for i in range(3):
         solved = full_dot(f_ref[...], loaded(i)) + full_dot(g_ref[...], loaded(3 + i))
@@ -223,42 +252,53 @@
         value, slope = both[:128], both[128:]
         t_ref[:, i] = value[:, :128].reshape(spans, 8, 128)
         t_ref[:, 3 + i] = slope[:, :128].reshape(spans, 8, 128)
-        value, slope = value[:, 128:], slope[:, 128:]
-        mixed = jnp.where(lane < 64, value, pltpu.roll(slope, 64, 1))
+        mixed = jnp.where(lane < 64, value[:, 128:], pltpu.roll(slope[:, 128:], 64, 1))
         t_ref[:, 6 + i] = mixed.reshape(spans, 8, 128)
-        last = jnp.where(lane == i, pltpu.roll(value, 64 + i, 1), last)
-        last = jnp.where(lane == 3 + i, pltpu.roll(slope, 67 + i, 1), last)
-    t_ref[:, 9] = last.reshape(spans, 8, 128)
     copies = [
         pltpu.make_async_copy(t_ref, o_ref.at[pl.ds(k * spans, spans)], sem.at[k])
         for k in range(o_ref.shape[0] // spans)
     ]
     for copy in copies:
         copy.start()
+
+    def last(c):
+        if c < 2:
+            return taken(6 + c)
+        first, second = taken(8 + 2 * (c - 2)), taken(9 + 2 * (c - 2))
+        return jnp.where(lane < 64, pltpu.roll(first, 64, 1), second)
+
+    for i in range(3):
+        solved = full_dot(f_ref[...], last(i)) + full_dot(g_ref[...], last(3 + i))
+        both = full_dot(w_ref[...], solved / e_ref[...])
+        l_ref[i] = both[:8]
+        l_ref[3 + i] = both[8:]
     for copy in copies:
         copy.wait()
 
 
-def own_row(spectra, damping, forward, forward_slope, inverse, samples, spans):
+def own_row(spectra, damping, last_damping, forward, forward_slope, inverse, slab_inverse, samples, spans):
     whole = pl.BlockSpec(memory_space=pltpu.VMEM)
     return pl.pallas_call(
         functools.partial(row_kernel, spans),
-        in_specs=[whole] * 5,
-        out_specs=pl.BlockSpec(memory_space=pltpu.HBM),
-        out_shape=pltpu.HBM((samples * spans, 10, 8, 128), jnp.float32),
+        in_specs=[whole] * 7,
+        out_specs=(pl.BlockSpec(memory_space=pltpu.HBM), whole),
+        out_shape=(
+            pltpu.HBM((samples * spans, 9, 8, 128), jnp.float32),
+            jax.ShapeDtypeStruct((6, 8, 128), jnp.float32),
+        ),
         scratch_shapes=[
-            pltpu.VMEM((spans, 10, 8, 128), jnp.float32),
+            pltpu.VMEM((spans, 9, 8, 128), jnp.float32),
             pltpu.SemaphoreType.DMA((samples,)),
         ],
         compiler_params=pltpu.CompilerParams(vmem_limit_bytes=32 * 1024 * 1024),
-    )(spectra, damping, forward, forward_slope, inverse)
-
-
-def slab_kernel(u_ref, w_ref, h_ref, l_ref, t_ref, x_ref, v_ref, g_ref):
+    )(spectra, damping, last_damping, forward, forward_slope, inverse, slab_inverse)
+
+
+def slab_kernel(u_ref, w_ref, h_ref, l_ref, t_ref, c_ref, x_ref, v_ref, g_ref):
     i = pl.program_id(0)
     rows = u_ref.shape[0]
     _, size_y, slab, size_x = v_ref.shape
-    flat = [r.reshape(rows * slab, 128) for r in (u_ref, w_ref, h_ref, l_ref)]
+    flat = [r.reshape(rows * slab, 128) for r in (u_ref, w_ref, h_ref)]
     out_v = v_ref.reshape(size_y * slab, size_x)
     out_g = g_ref.reshape(3, size_y * slab, size_x)
     lane = lax.broadcasted_iota(jnp.int32, (rows, 128), 1)
@@ -266,13 +306,9 @@
     for first in range(0, slab, 2):
         values, slopes = [], []
         for z in (first, first + 1):
-            value, slope, high, last = [r[pl.ds(z, rows, stride=slab), :] for r in flat]
-            value_high = jnp.where(lane < 64, high, pltpu.roll(last, 64 - i, 1))
-            slope_high = jnp.where(
-                lane < 64, pltpu.roll(high, 64, 1), pltpu.roll(last, 61 - i, 1)
-            )
-            value_high = jnp.where(lane <= 64, value_high, 0.0)
-            slope_high = jnp.where(lane <= 64, slope_high, 0.0)
+            value, slope, high = [r[pl.ds(z, rows, stride=slab), :] for r in flat]
+            value_high = jnp.where(lane < 64, high, 0.0)
+            slope_high = jnp.where(lane < 64, pltpu.roll(high, 64, 1), 0.0)
             values.append(jnp.concatenate([value, value_high], axis=1))
             slopes.append(jnp.concatenate([slope, slope_high], axis=1))
         across = (((1,), (1,)), ((), ()))
@@ -291,13 +327,15 @@
         for k, z in enumerate((first, first + 1)):
             place = pl.ds(z, size_y, stride=slab)
             lanes = slice(k * rows, k * rows + rows)
+            value_z = value[:, lanes] + c_ref[...] * l_ref[i, pl.ds(z, 1), :]
+            slope_z = slope[:, lanes] + c_ref[:half] * l_ref[3 + i, pl.ds(z, 1), :]
             both = jnp.dot(
-                three_of(value[:half, lanes], 1), x_ref[...], preferred_element_type=jnp.float32
+                three_of(value_z[:half], 1), x_ref[...], preferred_element_type=jnp.float32
             )
             out_v[place, :] = both[:size_y, :size_x]
             out_g[0, place, :] = both[:size_y, size_x:]
             both = jnp.dot(
-                three_of(jnp.concatenate([value[half:, lanes], slope[:, lanes]], axis=0), 1),
+                three_of(jnp.concatenate([value_z[half:], slope_z], axis=0), 1),
                 x_ref[:, :size_x],
                 preferred_element_type=jnp.float32,
             )
@@ -305,7 +343,7 @@
             out_g[2, place, :] = both[half : half + size_y]
 
 
-def slab_values(rows, wall_table, table_x, size_y):
+def slab_values(rows, last, wall_table, last_column, table_x, size_y):
     count = rows.shape[0]
     slab, size_x = rows.shape[2], table_x.shape[1] // 2
     whole = pl.BlockSpec(memory_space=pltpu.VMEM)
@@ -320,7 +358,8 @@
             piece(lambda i: i),
             piece(lambda i: i + 3),
             piece(lambda i: i + 6),
-            piece(lambda i: 9),
+            whole,
+            whole,
             whole,
             whole,
         ],
@@ -333,10 +372,10 @@
             jax.ShapeDtypeStruct((9, size_y, slab, size_x), jnp.float32),
         ),
         compiler_params=pltpu.CompilerParams(vmem_limit_bytes=60 * 1024 * 1024),
-    )(rows, rows, rows, rows, wall_table, table_x)
-
-
-def summed(planes):
+    )(rows, rows, rows, last, wall_table, last_column, table_x)
+
+
+def summed(planes, beside):
     count = lax.axis_size("sample")
     ring = count // 2
     index = lax.axis_index("sample")
@@ -355,10 +394,11 @@
         total = total + part
     pairs = [(i, (i + ring) % count) for i in range(count)]
     total = total + lax.ppermute(total, "sample", pairs)
+    total, beside = lax.optimization_barrier((total, beside))
     parts = [shifted(total, k) for k in range(ring - 1, 0, -1)] + [total]
     start = (ring - 1 - place) % ring
     gathered = lax.dynamic_slice_in_dim(jnp.stack(parts + parts), start, ring, axis=0)
-    return gathered.reshape(planes.shape)
+    return gathered.reshape(planes.shape), beside
 
 
 def on_device(
@@ -382,7 +422,6 @@
     back = [((i + 1) % spans, i) for i in range(spans)]
     below = lax.ppermute(field[-1], "span", ahead)
     above = lax.ppermute(field[0], "span", back)
-    total_square = summed(jnp.sum(field * field, axis=1))
     speed = jnp.transpose(velocity, (0, 3, 2, 1))
     free = spring_free(
         field,
@@ -395,6 +434,7 @@
         step_x,
         step_z,
     )
+    total_square, free = summed(jnp.sum(field * field, axis=1), free)
     slab_spring = 1.0 / (1.0 - total_square / samples / EXTENSIBILITY)
     new_fields = free - relax * slab_spring[:, None] * field
     moved = lax.all_to_all(new_fields, "sample", 0, 0, tiled=True)
@@ -424,12 +464,21 @@
     damping = 1.0 + TIME_STEP * VISCOSITY * (
         square_row + f32(square_z)[:, None] + rates
     )
-    back = own_row(
+    last_damping = 1.0 + TIME_STEP * VISCOSITY * (
+        f32(square_x)[None, :] + f32(square_z)[:, None] + mode_rates[size_y - 1]
+    )
+    inverse = np.stack([rows_z.T, rows_z.T @ slope_rows_z])
+    slab_inverse = lax.dynamic_index_in_dim(
+        f32(inverse.reshape(2, spans, slab, size_z)), lax.axis_index("span"), 1, keepdims=False
+    ).reshape(2 * slab, size_z)
+    back, last = own_row(
         spectra,
         damping,
+        last_damping,
         f32(rows_z[:, order]),
         f32((slope_rows_z @ rows_z)[:, order]),
-        f32(np.concatenate([rows_z.T, rows_z.T @ slope_rows_z])),
+        f32(inverse.reshape(2 * size_z, size_z)),
+        slab_inverse,
         samples,
         spans,
     )
@@ -441,7 +490,9 @@
     )
     new_velocity, new_gradient = slab_values(
         rows,
-        split_three(wall_table, 1),
+        last,
+        split_three(wall_table.at[:, size_y - 1].set(0.0), 1),
+        jnp.broadcast_to(wall_table[:, size_y - 1 : size_y], (wall_table.shape[0], 128)),
         stacked_three(np.concatenate([rows_x, (rows_x.T @ slope_rows_x).T], axis=1)),
         size_y,
     )

time: 220 us -> 212 us (0.964)
  waiting for transfers between devices: 128 us -> 110 us
  starting transfers between devices: 34 us -> 39.7 us
  local copies, waits for them, and re-layouts: 11.8 us -> 14.9 us
  other arithmetic: 7.41 us -> 10.5 us
    ppermute x1, waiting for transfers between devices: 8.93 us -> 0.01 us  [summed(): total = total + lax.ppermute(total, 'sample', pairs)]
    all_to_all x1, waiting for transfers between devices: 63.1 us -> 55.1 us  [on_device(): rows = lax.all_to_all(back, BOTH, 0, 0, tiled=True)]
    all_to_all x1, starting transfers between devices: 9.34 us -> 13.5 us  [on_device(): spectra = lax.all_to_all(message, BOTH, 0, 0, tiled=True)]
    unnamed x47 -> x51, local copies, waits for them, and re-layouts: 8.29 us -> 8.44 us
  transfers between devices with their start and end apart: 12 -> 12, of which waited for: 6 -> 8; matrix products, arithmetic and copies ran while one was open for 5% -> 7% of each run, Pallas kernels for 5% -> 5%
where the time goes in v4:
time: 212 us; the launch traced here: 211 us
  waiting for transfers between devices  110 us (52%)
  starting transfers between devices  39.7 us (19%)
  Pallas kernels  32.8 us (15%)
  local copies, waits for them, and re-layouts  14.9 us (7%)
  other arithmetic  10.5 us (5%)
    all_to_all x1, waiting for transfers between devices, on_device(): rows = lax.all_to_all(back, BOTH, 0, 0, tiled=True)  55.1 us
    all_to_all x1, waiting for transfers between devices, on_device(): moved = lax.all_to_all(new_fields, 'sample', 0, 0, tiled=True)  27.4 us
    all_to_all x1, waiting for transfers between devices, on_device(): spectra = lax.all_to_all(message, BOTH, 0, 0, tiled=True)  14.3 us
    all_to_all x1, starting transfers between devices, on_device(): spectra = lax.all_to_all(message, BOTH, 0, 0, tiled=True)  13.5 us
    pallas_call x1, Pallas kernels, slab_values(): pl.pallas_call(slab_kernel, grid=(3,), in_specs=[piece(lambda i: i), piec...  12.6 us
    ppermute x6, waiting for transfers between devices, shifted(): return lax.ppermute(values, 'sample', pairs)  12.1 us
    pallas_call x1, Pallas kernels, spring_free(): pl.pallas_call(functools.partial(free_kernel, scales), grid=(3,), in_spec...  10.2 us
    unnamed x51, local copies, waits for them, and re-layouts  8.44 us
  transfers between devices with their start and end apart: 12, of which 8 were waited for; matrix products, arithmetic and copies ran while one was open for 7% of the time, Pallas kernels for 5%

profile of v4, /device:TPU:5, one launch (start us, length us, event | category | flops | bytes accessed | tf_op | source)
XLA Modules:
  0.0 211.1 jit_solution(4361682321201437579)
XLA Ops:
  0.6 2.2 %multiply_reduce_fusion = f32[8,193,128]{2,1,0:T(8,128)S(1)} fusion(f32[3,1,128,8,193]{2,3,4,1,0:T(8,128)} %param.20), kind=kLoop, calls=%fused_computation.2 | loop fusion | flops 988160 | bytes 3162112 | tf_op jit(solution)/shard_map/reduce_sum | solution.py:437
  4.4 2.6 %collective-permute-start.1 = (f32[2,193,128]{2,1,0:T(8,128)S(1)}, f32[2,193,128]{2,1,0:T(8,128)S(1)}, u32[]{:S(2)}, u32[]{:S(2)}) collective-permute-start(f32[2,193,128]{2,1,0:T(8,128)S(1)} %get-tuple-element.36), channel_id=1, source_target_pairs={{0,32},{16,48},{32,0},{48,16},{64,96},{80,112},{96,64},{112,80},{1... | collective-permute-start | bytes 592904 | tf_op jit(solution)/shard_map/ppermute | solution.py:387
  8.6 1.4 copy-done.8
  10.0 1.6 collective-permute-start.5
  11.6 1.6 collective-permute-start.4
  13.9 1.9 collective-permute-done.1
  15.9 3.7 %collective-permute-start.3 = (f32[2,193,128]{2,1,0:T(8,128)S(1)}, f32[2,193,128]{2,1,0:T(8,128)}, u32[]{:S(2)}, u32[]{:S(2)}) collective-permute-start(f32[2,193,128]{2,1,0:T(8,128)S(1)} %fusion.7), channel_id=1, source_target_pairs={{0,64},{16,80},{32,96},{48,112},{64,0},{80,16},{96,32},{112,48},{1... | collective-permute-start | bytes 592904 | tf_op jit(solution)/shard_map/ppermute | solution.py:396
  21.8 10.2 %shard_map.193 = f32[8,3,193,128]{3,2,1,0:T(8,128)} custom-call(f32[8,3,193,128]{3,2,1,0:T(8,128)} %bitcast.76, f32[3,193,8,128]{3,2,1,0:T(8,128)} %bitcast.81, f32[3,193,8,128]{3,2,1,0:T(8,128)} %bitcast.80, f32[9,193,8,128]{3,2,1,0:T(8,128)} %bitcast.77, f32[3,193,128]{2,1,0:T(8,128)} %copy-done.17, f32[3,193,128]{2,1,0:T(8,128)} %copy-done.16, ...), custom_call_target="tpu_custom_call" | custom-call | flops 3000000000 | bytes 18000000 | tf_op jit(solution)/shard_map/pallas_call | solution.py:102
  33.0 1.5 collective-permute-start.6
  35.8 3.4 %collective-permute-done.6 = f32[2,193,128]{2,1,0:T(8,128)S(1)} collective-permute-done((f32[2,193,128]{2,1,0:T(8,128)S(1)}, f32[2,193,128]{2,1,0:T(8,128)S(1)}, u32[]{:S(2)}, u32[]{:S(2)}) %collective-permute-start.6) | collective-permute-done | bytes 197664 | tf_op jit(solution)/shard_map/ppermute | solution.py:387
  39.2 4.0 %collective-permute-done.7 = f32[2,193,128]{2,1,0:T(8,128)S(1)} collective-permute-done((f32[2,193,128]{2,1,0:T(8,128)S(1)}, f32[2,193,128]{2,1,0:T(8,128)S(1)}, u32[]{:S(2)}, u32[]{:S(2)}) %collective-permute-start.7) | collective-permute-done | bytes 197664 | tf_op jit(solution)/shard_map/ppermute | solution.py:387
  43.2 2.7 %collective-permute-done.8 = f32[2,193,128]{2,1,0:T(8,128)S(1)} collective-permute-done((f32[2,193,128]{2,1,0:T(8,128)S(1)}, f32[2,193,128]{2,1,0:T(8,128)S(1)}, u32[]{:S(2)}, u32[]{:S(2)}) %collective-permute-start.8) | collective-permute-done | bytes 197664 | tf_op jit(solution)/shard_map/ppermute | solution.py:387
  48.1 2.0 multiply_subtract_fusion
  50.1 4.8 %all-to-all-start = ((f32[8,3,193,128]{3,2,1,0:T(8,128)}), f32[8,3,193,128]{3,2,1,0:T(8,128)S(1)}, u32[]{:S(2)}, u32[]{:S(2)}) async-start(f32[8,3,193,128]{3,2,1,0:T(8,128)} %multiply_subtract_fusion), calls=%async_computation | async-start | bytes 4915200 | tf_op jit(solution)/shard_map/all_to_all | solution.py:440
  54.9 1.9 constant_dynamic-slice_fusion
  60.0 27.4 %all-to-all-done.n_ref = f32[8,3,193,128]{3,2,1,0:T(8,128)S(1)} async-done(((f32[8,3,193,128]{3,2,1,0:T(8,128)}), f32[8,3,193,128]{3,2,1,0:T(8,128)S(1)}, u32[]{:S(2)}, u32[]{:S(2)}) %all-to-all-start) | async-done | bytes 2371616 | tf_op jit(solution)/shard_map/all_to_all | solution.py:440
  88.3 5.0 %shard_map.194 = f32[2048,128]{1,0:T(8,128)} custom-call(f32[8,3,193,128]{3,2,1,0:T(8,128)S(1)} %all-to-all-done.n_ref, f32[193,128]{1,0:T(8,128)S(1)} %dynamic-slice_bitcast_fusion.s_ref, f32[3,256,128]{2,1,0:T(8,128)S(1)} %copy-done, bf16[512,768]{1,0:T(8,128)(2,1)S(1)} %pad_maximum_fusion.m_ref, f32[128,256]{1,0:T(8,128)S(1)} %copy-done.2), custom_call_target="tpu_custom_call" | custom-call | tf_op jit(solution)/shard_map/pallas_call | solution.py:221
  93.4 13.5 %all-to-all-start.1 = ((f32[128,2,8,128]{3,2,1,0:T(8,128)}), f32[128,2,8,128]{3,2,1,0:T(8,128)S(1)}, u32[]{:S(2)}, u32[]{:S(2)}) async-start(f32[128,2,8,128]{3,2,1,0:T(8,128)} %bitcast.26), calls=%async_computation.1 | async-start | bytes 2097152 | tf_op jit(solution)/shard_map/all_to_all | solution.py:459
  110.3 14.3 %all-to-all-done.1.in_ref = f32[128,2,8,128]{3,2,1,0:T(8,128)S(1)} async-done(((f32[128,2,8,128]{3,2,1,0:T(8,128)}), f32[128,2,8,128]{3,2,1,0:T(8,128)S(1)}, u32[]{:S(2)}, u32[]{:S(2)}) %all-to-all-start.1) | async-done | bytes 1048608 | tf_op jit(solution)/shard_map/all_to_all | solution.py:459
  124.6 4.9 %shard_map.195 = (f32[128,9,8,128]{3,2,1,0:T(8,128)}, f32[6,8,128]{2,1,0:T(8,128)S(1)}) custom-call(f32[128,2,8,128]{3,2,1,0:T(8,128)S(1)} %all-to-all-done.1.in_ref, f32[128,256]{1,0:T(8,128)S(1)} %multiply_add_fusion.d_ref, f32[128,128]{1,0:T(8,128)S(1)} %multiply_add_fusion.1.e_ref, f32[128,128]{1,0:T(8,128)S(1)} %copy-done.4, f32[128,128]{1,0:T(8,128)S(1)} %copy-done.3, ...), custom_call_target="tpu_custom_call" | custom-call | tf_op jit(solution)/shard_map/pallas_call | solution.py:281
  130.1 6.7 %all-to-all-start.2 = ((f32[128,9,8,128]{3,2,1,0:T(8,128)}), f32[128,9,8,128]{3,2,1,0:T(8,128)}, u32[]{:S(2)}, u32[]{:S(2)}) async-start(f32[128,9,8,128]{3,2,1,0:T(8,128)} %get-tuple-element.23), calls=%async_computation.2 | async-start | bytes 9437184 | tf_op jit(solution)/shard_map/all_to_all | solution.py:485
  140.8 1.8 copy.32
  142.6 55.1 %all-to-all-done.2.u_ref.w_ref.h_ref = f32[128,9,8,128]{3,2,1,0:T(8,128)} async-done(((f32[128,9,8,128]{3,2,1,0:T(8,128)}), f32[128,9,8,128]{3,2,1,0:T(8,128)}, u32[]{:S(2)}, u32[]{:S(2)}) %all-to-all-start.2) | async-done | bytes 4718624 | tf_op jit(solution)/shard_map/all_to_all | solution.py:485
  198.5 12.6 %shard_map.196 = (f32[3,193,8,128]{3,2,1,0:T(8,128)}, f32[9,193,8,128]{3,2,1,0:T(8,128)}) custom-call(f32[128,9,8,128]{3,2,1,0:T(8,128)} %all-to-all-done.2.u_ref.w_ref.h_ref, f32[128,9,8,128]{3,2,1,0:T(8,128)} %all-to-all-done.2.u_ref.w_ref.h_ref, f32[128,9,8,128]{3,2,1,0:T(8,128)} %all-to-all-done.2.u_ref.w_ref.h_ref, f32[6,8,128]{2,1,0:T(8,128)} %copy-done.5, ...), custom_call_target="tpu_custom_call" | custom-call | tf_op jit(solution)/shard_map/pallas_call | solution.py:354
  (88 shorter events, 23.3 us)
Async XLA Ops:
  2.8 5.3 %copy-start.7 = (f32[3,1,128,8,193]{2,3,4,1,0:T(8,128)S(1)}, f32[3,1,128,8,193]{2,3,4,1,0:T(8,128)}, u32[]{:S(2)}) copy-start(f32[3,1,128,8,193]{2,3,4,1,0:T(8,128)} %param.20) | copy-start | bytes 7114756
  3.0 10.9 %collective-permute-start = (f32[2,193,128]{2,1,0:T(8,128)S(1)}, f32[2,193,128]{2,1,0:T(8,128)S(1)}, u32[]{:S(2)}, u32[]{:S(2)}) collective-permute-start(f32[2,193,128]{2,1,0:T(8,128)S(1)} %get-tuple-element.35), channel_id=1, source_target_pairs={{0,16},{16,32},{32,48},{48,0},{64,80},{80,96},{96,112},{112,64},{1... | collective-permute-start | bytes 592904 | tf_op jit(solution)/shard_map/ppermute | solution.py:387
  4.4 11.5 %collective-permute-start.1 = (f32[2,193,128]{2,1,0:T(8,128)S(1)}, f32[2,193,128]{2,1,0:T(8,128)S(1)}, u32[]{:S(2)}, u32[]{:S(2)}) collective-permute-start(f32[2,193,128]{2,1,0:T(8,128)S(1)} %get-tuple-element.36), channel_id=1, source_target_pairs={{0,32},{16,48},{32,0},{48,16},{64,96},{80,112},{96,64},{112,80},{1... | collective-permute-start | bytes 592904 | tf_op jit(solution)/shard_map/ppermute | solution.py:387
  7.0 6.2 %copy-start.13 = (f32[193,193]{1,0:T(8,128)S(1)}, f32[193,193]{1,0:T(8,128)}, u32[]{:S(2)}) copy-start(f32[193,193]{1,0:T(8,128)} %param.24) | copy-start | bytes 446992
  7.0 8.9 %collective-permute-start.2 = (f32[2,193,128]{2,1,0:T(8,128)S(1)}, f32[2,193,128]{2,1,0:T(8,128)S(1)}, u32[]{:S(2)}, u32[]{:S(2)}) collective-permute-start(f32[2,193,128]{2,1,0:T(8,128)S(1)} %get-tuple-element.37), channel_id=1, source_target_pairs={{0,48},{16,0},{32,16},{48,32},{64,112},{80,64},{96,80},{112,96},{1... | collective-permute-start | bytes 592904 | tf_op jit(solution)/shard_map/ppermute | solution.py:387
  10.0 10.9 %collective-permute-start.5 = (f32[3,193,128]{2,1,0:T(8,128)S(1)}, f32[3,193,128]{2,1,0:T(8,128)S(1)}, u32[]{:S(2)}, u32[]{:S(2)}) collective-permute-start(f32[3,193,128]{2,1,0:T(8,128)S(1)} %get-tuple-element.33), channel_id=1, source_target_pairs={{1,0},{2,1},{3,2},{4,3},{5,4},{6,5},{7,6},{8,7},{9,8},{10,9},{11,1... | collective-permute-start | bytes 889352 | tf_op jit(solution)/shard_map/ppermute | solution.py:424
  11.6 9.4 %collective-permute-start.4 = (f32[3,193,128]{2,1,0:T(8,128)S(1)}, f32[3,193,128]{2,1,0:T(8,128)S(1)}, u32[]{:S(2)}, u32[]{:S(2)}) collective-permute-start(f32[3,193,128]{2,1,0:T(8,128)S(1)} %get-tuple-element.34), channel_id=1, source_target_pairs={{0,1},{1,2},{2,3},{3,4},{4,5},{5,6},{6,7},{7,8},{8,9},{9,10},{10,1... | collective-permute-start | bytes 889352 | tf_op jit(solution)/shard_map/ppermute | solution.py:423
  15.9 16.1 %collective-permute-start.3 = (f32[2,193,128]{2,1,0:T(8,128)S(1)}, f32[2,193,128]{2,1,0:T(8,128)}, u32[]{:S(2)}, u32[]{:S(2)}) collective-permute-start(f32[2,193,128]{2,1,0:T(8,128)S(1)} %fusion.7), channel_id=1, source_target_pairs={{0,64},{16,80},{32,96},{48,112},{64,0},{80,16},{96,32},{112,48},{1... | collective-permute-start | bytes 592904 | tf_op jit(solution)/shard_map/ppermute | solution.py:396
  33.0 6.2 %collective-permute-start.6 = (f32[2,193,128]{2,1,0:T(8,128)S(1)}, f32[2,193,128]{2,1,0:T(8,128)S(1)}, u32[]{:S(2)}, u32[]{:S(2)}) collective-permute-start(f32[2,193,128]{2,1,0:T(8,128)S(1)} %add.112), channel_id=1, source_target_pairs={{0,48},{16,0},{32,16},{48,32},{64,112},{80,64},{96,80},{112,96},{1... | collective-permute-start | bytes 592904 | tf_op jit(solution)/shard_map/ppermute | solution.py:387
  34.5 11.5 %collective-permute-start.8 = (f32[2,193,128]{2,1,0:T(8,128)S(1)}, f32[2,193,128]{2,1,0:T(8,128)S(1)}, u32[]{:S(2)}, u32[]{:S(2)}) collective-permute-start(f32[2,193,128]{2,1,0:T(8,128)S(1)} %add.112), channel_id=1, source_target_pairs={{0,16},{16,32},{32,48},{48,0},{64,80},{80,96},{96,112},{112,64},{1... | collective-permute-start | bytes 592904 | tf_op jit(solution)/shard_map/ppermute | solution.py:387
  34.5 8.7 %collective-permute-start.7 = (f32[2,193,128]{2,1,0:T(8,128)S(1)}, f32[2,193,128]{2,1,0:T(8,128)S(1)}, u32[]{:S(2)}, u32[]{:S(2)}) collective-permute-start(f32[2,193,128]{2,1,0:T(8,128)S(1)} %add.112), channel_id=1, source_target_pairs={{0,32},{16,48},{32,0},{48,16},{64,96},{80,112},{96,64},{112,80},{1... | collective-permute-start | bytes 592904 | tf_op jit(solution)/shard_map/ppermute | solution.py:387
  50.1 4.8 %copy-start.11 = (f32[193,193]{1,0:T(8,128)S(1)}, f32[193,193]{1,0:T(8,128)}, u32[]{:S(2)}) copy-start(f32[193,193]{1,0:T(8,128)} %param.25) | copy-start | bytes 446992
  50.1 37.3 %all-to-all-start = ((f32[8,3,193,128]{3,2,1,0:T(8,128)}), f32[8,3,193,128]{3,2,1,0:T(8,128)S(1)}, u32[]{:S(2)}, u32[]{:S(2)}) async-start(f32[8,3,193,128]{3,2,1,0:T(8,128)} %multiply_subtract_fusion), calls=%async_computation | async-start | bytes 4915200 | tf_op jit(solution)/shard_map/all_to_all | solution.py:440
  57.2 30.2 %copy-start.2 = (f32[128,256]{1,0:T(8,128)S(1)}, f32[128,256]{1,0:T(8,128)}, u32[]{:S(2)}) copy-start(f32[128,256]{1,0:T(8,128)} %constant.117.clone.x_ref) | copy-start | bytes 393220
  93.4 13.6 %copy-start.18 = (f32[193]{0:T(256)S(1)}, f32[193]{0:T(256)}, u32[]{:S(2)}) copy-start(f32[193]{0:T(256)} %param.27) | copy-start | bytes 2320
  93.4 14.2 %copy-start.19 = (f32[128]{0:T(128)S(1)}, f32[128]{0:T(128)}, u32[]{:S(2)}) copy-start(f32[128]{0:T(128)} %constant.118.clone) | copy-start | bytes 1540
  93.4 15.4 %copy-start.20 = (f32[128]{0:T(128)S(1)}, f32[128]{0:T(128)}, u32[]{:S(2)}) copy-start(f32[128]{0:T(128)} %constant.119.clone) | copy-start | bytes 1540
  93.4 31.3 %copy-start.1 = (f32[256,128]{1,0:T(8,128)S(1)}, f32[256,128]{1,0:T(8,128)}, u32[]{:S(2)}) copy-start(f32[256,128]{1,0:T(8,128)} %constant.123.clone.b_ref) | copy-start | bytes 393220
  93.4 31.3 %copy-start.3 = (f32[128,128]{1,0:T(8,128)S(1)}, f32[128,128]{1,0:T(8,128)}, u32[]{:S(2)}) copy-start(f32[128,128]{1,0:T(8,128)} %constant.122.clone.g_ref) | copy-start | bytes 196612
  93.4 31.2 %copy-start.4 = (f32[128,128]{1,0:T(8,128)S(1)}, f32[128,128]{1,0:T(8,128)}, u32[]{:S(2)}) copy-start(f32[128,128]{1,0:T(8,128)} %constant.121.clone.f_ref) | copy-start | bytes 196612
  93.4 31.2 %all-to-all-start.1 = ((f32[128,2,8,128]{3,2,1,0:T(8,128)}), f32[128,2,8,128]{3,2,1,0:T(8,128)S(1)}, u32[]{:S(2)}, u32[]{:S(2)}) async-start(f32[128,2,8,128]{3,2,1,0:T(8,128)} %bitcast.26), calls=%async_computation.1 | async-start | bytes 2097152 | tf_op jit(solution)/shard_map/all_to_all | solution.py:459
  130.1 7.3 %copy-start.14 = (f32[193,193]{1,0:T(8,128)S(1)}, f32[193,193]{1,0:T(8,128)}, u32[]{:S(2)}) copy-start(f32[193,193]{1,0:T(8,128)} %param.24) | copy-start | bytes 446992
  130.1 7.3 %copy-start.15 = (f32[193,193]{1,0:T(8,128)S(1)}, f32[193,193]{1,0:T(8,128)}, u32[]{:S(2)}) copy-start(f32[193,193]{1,0:T(8,128)} %param.26) | copy-start | bytes 446992
  130.1 67.6 %all-to-all-start.2 = ((f32[128,9,8,128]{3,2,1,0:T(8,128)}), f32[128,9,8,128]{3,2,1,0:T(8,128)}, u32[]{:S(2)}, u32[]{:S(2)}) async-start(f32[128,9,8,128]{3,2,1,0:T(8,128)} %get-tuple-element.23), calls=%async_computation.2 | async-start | bytes 9437184 | tf_op jit(solution)/shard_map/all_to_all | solution.py:485
  (9 other events, 11.4 us)

commit v5 on v4

--- a/solution.py
+++ b/solution.py
@@ -49,46 +49,58 @@
     return jnp.asarray(np.asarray(values, np.float32))
 
 
-def free_kernel(scales, f_ref, w_ref, v_ref, g_ref, lo_ref, hi_ref, d_ref, e_ref, o_ref):
+def free_kernel(
+    scales, f_ref, p_ref, w_ref, v_ref, g_ref, lo_ref, hi_ref, d_ref, e_ref, o_ref, s_ref
+):
     scale_x, scale_z, scale_c, scale_w = scales
-    i = pl.program_id(0)
     slab, _, size_y, size_x = f_ref.shape
+    block = p_ref.shape[2]
+    here = pl.ds(pl.multiple_of(pl.program_id(0) * block, 8), block)
+
+    @pl.when(pl.program_id(0) == 0)
+    def _():
+        for i in range(3):
+            for z in range(0, slab, 2):
+                pair = jnp.concatenate([f_ref[z, i], f_ref[z + 1, i]], axis=1)
+                high = pair.astype(jnp.bfloat16)
+                low = (pair - high.astype(jnp.float32)).astype(jnp.bfloat16)
+                slope = jnp.dot(d_ref[...], high, preferred_element_type=jnp.float32)
+                slope += jnp.dot(d_ref[...], low, preferred_element_type=jnp.float32)
+                slope += jnp.dot(e_ref[...], high, preferred_element_type=jnp.float32)
+                s_ref[z, i, :size_y, :] = slope[:, :size_x]
+                s_ref[z + 1, i, :size_y, :] = slope[:, size_x:]
+
     noise, speed, tensor = [
-        r.reshape(r.shape[0], size_y * slab, size_x) for r in (w_ref, v_ref, g_ref)
+        r.reshape(r.shape[0], block * slab, size_x) for r in (w_ref, v_ref, g_ref)
     ]
-    slopes = []
     for z in range(slab):
-        plane = pl.ds(z, size_y, stride=slab)
-        own = f_ref[z, i]
-        if z % 2 == 0:
-            pair = jnp.concatenate([own, f_ref[z + 1, i]], axis=1)
-            high = pair.astype(jnp.bfloat16)
-            low = (pair - high.astype(jnp.float32)).astype(jnp.bfloat16)
-            slope = jnp.dot(d_ref[...], high, preferred_element_type=jnp.float32)
-            slope += jnp.dot(d_ref[...], low, preferred_element_type=jnp.float32)
-            slope += jnp.dot(e_ref[...], high, preferred_element_type=jnp.float32)
-            slopes = [slope[:, :size_x], slope[:, size_x:]]
-        slope_y = slopes[z % 2]
-        upper = hi_ref[i] if z == slab - 1 else f_ref[z + 1, i]
-        lower = lo_ref[i] if z == 0 else f_ref[z - 1, i]
-        slope_x = pltpu.roll(own, size_x - 1, 1) - pltpu.roll(own, 1, 1)
-        advect = (
-            speed[0, plane, :] * (scale_x * slope_x)
-            + speed[1, plane, :] * slope_y
-            + speed[2, plane, :] * (scale_z * (upper - lower))
-        )
-        stretch = (
-            tensor[0, plane, :] * f_ref[z, 0]
-            + tensor[1, plane, :] * f_ref[z, 1]
-            + tensor[2, plane, :] * f_ref[z, 2]
-        )
-        result = own + TIME_STEP * (stretch - advect)
-        result = result + scale_c * (upper - 2.0 * own + lower)
-        o_ref[z, 0] = result + scale_w * noise[0, plane, :]
+        plane = pl.ds(z, block, stride=slab)
+        speed_x, speed_y, speed_z = [speed[c, plane, :] for c in range(3)]
+        parts = [p_ref[z, c] for c in range(3)]
+        for i in range(3):
+            own = parts[i]
+            upper = hi_ref[i] if z == slab - 1 else p_ref[z + 1, i]
+            lower = lo_ref[i] if z == 0 else p_ref[z - 1, i]
+            slope_x = pltpu.roll(own, size_x - 1, 1) - pltpu.roll(own, 1, 1)
+            advect = (
+                speed_x * (scale_x * slope_x)
+                + speed_y * s_ref[z, i, here, :]
+                + speed_z * (scale_z * (upper - lower))
+            )
+            stretch = (
+                tensor[3 * i, plane, :] * parts[0]
+                + tensor[3 * i + 1, plane, :] * parts[1]
+                + tensor[3 * i + 2, plane, :] * parts[2]
+            )
+            result = own + TIME_STEP * (stretch - advect)
+            result = result + scale_c * (upper - 2.0 * own + lower)
+            o_ref[z, i] = result + scale_w * noise[i, plane, :]
 
 
 def spring_free(planes, wiener, velocity, gradient, below, above, wall_derivative, step_x, step_z):
     slab, _, size_y, size_x = planes.shape
+    block = 40
+    steps = -(-size_y // block)
     whole = pl.BlockSpec(memory_space=pltpu.VMEM)
     high = lax.reduce_precision(wall_derivative, 8, 7)
     low = (wall_derivative - high).astype(jnp.bfloat16)
@@ -99,24 +111,22 @@
         DIFFUSIVITY * TIME_STEP / (step_z * step_z),
         math.sqrt(TIME_STEP / WEISSENBERG),
     )
+
+    def rows(count):
+        return pl.BlockSpec((count, block, slab, size_x), lambda j: (0, j, 0, 0))
+
+    across = pl.BlockSpec((slab, 3, block, size_x), lambda j: (0, 0, j, 0))
+    edge = pl.BlockSpec((3, block, size_x), lambda j: (0, j, 0))
     return pl.pallas_call(
         functools.partial(free_kernel, scales),
-        grid=(3,),
-        in_specs=[
-            whole,
-            pl.BlockSpec((1, size_y, slab, size_x), lambda i: (i, 0, 0, 0)),
-            whole,
-            pl.BlockSpec((3, size_y, slab, size_x), lambda i: (i, 0, 0, 0)),
-            whole,
-            whole,
-            whole,
-            whole,
-        ],
-        out_specs=pl.BlockSpec((slab, 1, size_y, size_x), lambda i: (0, i, 0, 0)),
+        grid=(steps,),
+        in_specs=[whole, across, rows(3), rows(3), rows(9), edge, edge, whole, whole],
+        out_specs=across,
         out_shape=pltpu.HBM(planes.shape, jnp.float32),
+        scratch_shapes=[pltpu.VMEM((slab, 3, steps * block, size_x), jnp.float32)],
         compiler_params=pltpu.CompilerParams(vmem_limit_bytes=60 * 1024 * 1024),
         cost_estimate=pl.CostEstimate(flops=3 * 10**9, bytes_accessed=18 * 10**6, transcendentals=0),
-    )(planes, wiener, velocity, gradient, below, above, high, low)
+    )(planes, planes, wiener, velocity, gradient, below, above, high, low)
 
 
 def padded(values, rows, columns):
@@ -246,20 +256,22 @@
     def loaded(c):
         return jnp.concatenate([taken(c), taken(8 + c)], axis=1)
 
+    samples = o_ref.shape[0] // spans
+    copies = []
     for i in range(3):
         solved = full_dot(f_ref[...], loaded(i)) + full_dot(g_ref[...], loaded(3 + i))
         both = full_dot(b_ref[...], solved / d_ref[...])
         value, slope = both[:128], both[128:]
-        t_ref[:, i] = value[:, :128].reshape(spans, 8, 128)
-        t_ref[:, 3 + i] = slope[:, :128].reshape(spans, 8, 128)
+        t_ref[i, :, 0] = value[:, :128].reshape(spans, 8, 128)
+        t_ref[i, :, 1] = slope[:, :128].reshape(spans, 8, 128)
         mixed = jnp.where(lane < 64, value[:, 128:], pltpu.roll(slope[:, 128:], 64, 1))
-        t_ref[:, 6 + i] = mixed.reshape(spans, 8, 128)
-    copies = [
-        pltpu.make_async_copy(t_ref, o_ref.at[pl.ds(k * spans, spans)], sem.at[k])
-        for k in range(o_ref.shape[0] // spans)
-    ]
-    for copy in copies:
-        copy.start()
+        t_ref[i, :, 2] = mixed.reshape(spans, 8, 128)
+        for k in range(samples):
+            copy = pltpu.make_async_copy(
+                t_ref.at[i], o_ref.at[pl.ds(k * spans, spans), i], sem.at[i, k]
+            )
+            copy.start()
+            copies.append(copy)
 
     def last(c):
         if c < 2:
@@ -283,22 +295,23 @@
         in_specs=[whole] * 7,
         out_specs=(pl.BlockSpec(memory_space=pltpu.HBM), whole),
         out_shape=(
-            pltpu.HBM((samples * spans, 9, 8, 128), jnp.float32),
+            pltpu.HBM((samples * spans, 3, 3, 8, 128), jnp.float32),
             jax.ShapeDtypeStruct((6, 8, 128), jnp.float32),
         ),
         scratch_shapes=[
-            pltpu.VMEM((spans, 9, 8, 128), jnp.float32),
-            pltpu.SemaphoreType.DMA((samples,)),
+            pltpu.VMEM((3, spans, 3, 8, 128), jnp.float32),
+            pltpu.SemaphoreType.DMA((3, samples)),
         ],
         compiler_params=pltpu.CompilerParams(vmem_limit_bytes=32 * 1024 * 1024),
     )(spectra, damping, last_damping, forward, forward_slope, inverse, slab_inverse)
 
 
-def slab_kernel(u_ref, w_ref, h_ref, l_ref, t_ref, c_ref, x_ref, v_ref, g_ref):
+def slab_kernel(r_ref, l_ref, t_ref, c_ref, x_ref, v_ref, g_ref):
     i = pl.program_id(0)
-    rows = u_ref.shape[0]
+    rows = r_ref.shape[0]
     _, size_y, slab, size_x = v_ref.shape
-    flat = [r.reshape(rows * slab, 128) for r in (u_ref, w_ref, h_ref)]
+    flat = r_ref.reshape(rows * 3 * slab, 128)
+    column = jnp.broadcast_to(c_ref[...], (c_ref.shape[0], 128))
     out_v = v_ref.reshape(size_y * slab, size_x)
     out_g = g_ref.reshape(3, size_y * slab, size_x)
     lane = lax.broadcasted_iota(jnp.int32, (rows, 128), 1)
@@ -306,7 +319,9 @@
     for first in range(0, slab, 2):
         values, slopes = [], []
         for z in (first, first + 1):
-            value, slope, high = [r[pl.ds(z, rows, stride=slab), :] for r in flat]
+            value, slope, high = [
+                flat[pl.ds(slab * part + z, rows, stride=3 * slab), :] for part in range(3)
+            ]
             value_high = jnp.where(lane < 64, high, 0.0)
             slope_high = jnp.where(lane < 64, pltpu.roll(high, 64, 1), 0.0)
             values.append(jnp.concatenate([value, value_high], axis=1))
@@ -327,8 +342,8 @@
         for k, z in enumerate((first, first + 1)):
             place = pl.ds(z, size_y, stride=slab)
             lanes = slice(k * rows, k * rows + rows)
-            value_z = value[:, lanes] + c_ref[...] * l_ref[i, pl.ds(z, 1), :]
-            slope_z = slope[:, lanes] + c_ref[:half] * l_ref[3 + i, pl.ds(z, 1), :]
+            value_z = value[:, lanes] + column * l_ref[i, pl.ds(z, 1), :]
+            slope_z = slope[:, lanes] + column[:half] * l_ref[3 + i, pl.ds(z, 1), :]
             both = jnp.dot(
                 three_of(value_z[:half], 1), x_ref[...], preferred_element_type=jnp.float32
             )
@@ -345,19 +360,14 @@
 
 def slab_values(rows, last, wall_table, last_column, table_x, size_y):
     count = rows.shape[0]
-    slab, size_x = rows.shape[2], table_x.shape[1] // 2
+    slab, size_x = rows.shape[3], table_x.shape[1] // 2
     whole = pl.BlockSpec(memory_space=pltpu.VMEM)
-
-    def piece(place):
-        return pl.BlockSpec((count, 1, slab, 128), lambda i: (0, place(i), 0, 0))
 
     return pl.pallas_call(
         slab_kernel,
         grid=(3,),
         in_specs=[
-            piece(lambda i: i),
-            piece(lambda i: i + 3),
-            piece(lambda i: i + 6),
+            pl.BlockSpec((count, 1, 3, slab, 128), lambda i: (0, i, 0, 0, 0)),
             whole,
             whole,
             whole,
@@ -372,7 +382,7 @@
             jax.ShapeDtypeStruct((9, size_y, slab, size_x), jnp.float32),
         ),
         compiler_params=pltpu.CompilerParams(vmem_limit_bytes=60 * 1024 * 1024),
-    )(rows, rows, rows, last, wall_table, last_column, table_x)
+    )(rows, last, wall_table, last_column, table_x)
 
 
 def summed(planes, beside):
@@ -492,7 +502,7 @@
         rows,
         last,
         split_three(wall_table.at[:, size_y - 1].set(0.0), 1),
-        jnp.broadcast_to(wall_table[:, size_y - 1 : size_y], (wall_table.shape[0], 128)),
+        wall_table[:, size_y - 1 : size_y],
         stacked_three(np.concatenate([rows_x, (rows_x.T @ slope_rows_x).T], axis=1)),
         size_y,
     )

time: 212 us -> 204 us (0.962)
  starting transfers between devices: 39.7 us -> 35.2 us
    all_to_all x1, starting transfers between devices: 13.5 us -> 8.7 us  [on_device(): spectra = lax.all_to_all(message, BOTH, 0, 0, tiled=True)]
    unnamed x51 -> x53, local copies, waits for them, and re-layouts: 8.44 us -> 7.62 us
  transfers between devices with their start and end apart: 12 -> 12, of which waited for: 8 -> 7; matrix products, arithmetic and copies ran while one was open for 7% -> 8% of each run, Pallas kernels for 5% -> 6%
where the time goes in v5:
time: 204 us
  waiting for transfers between devices  110 us (54%)
  starting transfers between devices  35.2 us (17%)
  Pallas kernels  32.4 us (16%)
  local copies, waits for them, and re-layouts  13.2 us (6%)
  other arithmetic  10.2 us (5%)
  matrix products  2.06 us (1%)
    all_to_all x1, waiting for transfers between devices, on_device(): rows = lax.all_to_all(back, BOTH, 0, 0, tiled=True)  54.5 us
    all_to_all x1, waiting for transfers between devices, on_device(): moved = lax.all_to_all(new_fields, 'sample', 0, 0, tiled=True)  27.2 us
    all_to_all x1, waiting for transfers between devices, on_device(): spectra = lax.all_to_all(message, BOTH, 0, 0, tiled=True)  14.3 us
    ppermute x6, waiting for transfers between devices, shifted(): return lax.ppermute(values, 'sample', pairs)  13.5 us
    pallas_call x1, Pallas kernels, slab_values(): pl.pallas_call(slab_kernel, grid=(3,), in_specs=[pl.BlockSpec((count, 1,...  12.5 us
    pallas_call x1, Pallas kernels, spring_free(): pl.pallas_call(functools.partial(free_kernel, scales), grid=(steps,), in_...  11.2 us
    ppermute x6, starting transfers between devices, shifted(): return lax.ppermute(values, 'sample', pairs)  9.2 us
    all_to_all x1, starting transfers between devices, on_device(): spectra = lax.all_to_all(message, BOTH, 0, 0, tiled=True)  8.7 us
  transfers between devices with their start and end apart: 12, of which 7 were waited for; matrix products, arithmetic and copies ran while one was open for 8% of the time, Pallas kernels for 6%

profile of v5, /device:TPU:5, one launch (start us, length us, event | category | flops | bytes accessed | tf_op | source)
XLA Modules:
  0.0 203.7 jit_solution(13162856034121607348)
XLA Ops:
  0.6 2.1 %multiply_reduce_fusion = f32[8,193,128]{2,1,0:T(8,128)S(1)} fusion(f32[3,1,128,8,193]{2,3,4,1,0:T(8,128)} %param.20), kind=kLoop, calls=%fused_computation.2 | loop fusion | flops 988160 | bytes 3162112 | tf_op jit(solution)/shard_map/reduce_sum | solution.py:447
  4.4 2.6 %collective-permute-start.1 = (f32[2,193,128]{2,1,0:T(8,128)S(1)}, f32[2,193,128]{2,1,0:T(8,128)S(1)}, u32[]{:S(2)}, u32[]{:S(2)}) collective-permute-start(f32[2,193,128]{2,1,0:T(8,128)S(1)} %get-tuple-element.33), channel_id=1, source_target_pairs={{0,32},{16,48},{32,0},{48,16},{64,96},{80,112},{96,64},{112,80},{1... | collective-permute-start | bytes 592904 | tf_op jit(solution)/shard_map/ppermute | solution.py:397
  8.6 1.6 collective-permute-start.5
  10.2 1.6 collective-permute-start.4
  12.5 3.4 %collective-permute-done.1 = f32[2,193,128]{2,1,0:T(8,128)S(1)} collective-permute-done((f32[2,193,128]{2,1,0:T(8,128)S(1)}, f32[2,193,128]{2,1,0:T(8,128)S(1)}, u32[]{:S(2)}, u32[]{:S(2)}) %collective-permute-start.1) | collective-permute-done | bytes 197664 | tf_op jit(solution)/shard_map/ppermute | solution.py:397
  15.9 3.7 %collective-permute-start.3 = (f32[2,193,128]{2,1,0:T(8,128)S(1)}, f32[2,193,128]{2,1,0:T(8,128)S(1)}, u32[]{:S(2)}, u32[]{:S(2)}) collective-permute-start(f32[2,193,128]{2,1,0:T(8,128)S(1)} %fusion.7), channel_id=1, source_target_pairs={{0,64},{16,80},{32,96},{48,112},{64,0},{80,16},{96,32},{112,48},{1... | collective-permute-start | bytes 592904 | tf_op jit(solution)/shard_map/ppermute | solution.py:406
  20.4 11.2 %shard_map.193 = f32[8,3,193,128]{3,2,1,0:T(8,128)} custom-call(f32[8,3,193,128]{3,2,1,0:T(8,128)} %bitcast.75, f32[8,3,193,128]{3,2,1,0:T(8,128)} %bitcast.76, f32[3,193,8,128]{3,2,1,0:T(8,128)} %bitcast.82, f32[3,193,8,128]{3,2,1,0:T(8,128)} %bitcast.81, f32[9,193,8,128]{3,2,1,0:T(8,128)} %bitcast.78, f32[3,193,128]{2,1,0:T(8,128)} %copy-done.18, ...), custom_call_target="tpu_custom_call" | custom-call | flops 3000000000 | bytes 18000000 | tf_op jit(solution)/shard_map/pallas_call | solution.py:120
  31.7 2.9 %collective-permute-start.6 = (f32[2,193,128]{2,1,0:T(8,128)S(1)}, f32[2,193,128]{2,1,0:T(8,128)S(1)}, u32[]{:S(2)}, u32[]{:S(2)}) collective-permute-start(f32[2,193,128]{2,1,0:T(8,128)S(1)} %add.112), channel_id=1, source_target_pairs={{0,48},{16,0},{32,16},{48,32},{64,112},{80,64},{96,80},{112,96},{1... | collective-permute-start | bytes 592904 | tf_op jit(solution)/shard_map/ppermute | solution.py:397
  35.9 2.2 %collective-permute-done.6 = f32[2,193,128]{2,1,0:T(8,128)S(1)} collective-permute-done((f32[2,193,128]{2,1,0:T(8,128)S(1)}, f32[2,193,128]{2,1,0:T(8,128)S(1)}, u32[]{:S(2)}, u32[]{:S(2)}) %collective-permute-start.6) | collective-permute-done | bytes 197664 | tf_op jit(solution)/shard_map/ppermute | solution.py:397
  38.1 5.2 %collective-permute-done.7 = f32[2,193,128]{2,1,0:T(8,128)S(1)} collective-permute-done((f32[2,193,128]{2,1,0:T(8,128)S(1)}, f32[2,193,128]{2,1,0:T(8,128)S(1)}, u32[]{:S(2)}, u32[]{:S(2)}) %collective-permute-start.7) | collective-permute-done | bytes 197664 | tf_op jit(solution)/shard_map/ppermute | solution.py:397
  43.3 2.7 %collective-permute-done.8 = f32[2,193,128]{2,1,0:T(8,128)S(1)} collective-permute-done((f32[2,193,128]{2,1,0:T(8,128)S(1)}, f32[2,193,128]{2,1,0:T(8,128)S(1)}, u32[]{:S(2)}, u32[]{:S(2)}) %collective-permute-start.8) | collective-permute-done | bytes 197664 | tf_op jit(solution)/shard_map/ppermute | solution.py:397
  48.8 2.0 %multiply_subtract_fusion = f32[8,3,193,128]{3,2,1,0:T(8,128)} fusion(f32[8,3,193,128]{3,2,1,0:T(8,128)S(1)} %copy-done.10, f32[8,193,128]{2,1,0:T(8,128)S(1)} %broadcast_multiply_fusion, f32[3,1,128,8,193]{2,3,4,1,0:T(8,128)S(1)} %copy-done.9), kind=kLoop, calls=%fused_computation.1 | loop fusion | flops 1185792 | bytes 7905280 | tf_op jit(solution)/shard_map/sub | solution.py:449
  50.8 3.8 %all-to-all-start = ((f32[8,3,193,128]{3,2,1,0:T(8,128)}), f32[8,3,193,128]{3,2,1,0:T(8,128)S(1)}, u32[]{:S(2)}, u32[]{:S(2)}) async-start(f32[8,3,193,128]{3,2,1,0:T(8,128)} %multiply_subtract_fusion), calls=%async_computation | async-start | bytes 4915200 | tf_op jit(solution)/shard_map/all_to_all | solution.py:450
  54.6 1.9 constant_dynamic-slice_fusion
  59.7 27.2 %all-to-all-done.n_ref = f32[8,3,193,128]{3,2,1,0:T(8,128)S(1)} async-done(((f32[8,3,193,128]{3,2,1,0:T(8,128)}), f32[8,3,193,128]{3,2,1,0:T(8,128)S(1)}, u32[]{:S(2)}, u32[]{:S(2)}) %all-to-all-start) | async-done | bytes 2371616 | tf_op jit(solution)/shard_map/all_to_all | solution.py:450
  87.9 5.0 %shard_map.194 = f32[2048,128]{1,0:T(8,128)} custom-call(f32[8,3,193,128]{3,2,1,0:T(8,128)S(1)} %all-to-all-done.n_ref, f32[193,128]{1,0:T(8,128)S(1)} %dynamic-slice_bitcast_fusion.s_ref, f32[3,256,128]{2,1,0:T(8,128)S(1)} %copy-done, bf16[512,768]{1,0:T(8,128)(2,1)S(1)} %pad_maximum_fusion.m_ref, f32[128,256]{1,0:T(8,128)S(1)} %copy-done.2), custom_call_target="tpu_custom_call" | custom-call | tf_op jit(solution)/shard_map/pallas_call | solution.py:231
  93.0 8.7 %all-to-all-start.1 = ((f32[128,2,8,128]{3,2,1,0:T(8,128)}), f32[128,2,8,128]{3,2,1,0:T(8,128)S(1)}, u32[]{:S(2)}, u32[]{:S(2)}) async-start(f32[128,2,8,128]{3,2,1,0:T(8,128)} %bitcast.26), calls=%async_computation.1 | async-start | bytes 2097152 | tf_op jit(solution)/shard_map/all_to_all | solution.py:469
  105.1 14.3 %all-to-all-done.1.in_ref = f32[128,2,8,128]{3,2,1,0:T(8,128)S(1)} async-done(((f32[128,2,8,128]{3,2,1,0:T(8,128)}), f32[128,2,8,128]{3,2,1,0:T(8,128)S(1)}, u32[]{:S(2)}, u32[]{:S(2)}) %all-to-all-start.1) | async-done | bytes 1048608 | tf_op jit(solution)/shard_map/all_to_all | solution.py:469
  119.4 3.6 %shard_map.195 = (f32[128,3,3,8,128]{4,3,2,1,0:T(8,128)}, f32[6,8,128]{2,1,0:T(8,128)S(1)}) custom-call(f32[128,2,8,128]{3,2,1,0:T(8,128)S(1)} %all-to-all-done.1.in_ref, f32[128,256]{1,0:T(8,128)S(1)} %multiply_add_fusion.d_ref, f32[128,128]{1,0:T(8,128)S(1)} %multiply_add_fusion.1.e_ref, f32[128,128]{1,0:T(8,128)S(1)} %copy-done.4, ...), custom_call_target="tpu_custom_call" | custom-call | tf_op jit(solution)/shard_map/pallas_call | solution.py:293
  123.6 6.7 %all-to-all-start.2 = ((f32[128,3,3,8,128]{4,3,2,1,0:T(8,128)}), f32[128,3,3,8,128]{4,3,2,1,0:T(8,128)}, u32[]{:S(2)}, u32[]{:S(2)}) async-start(f32[128,3,3,8,128]{4,3,2,1,0:T(8,128)} %get-tuple-element.23), calls=%async_computation.2 | async-start | bytes 9437184 | tf_op jit(solution)/shard_map/all_to_all | solution.py:495
  131.4 1.6 fusion.10
  134.8 1.8 copy.26
  136.7 54.5 %all-to-all-done.2.r_ref = f32[128,3,3,8,128]{4,3,2,1,0:T(8,128)} async-done(((f32[128,3,3,8,128]{4,3,2,1,0:T(8,128)}), f32[128,3,3,8,128]{4,3,2,1,0:T(8,128)}, u32[]{:S(2)}, u32[]{:S(2)}) %all-to-all-start.2) | async-done | bytes 4718624 | tf_op jit(solution)/shard_map/all_to_all | solution.py:495
  191.2 12.5 %shard_map.196 = (f32[3,193,8,128]{3,2,1,0:T(8,128)}, f32[9,193,8,128]{3,2,1,0:T(8,128)}) custom-call(f32[128,3,3,8,128]{4,3,2,1,0:T(8,128)} %all-to-all-done.2.r_ref, f32[6,8,128]{2,1,0:T(8,128)} %copy-done.5, bf16[416,768]{1,0:T(8,128)(2,1)} %pad_maximum_fusion.1.t_ref, f32[416,1]{1,0:T(8,128)} %get-tuple-element.37.c_ref, ...), custom_call_target="tpu_custom_call" | custom-call | tf_op jit(solution)/shard_map/pallas_call | solution.py:366
  (89 shorter events, 19.8 us)
Async XLA Ops:
  2.8 5.3 %copy-start.8 = (f32[3,1,128,8,193]{2,3,4,1,0:T(8,128)S(1)}, f32[3,1,128,8,193]{2,3,4,1,0:T(8,128)}, u32[]{:S(2)}) copy-start(f32[3,1,128,8,193]{2,3,4,1,0:T(8,128)} %param.20) | copy-start | bytes 7114756
  3.0 9.5 %collective-permute-start = (f32[2,193,128]{2,1,0:T(8,128)S(1)}, f32[2,193,128]{2,1,0:T(8,128)S(1)}, u32[]{:S(2)}, u32[]{:S(2)}) collective-permute-start(f32[2,193,128]{2,1,0:T(8,128)S(1)} %get-tuple-element.32), channel_id=1, source_target_pairs={{0,16},{16,32},{32,48},{48,0},{64,80},{80,96},{96,112},{112,64},{1... | collective-permute-start | bytes 592904 | tf_op jit(solution)/shard_map/ppermute | solution.py:397
  4.4 11.5 %collective-permute-start.1 = (f32[2,193,128]{2,1,0:T(8,128)S(1)}, f32[2,193,128]{2,1,0:T(8,128)S(1)}, u32[]{:S(2)}, u32[]{:S(2)}) collective-permute-start(f32[2,193,128]{2,1,0:T(8,128)S(1)} %get-tuple-element.33), channel_id=1, source_target_pairs={{0,32},{16,48},{32,0},{48,16},{64,96},{80,112},{96,64},{112,80},{1... | collective-permute-start | bytes 592904 | tf_op jit(solution)/shard_map/ppermute | solution.py:397
  7.0 4.8 %copy-start.14 = (f32[193,193]{1,0:T(8,128)S(1)}, f32[193,193]{1,0:T(8,128)}, u32[]{:S(2)}) copy-start(f32[193,193]{1,0:T(8,128)} %param.24) | copy-start | bytes 446992
  7.0 8.9 %collective-permute-start.2 = (f32[2,193,128]{2,1,0:T(8,128)S(1)}, f32[2,193,128]{2,1,0:T(8,128)S(1)}, u32[]{:S(2)}, u32[]{:S(2)}) collective-permute-start(f32[2,193,128]{2,1,0:T(8,128)S(1)} %get-tuple-element.34), channel_id=1, source_target_pairs={{0,48},{16,0},{32,16},{48,32},{64,112},{80,64},{96,80},{112,96},{1... | collective-permute-start | bytes 592904 | tf_op jit(solution)/shard_map/ppermute | solution.py:397
  8.5 11.1 %copy-start.6 = (f32[3,1,128,8,193]{2,4,0,3,1:T(8,128)}, f32[3,1,128,8,193]{2,4,0,3,1:T(8,128)S(1)}, u32[]{:S(2)}) copy-start(f32[3,1,128,8,193]{2,4,0,3,1:T(8,128)S(1)} %copy.39) | copy-start | bytes 7114756
  8.6 11.0 %collective-permute-start.5 = (f32[3,193,128]{2,1,0:T(8,128)S(1)}, f32[3,193,128]{2,1,0:T(8,128)S(1)}, u32[]{:S(2)}, u32[]{:S(2)}) collective-permute-start(f32[3,193,128]{2,1,0:T(8,128)S(1)} %get-tuple-element.30), channel_id=1, source_target_pairs={{1,0},{2,1},{3,2},{4,3},{5,4},{6,5},{7,6},{8,7},{9,8},{10,9},{11,1... | collective-permute-start | bytes 889352 | tf_op jit(solution)/shard_map/ppermute | solution.py:434
  10.2 9.4 %collective-permute-start.4 = (f32[3,193,128]{2,1,0:T(8,128)S(1)}, f32[3,193,128]{2,1,0:T(8,128)S(1)}, u32[]{:S(2)}, u32[]{:S(2)}) collective-permute-start(f32[3,193,128]{2,1,0:T(8,128)S(1)} %get-tuple-element.31), channel_id=1, source_target_pairs={{0,1},{1,2},{2,3},{3,4},{4,5},{5,6},{6,7},{7,8},{8,9},{9,10},{10,1... | collective-permute-start | bytes 889352 | tf_op jit(solution)/shard_map/ppermute | solution.py:433
  15.9 15.7 %collective-permute-start.3 = (f32[2,193,128]{2,1,0:T(8,128)S(1)}, f32[2,193,128]{2,1,0:T(8,128)S(1)}, u32[]{:S(2)}, u32[]{:S(2)}) collective-permute-start(f32[2,193,128]{2,1,0:T(8,128)S(1)} %fusion.7), channel_id=1, source_target_pairs={{0,64},{16,80},{32,96},{48,112},{64,0},{80,16},{96,32},{112,48},{1... | collective-permute-start | bytes 592904 | tf_op jit(solution)/shard_map/ppermute | solution.py:406
  31.7 6.3 %collective-permute-start.6 = (f32[2,193,128]{2,1,0:T(8,128)S(1)}, f32[2,193,128]{2,1,0:T(8,128)S(1)}, u32[]{:S(2)}, u32[]{:S(2)}) collective-permute-start(f32[2,193,128]{2,1,0:T(8,128)S(1)} %add.112), channel_id=1, source_target_pairs={{0,48},{16,0},{32,16},{48,32},{64,112},{80,64},{96,80},{112,96},{1... | collective-permute-start | bytes 592904 | tf_op jit(solution)/shard_map/ppermute | solution.py:397
  34.6 11.5 %collective-permute-start.8 = (f32[2,193,128]{2,1,0:T(8,128)S(1)}, f32[2,193,128]{2,1,0:T(8,128)S(1)}, u32[]{:S(2)}, u32[]{:S(2)}) collective-permute-start(f32[2,193,128]{2,1,0:T(8,128)S(1)} %add.112), channel_id=1, source_target_pairs={{0,16},{16,32},{32,48},{48,0},{64,80},{80,96},{96,112},{112,64},{1... | collective-permute-start | bytes 592904 | tf_op jit(solution)/shard_map/ppermute | solution.py:397
  34.6 8.7 %collective-permute-start.7 = (f32[2,193,128]{2,1,0:T(8,128)S(1)}, f32[2,193,128]{2,1,0:T(8,128)S(1)}, u32[]{:S(2)}, u32[]{:S(2)}) collective-permute-start(f32[2,193,128]{2,1,0:T(8,128)S(1)} %add.112), channel_id=1, source_target_pairs={{0,32},{16,48},{32,0},{48,16},{64,96},{80,112},{96,64},{112,80},{1... | collective-permute-start | bytes 592904 | tf_op jit(solution)/shard_map/ppermute | solution.py:397
  50.8 36.1 %all-to-all-start = ((f32[8,3,193,128]{3,2,1,0:T(8,128)}), f32[8,3,193,128]{3,2,1,0:T(8,128)S(1)}, u32[]{:S(2)}, u32[]{:S(2)}) async-start(f32[8,3,193,128]{3,2,1,0:T(8,128)} %multiply_subtract_fusion), calls=%async_computation | async-start | bytes 4915200 | tf_op jit(solution)/shard_map/all_to_all | solution.py:450
  56.9 30.0 %copy-start.2 = (f32[128,256]{1,0:T(8,128)S(1)}, f32[128,256]{1,0:T(8,128)}, u32[]{:S(2)}) copy-start(f32[128,256]{1,0:T(8,128)} %constant.117.clone.x_ref) | copy-start | bytes 393220
  93.0 8.8 %copy-start.19 = (f32[193]{0:T(256)S(1)}, f32[193]{0:T(256)}, u32[]{:S(2)}) copy-start(f32[193]{0:T(256)} %param.27) | copy-start | bytes 2320
  93.0 9.3 %copy-start.20 = (f32[128]{0:T(128)S(1)}, f32[128]{0:T(128)}, u32[]{:S(2)}) copy-start(f32[128]{0:T(128)} %constant.118.clone) | copy-start | bytes 1540
  93.0 10.6 %copy-start.21 = (f32[128]{0:T(128)S(1)}, f32[128]{0:T(128)}, u32[]{:S(2)}) copy-start(f32[128]{0:T(128)} %constant.119.clone) | copy-start | bytes 1540
  93.0 26.4 %copy-start.1 = (f32[256,128]{1,0:T(8,128)S(1)}, f32[256,128]{1,0:T(8,128)}, u32[]{:S(2)}) copy-start(f32[256,128]{1,0:T(8,128)} %constant.123.clone.b_ref) | copy-start | bytes 393220
  93.0 26.4 %copy-start.3 = (f32[128,128]{1,0:T(8,128)S(1)}, f32[128,128]{1,0:T(8,128)}, u32[]{:S(2)}) copy-start(f32[128,128]{1,0:T(8,128)} %constant.122.clone.g_ref) | copy-start | bytes 196612
  93.0 26.4 %copy-start.4 = (f32[128,128]{1,0:T(8,128)S(1)}, f32[128,128]{1,0:T(8,128)}, u32[]{:S(2)}) copy-start(f32[128,128]{1,0:T(8,128)} %constant.121.clone.f_ref) | copy-start | bytes 196612
  93.0 26.4 %all-to-all-start.1 = ((f32[128,2,8,128]{3,2,1,0:T(8,128)}), f32[128,2,8,128]{3,2,1,0:T(8,128)S(1)}, u32[]{:S(2)}, u32[]{:S(2)}) async-start(f32[128,2,8,128]{3,2,1,0:T(8,128)} %bitcast.26), calls=%async_computation.1 | async-start | bytes 2097152 | tf_op jit(solution)/shard_map/all_to_all | solution.py:469
  123.6 7.3 %copy-start.15 = (f32[193,193]{1,0:T(8,128)S(1)}, f32[193,193]{1,0:T(8,128)}, u32[]{:S(2)}) copy-start(f32[193,193]{1,0:T(8,128)} %param.24) | copy-start | bytes 446992
  123.6 7.3 %copy-start.16 = (f32[193,193]{1,0:T(8,128)S(1)}, f32[193,193]{1,0:T(8,128)}, u32[]{:S(2)}) copy-start(f32[193,193]{1,0:T(8,128)} %param.26) | copy-start | bytes 446992
  123.6 67.6 %all-to-all-start.2 = ((f32[128,3,3,8,128]{4,3,2,1,0:T(8,128)}), f32[128,3,3,8,128]{4,3,2,1,0:T(8,128)}, u32[]{:S(2)}, u32[]{:S(2)}) async-start(f32[128,3,3,8,128]{4,3,2,1,0:T(8,128)} %get-tuple-element.23), calls=%async_computation.2 | async-start | bytes 9437184 | tf_op jit(solution)/shard_map/all_to_all | solution.py:495
  (10 other events, 16.8 us)

commit v6 on v5

--- a/solution.py
+++ b/solution.py
@@ -49,27 +49,39 @@
     return jnp.asarray(np.asarray(values, np.float32))
 
 
-def free_kernel(
-    scales, f_ref, p_ref, w_ref, v_ref, g_ref, lo_ref, hi_ref, d_ref, e_ref, o_ref, s_ref
-):
+def slope_kernel(f_ref, d_ref, e_ref, o_ref):
+    size_x = f_ref.shape[3]
+    for i in range(3):
+        pair = jnp.concatenate([f_ref[0, i], f_ref[1, i]], axis=1)
+        high = pair.astype(jnp.bfloat16)
+        low = (pair - high.astype(jnp.float32)).astype(jnp.bfloat16)
+        slope = jnp.dot(d_ref[...], high, preferred_element_type=jnp.float32)
+        slope += jnp.dot(d_ref[...], low, preferred_element_type=jnp.float32)
+        slope += jnp.dot(e_ref[...], high, preferred_element_type=jnp.float32)
+        o_ref[0, i] = slope[:, :size_x]
+        o_ref[1, i] = slope[:, size_x:]
+
+
+def wall_slope(planes, wall_derivative):
+    slab, _, size_y, size_x = planes.shape
+    high = lax.reduce_precision(wall_derivative, 8, 7)
+    low = (wall_derivative - high).astype(jnp.bfloat16)
+    whole = pl.BlockSpec(memory_space=pltpu.VMEM)
+    pair = pl.BlockSpec((2, 3, size_y, size_x), lambda j: (j, 0, 0, 0))
+    return pl.pallas_call(
+        slope_kernel,
+        grid=(slab // 2,),
+        in_specs=[pair, whole, whole],
+        out_specs=pair,
+        out_shape=pltpu.HBM(planes.shape, jnp.float32),
+        compiler_params=pltpu.CompilerParams(vmem_limit_bytes=24 * 1024 * 1024),
+        cost_estimate=pl.CostEstimate(flops=10**9, bytes_accessed=6 * 10**6, transcendentals=0),
+    )(planes, high.astype(jnp.bfloat16), low)
+
+
+def free_kernel(scales, p_ref, s_ref, w_ref, v_ref, g_ref, lo_ref, hi_ref, o_ref):
     scale_x, scale_z, scale_c, scale_w = scales
-    slab, _, size_y, size_x = f_ref.shape
-    block = p_ref.shape[2]
-    here = pl.ds(pl.multiple_of(pl.program_id(0) * block, 8), block)
-
-    @pl.when(pl.program_id(0) == 0)
-    def _():
-        for i in range(3):
-            for z in range(0, slab, 2):
-                pair = jnp.concatenate([f_ref[z, i], f_ref[z + 1, i]], axis=1)
-                high = pair.astype(jnp.bfloat16)
-                low = (pair - high.astype(jnp.float32)).astype(jnp.bfloat16)
-                slope = jnp.dot(d_ref[...], high, preferred_element_type=jnp.float32)
-                slope += jnp.dot(d_ref[...], low, preferred_element_type=jnp.float32)
-                slope += jnp.dot(e_ref[...], high, preferred_element_type=jnp.float32)
-                s_ref[z, i, :size_y, :] = slope[:, :size_x]
-                s_ref[z + 1, i, :size_y, :] = slope[:, size_x:]
-
+    slab, _, block, size_x = p_ref.shape
     noise, speed, tensor = [
         r.reshape(r.shape[0], block * slab, size_x) for r in (w_ref, v_ref, g_ref)
     ]
@@ -84,7 +96,7 @@
             slope_x = pltpu.roll(own, size_x - 1, 1) - pltpu.roll(own, 1, 1)
             advect = (
                 speed_x * (scale_x * slope_x)
-                + speed_y * s_ref[z, i, here, :]
+                + speed_y * s_ref[z, i]
                 + speed_z * (scale_z * (upper - lower))
             )
             stretch = (
@@ -97,14 +109,9 @@
             o_ref[z, i] = result + scale_w * noise[i, plane, :]
 
 
-def spring_free(planes, wiener, velocity, gradient, below, above, wall_derivative, step_x, step_z):
+def spring_free(planes, slope, wiener, velocity, gradient, below, above, step_x, step_z):
     slab, _, size_y, size_x = planes.shape
     block = 40
-    steps = -(-size_y // block)
-    whole = pl.BlockSpec(memory_space=pltpu.VMEM)
-    high = lax.reduce_precision(wall_derivative, 8, 7)
-    low = (wall_derivative - high).astype(jnp.bfloat16)
-    high = high.astype(jnp.bfloat16)
     scales = (
         1.0 / (2.0 * step_x),
         1.0 / (2.0 * step_z),
@@ -119,14 +126,13 @@
     edge = pl.BlockSpec((3, block, size_x), lambda j: (0, j, 0))
     return pl.pallas_call(
         functools.partial(free_kernel, scales),
-        grid=(steps,),
-        in_specs=[whole, across, rows(3), rows(3), rows(9), edge, edge, whole, whole],
+        grid=(-(-size_y // block),),
+        in_specs=[across, across, rows(3), rows(3), rows(9), edge, edge],
         out_specs=across,
         out_shape=pltpu.HBM(planes.shape, jnp.float32),
-        scratch_shapes=[pltpu.VMEM((slab, 3, steps * block, size_x), jnp.float32)],
         compiler_params=pltpu.CompilerParams(vmem_limit_bytes=60 * 1024 * 1024),
-        cost_estimate=pl.CostEstimate(flops=3 * 10**9, bytes_accessed=18 * 10**6, transcendentals=0),
-    )(planes, planes, wiener, velocity, gradient, below, above, high, low)
+        cost_estimate=pl.CostEstimate(flops=10**8, bytes_accessed=19 * 10**6, transcendentals=0),
+    )(planes, slope, wiener, velocity, gradient, below, above)
 
 
 def padded(values, rows, columns):
@@ -385,7 +391,7 @@
     )(rows, last, wall_table, last_column, table_x)
 
 
-def summed(planes, beside):
+def summed(planes, early, rest):
     count = lax.axis_size("sample")
     ring = count // 2
     index = lax.axis_index("sample")
@@ -402,13 +408,54 @@
     total = ahead[0]
     for part in [shifted(ahead[k], k) for k in range(1, ring)]:
         total = total + part
+    total, early = lax.optimization_barrier((total, early))
     pairs = [(i, (i + ring) % count) for i in range(count)]
     total = total + lax.ppermute(total, "sample", pairs)
-    total, beside = lax.optimization_barrier((total, beside))
-    parts = [shifted(total, k) for k in range(ring - 1, 0, -1)] + [total]
-    start = (ring - 1 - place) % ring
-    gathered = lax.dynamic_slice_in_dim(jnp.stack(parts + parts), start, ring, axis=0)
-    return gathered.reshape(planes.shape), beside
+    total, beside = lax.optimization_barrier((total, rest(early)))
+    return place, [total] + [shifted(total, k) for k in range(1, ring)], beside
+
+
+def finish_kernel(relax, samples, at_ref, *refs):
+    *quarters, a_ref, f_ref, o_ref, s_ref = refs
+    for k, quarter in enumerate(quarters):
+
+        @pl.when(pl.program_id(0) == k)
+        def _(quarter=quarter):
+            for j in range(quarter.shape[0]):
+                spring = 1.0 / (1.0 - quarter[j] / samples / EXTENSIBILITY)
+                s_ref[j] = spring
+                scale = relax * spring
+                for c in range(3):
+                    o_ref[j, c] = a_ref[j, c] - scale * f_ref[j, c]
+
+
+def finished(place, quarters, free, planes, relax, samples):
+    slab, _, size_y, size_x = planes.shape
+    ring = len(quarters)
+    part = slab // ring
+    whole = pl.BlockSpec(memory_space=pltpu.VMEM)
+
+    def quarter(k, at):
+        return lax.rem(at[0] + ring - k, ring)
+
+    each = pl.BlockSpec((part, 3, size_y, size_x), lambda k, at: (quarter(k, at), 0, 0, 0))
+    return pl.pallas_call(
+        functools.partial(finish_kernel, relax, samples),
+        grid_spec=pltpu.PrefetchScalarGridSpec(
+            num_scalar_prefetch=1,
+            grid=(ring,),
+            in_specs=[whole] * ring + [each, each],
+            out_specs=(
+                each,
+                pl.BlockSpec((part, size_y, size_x), lambda k, at: (quarter(k, at), 0, 0)),
+            ),
+        ),
+        out_shape=(
+            pltpu.HBM(planes.shape, jnp.float32),
+            jax.ShapeDtypeStruct((slab, size_y, size_x), jnp.float32),
+        ),
+        compiler_params=pltpu.CompilerParams(vmem_limit_bytes=60 * 1024 * 1024),
+    )(jnp.reshape(place, (1,)).astype(jnp.int32), *quarters, free, planes)
 
 
 def on_device(
@@ -433,20 +480,23 @@
     below = lax.ppermute(field[-1], "span", ahead)
     above = lax.ppermute(field[0], "span", back)
     speed = jnp.transpose(velocity, (0, 3, 2, 1))
-    free = spring_free(
-        field,
-        jnp.transpose(wiener[:, 0], (0, 3, 2, 1)),
-        speed,
-        jnp.transpose(gradient, (0, 3, 2, 1)),
-        below,
-        above,
-        wall_derivative,
-        step_x,
-        step_z,
-    )
-    total_square, free = summed(jnp.sum(field * field, axis=1), free)
-    slab_spring = 1.0 / (1.0 - total_square / samples / EXTENSIBILITY)
-    new_fields = free - relax * slab_spring[:, None] * field
+
+    def rest(slope):
+        return spring_free(
+            field,
+            slope,
+            jnp.transpose(wiener[:, 0], (0, 3, 2, 1)),
+            speed,
+            jnp.transpose(gradient, (0, 3, 2, 1)),
+            below,
+            above,
+            step_x,
+            step_z,
+        )
+
+    slope = wall_slope(field, wall_derivative)
+    place, quarters, free = summed(jnp.sum(field * field, axis=1), slope, rest)
+    new_fields, slab_spring = finished(place, quarters, free, field, relax, samples)
     moved = lax.all_to_all(new_fields, "sample", 0, 0, tiled=True)
 
     own_velocity = lax.dynamic_index_in_dim(

time: 204 us -> 209 us (1.025)
  Pallas kernels: 32.4 us -> 38.8 us
  starting transfers between devices: 35.2 us -> 38.8 us
  other arithmetic: 10.2 us -> 7.31 us
  local copies, waits for them, and re-layouts: 13.2 us -> 11.1 us
    pallas_call x1 -> x3, Pallas kernels: 11.2 us -> 17.6 us  [the longest x1 9.76 us: spring_free(): pl.pallas_call(functools.partial(free_kernel, scales), grid=(-(-size_y //...]
    all_to_all x1, starting transfers between devices: 8.7 us -> 12.9 us  [on_device(): spectra = lax.all_to_all(message, BOTH, 0, 0, tiled=True)]
    unnamed x53 -> x46, local copies, waits for them, and re-layouts: 7.62 us -> 5.42 us
  transfers between devices with their start and end apart: 12 -> 12, of which waited for: 7 -> 6; matrix products, arithmetic and copies ran while one was open for 8% -> 8% of each run, Pallas kernels for 6% -> 6%
where the time goes in v6:
time: 209 us
  waiting for transfers between devices  109 us (52%)
  starting transfers between devices  38.8 us (19%)
  Pallas kernels  38.8 us (19%)
  local copies, waits for them, and re-layouts  11.1 us (5%)
  other arithmetic  7.31 us (3%)
  matrix products  2.98 us (1%)
    all_to_all x1, waiting for transfers between devices, on_device(): rows = lax.all_to_all(back, BOTH, 0, 0, tiled=True)  54.7 us
    all_to_all x1, waiting for transfers between devices, on_device(): moved = lax.all_to_all(new_fields, 'sample', 0, 0, tiled=True)  26.7 us
    all_to_all x1, waiting for transfers between devices, on_device(): spectra = lax.all_to_all(message, BOTH, 0, 0, tiled=True)  14.3 us
    ppermute x6, waiting for transfers between devices, shifted(): return lax.ppermute(values, 'sample', pairs)  13.2 us
    all_to_all x1, starting transfers between devices, on_device(): spectra = lax.all_to_all(message, BOTH, 0, 0, tiled=True)  12.9 us
    pallas_call x1, Pallas kernels, slab_values(): pl.pallas_call(slab_kernel, grid=(3,), in_specs=[pl.BlockSpec((count, 1,...  12.5 us
    pallas_call x1, Pallas kernels, spring_free(): pl.pallas_call(functools.partial(free_kernel, scales), grid=(-(-size_y //...  9.76 us
    ppermute x6, starting transfers between devices, shifted(): return lax.ppermute(values, 'sample', pairs)  8.59 us
  transfers between devices with their start and end apart: 12, of which 6 were waited for; matrix products, arithmetic and copies ran while one was open for 8% of the time, Pallas kernels for 6%

profile of v6, /device:TPU:5, one launch (start us, length us, event | category | flops | bytes accessed | tf_op | source)
XLA Modules:
  0.0 208.8 jit_solution(3569514645548933312)
XLA Ops:
  0.7 2.3 %multiply_reduce_fusion = f32[8,193,128]{2,1,0:T(8,128)S(1)} fusion(f32[3,1,128,8,193]{2,3,4,1,0:T(8,128)} %param.20), kind=kLoop, calls=%fused_computation.1 | loop fusion | flops 988160 | bytes 3162112 | tf_op jit(solution)/shard_map/reduce_sum | solution.py:498
  4.5 2.6 %collective-permute-start.1 = (f32[2,193,128]{2,1,0:T(8,128)S(1)}, f32[2,193,128]{2,1,0:T(8,128)S(1)}, u32[]{:S(2)}, u32[]{:S(2)}) collective-permute-start(f32[2,193,128]{2,1,0:T(8,128)S(1)} %get-tuple-element.41), channel_id=1, source_target_pairs={{0,32},{16,48},{32,0},{48,16},{64,96},{80,112},{96,64},{112,80},{1... | collective-permute-start | bytes 592904 | tf_op jit(solution)/shard_map/ppermute | solution.py:403
  8.8 1.6 collective-permute-start.5
  10.4 1.6 collective-permute-start.4
  12.0 3.0 %shard_map.193.s_ref = f32[8,3,193,128]{3,2,1,0:T(8,128)} custom-call(f32[8,3,193,128]{3,2,1,0:T(8,128)S(1)} %bitcast.60, bf16[193,193]{1,0:T(8,128)(2,1)S(1)} %get-tuple-element.50.d_ref, bf16[193,193]{1,0:T(8,128)(2,1)S(1)} %get-tuple-element.49.e_ref), custom_call_target="tpu_custom_call" | custom-call | flops 1000000000 | bytes 6000000 | tf_op jit(solution)/shard_map/pallas_call | solution.py:71
  16.1 3.7 %collective-permute-start.3 = (f32[2,193,128]{2,1,0:T(8,128)S(1)}, f32[2,193,128]{2,1,0:T(8,128)S(1)}, u32[]{:S(2)}, u32[]{:S(2)}) collective-permute-start(f32[2,193,128]{2,1,0:T(8,128)S(1)} %fusion.7), channel_id=1, source_target_pairs={{0,64},{16,80},{32,96},{48,112},{64,0},{80,16},{96,32},{112,48},{1... | collective-permute-start | bytes 592904 | tf_op jit(solution)/shard_map/ppermute | solution.py:413
  20.6 9.8 %shard_map.194.refs_4_ = f32[8,3,193,128]{3,2,1,0:T(8,128)} custom-call(f32[8,3,193,128]{3,2,1,0:T(8,128)} %bitcast.61, f32[8,3,193,128]{3,2,1,0:T(8,128)} %shard_map.193.s_ref, f32[3,193,8,128]{3,2,1,0:T(8,128)} %bitcast.67, f32[3,193,8,128]{3,2,1,0:T(8,128)} %bitcast.66, f32[9,193,8,128]{3,2,1,0:T(8,128)} %bitcast.64, f32[3,193,128]{2,1,0:T(8,128)} %copy-done.15, ...), custom_call_target="tpu_custom_call" | custom-call | flops 100000000 | bytes 19000000 | tf_op jit(solution)/shard_map/pallas_call | solution.py:127
  30.4 2.9 %collective-permute-start.8 = (f32[2,193,128]{2,1,0:T(8,128)S(1)}, f32[2,193,128]{2,1,0:T(8,128)S(1)}, u32[]{:S(2)}, u32[]{:S(2)}) collective-permute-start(f32[2,193,128]{2,1,0:T(8,128)S(1)} %add.106.refs_0_), channel_id=1, source_target_pairs={{0,48},{16,0},{32,16},{48,32},{64,112},{80,64},{96,80},{112,96},{1... | collective-permute-start | bytes 592904 | tf_op jit(solution)/shard_map/ppermute | solution.py:403
  33.9 7.5 %collective-permute-done.8.refs_3_ = f32[2,193,128]{2,1,0:T(8,128)S(1)} collective-permute-done((f32[2,193,128]{2,1,0:T(8,128)S(1)}, f32[2,193,128]{2,1,0:T(8,128)S(1)}, u32[]{:S(2)}, u32[]{:S(2)}) %collective-permute-start.8) | collective-permute-done | bytes 197664 | tf_op jit(solution)/shard_map/ppermute | solution.py:403
  41.5 4.6 %collective-permute-done.6.refs_1_ = f32[2,193,128]{2,1,0:T(8,128)S(1)} collective-permute-done((f32[2,193,128]{2,1,0:T(8,128)S(1)}, f32[2,193,128]{2,1,0:T(8,128)S(1)}, u32[]{:S(2)}, u32[]{:S(2)}) %collective-permute-start.6) | collective-permute-done | bytes 197664 | tf_op jit(solution)/shard_map/ppermute | solution.py:403
  46.7 4.9 %shard_map.195 = (f32[8,3,193,128]{3,2,1,0:T(8,128)}, f32[8,193,128]{2,1,0:T(8,128)}) custom-call(s32[1]{0:T(128)} %bitcast.at_ref, f32[2,193,128]{2,1,0:T(8,128)} %copy-done.13, f32[2,193,128]{2,1,0:T(8,128)} %copy-done.18, f32[2,193,128]{2,1,0:T(8,128)} %copy-done.17, f32[2,193,128]{2,1,0:T(8,128)} %copy-done.16, f32[8,3,193,128]{3,2,1,0:T(8,128)} %shard_map.194.refs_4_, ...), custom_call_target="tpu_custom_call" | custom-call | tf_op jit(solution)/shard_map/pallas_call | solution.py:442
  51.6 3.8 %all-to-all-start = ((f32[8,3,193,128]{3,2,1,0:T(8,128)}), f32[8,3,193,128]{3,2,1,0:T(8,128)S(1)}, u32[]{:S(2)}, u32[]{:S(2)}) async-start(f32[8,3,193,128]{3,2,1,0:T(8,128)} %get-tuple-element.29), calls=%async_computation | async-start | bytes 4915200 | tf_op jit(solution)/shard_map/all_to_all | solution.py:500
  55.4 1.9 constant_dynamic-slice_fusion
  57.9 2.3 %convolution_bitcast_fusion.v_ref = f32[3,256,128]{2,1,0:T(8,128)} fusion(f32[3,128,1,193]{1,2,3,0:T(1,128)S(1)} %constant_dynamic-slice_fusion, f32[193,193]{1,0:T(8,128)} %param.25), kind=kOutput, calls=%fused_computation.4 | convolution fusion | flops 227672064 | bytes 838660 | tf_op jit(solution)/shard_map/my,cyx->cmx/dot_general | solution.py:507
  61.1 26.7 %all-to-all-done.n_ref = f32[8,3,193,128]{3,2,1,0:T(8,128)S(1)} async-done(((f32[8,3,193,128]{3,2,1,0:T(8,128)}), f32[8,3,193,128]{3,2,1,0:T(8,128)S(1)}, u32[]{:S(2)}, u32[]{:S(2)}) %all-to-all-start) | async-done | bytes 2371616 | tf_op jit(solution)/shard_map/all_to_all | solution.py:500
  88.8 5.0 %shard_map.196 = f32[2048,128]{1,0:T(8,128)} custom-call(f32[8,3,193,128]{3,2,1,0:T(8,128)S(1)} %all-to-all-done.n_ref, f32[193,128]{1,0:T(8,128)S(1)} %dynamic-slice_bitcast_fusion.s_ref, f32[3,256,128]{2,1,0:T(8,128)S(1)} %copy-done.1, bf16[512,768]{1,0:T(8,128)(2,1)S(1)} %pad_maximum_fusion.m_ref, f32[128,256]{1,0:T(8,128)S(1)} %copy-done.3), custom_call_target="tpu_custom_call" | custom-call | tf_op jit(solution)/shard_map/pallas_call | solution.py:237
  93.8 12.9 %all-to-all-start.1 = ((f32[128,2,8,128]{3,2,1,0:T(8,128)}), f32[128,2,8,128]{3,2,1,0:T(8,128)S(1)}, u32[]{:S(2)}, u32[]{:S(2)}) async-start(f32[128,2,8,128]{3,2,1,0:T(8,128)} %bitcast.22), calls=%async_computation.1 | async-start | bytes 2097152 | tf_op jit(solution)/shard_map/all_to_all | solution.py:519
  110.1 14.3 %all-to-all-done.1.in_ref = f32[128,2,8,128]{3,2,1,0:T(8,128)S(1)} async-done(((f32[128,2,8,128]{3,2,1,0:T(8,128)}), f32[128,2,8,128]{3,2,1,0:T(8,128)S(1)}, u32[]{:S(2)}, u32[]{:S(2)}) %all-to-all-start.1) | async-done | bytes 1048608 | tf_op jit(solution)/shard_map/all_to_all | solution.py:519
  124.4 3.6 %shard_map.197 = (f32[128,3,3,8,128]{4,3,2,1,0:T(8,128)}, f32[6,8,128]{2,1,0:T(8,128)S(1)}) custom-call(f32[128,2,8,128]{3,2,1,0:T(8,128)S(1)} %all-to-all-done.1.in_ref, f32[128,256]{1,0:T(8,128)S(1)} %multiply_add_fusion.d_ref, f32[128,128]{1,0:T(8,128)S(1)} %multiply_add_fusion.1.e_ref, f32[128,128]{1,0:T(8,128)S(1)} %copy-done.5, ...), custom_call_target="tpu_custom_call" | custom-call | tf_op jit(solution)/shard_map/pallas_call | solution.py:299
  128.6 6.7 %all-to-all-start.2 = ((f32[128,3,3,8,128]{4,3,2,1,0:T(8,128)}), f32[128,3,3,8,128]{4,3,2,1,0:T(8,128)}, u32[]{:S(2)}, u32[]{:S(2)}) async-start(f32[128,3,3,8,128]{4,3,2,1,0:T(8,128)} %get-tuple-element.31), calls=%async_computation.2 | async-start | bytes 9437184 | tf_op jit(solution)/shard_map/all_to_all | solution.py:545
  136.4 1.5 fusion.10
  139.7 1.8 copy.26
  141.5 54.7 %all-to-all-done.2.r_ref = f32[128,3,3,8,128]{4,3,2,1,0:T(8,128)} async-done(((f32[128,3,3,8,128]{4,3,2,1,0:T(8,128)}), f32[128,3,3,8,128]{4,3,2,1,0:T(8,128)}, u32[]{:S(2)}, u32[]{:S(2)}) %all-to-all-start.2) | async-done | bytes 4718624 | tf_op jit(solution)/shard_map/all_to_all | solution.py:545
  196.2 12.5 %shard_map.198 = (f32[3,193,8,128]{3,2,1,0:T(8,128)}, f32[9,193,8,128]{3,2,1,0:T(8,128)}) custom-call(f32[128,3,3,8,128]{4,3,2,1,0:T(8,128)} %all-to-all-done.2.r_ref, f32[6,8,128]{2,1,0:T(8,128)} %copy-done.6, bf16[416,768]{1,0:T(8,128)(2,1)} %pad_maximum_fusion.1.t_ref, f32[416,1]{1,0:T(8,128)} %get-tuple-element.45.c_ref, ...), custom_call_target="tpu_custom_call" | custom-call | tf_op jit(solution)/shard_map/pallas_call | solution.py:372
  (80 shorter events, 15.8 us)
Async XLA Ops:
  0.6 7.6 %copy-start.8 = (f32[3,1,128,8,193]{2,3,4,1,0:T(8,128)S(1)}, f32[3,1,128,8,193]{2,3,4,1,0:T(8,128)}, u32[]{:S(2)}) copy-start(f32[3,1,128,8,193]{2,3,4,1,0:T(8,128)} %param.20) | copy-start | bytes 7114756
  3.2 11.8 %collective-permute-start = (f32[2,193,128]{2,1,0:T(8,128)S(1)}, f32[2,193,128]{2,1,0:T(8,128)S(1)}, u32[]{:S(2)}, u32[]{:S(2)}) collective-permute-start(f32[2,193,128]{2,1,0:T(8,128)S(1)} %get-tuple-element.40), channel_id=1, source_target_pairs={{0,16},{16,32},{32,48},{48,0},{64,80},{80,96},{96,112},{112,64},{1... | collective-permute-start | bytes 592904 | tf_op jit(solution)/shard_map/ppermute | solution.py:403
  4.5 11.5 %collective-permute-start.1 = (f32[2,193,128]{2,1,0:T(8,128)S(1)}, f32[2,193,128]{2,1,0:T(8,128)S(1)}, u32[]{:S(2)}, u32[]{:S(2)}) collective-permute-start(f32[2,193,128]{2,1,0:T(8,128)S(1)} %get-tuple-element.41), channel_id=1, source_target_pairs={{0,32},{16,48},{32,0},{48,16},{64,96},{80,112},{96,64},{112,80},{1... | collective-permute-start | bytes 592904 | tf_op jit(solution)/shard_map/ppermute | solution.py:403
  7.2 8.9 %collective-permute-start.2 = (f32[2,193,128]{2,1,0:T(8,128)S(1)}, f32[2,193,128]{2,1,0:T(8,128)S(1)}, u32[]{:S(2)}, u32[]{:S(2)}) collective-permute-start(f32[2,193,128]{2,1,0:T(8,128)S(1)} %get-tuple-element.42), channel_id=1, source_target_pairs={{0,48},{16,0},{32,16},{48,32},{64,112},{80,64},{96,80},{112,96},{1... | collective-permute-start | bytes 592904 | tf_op jit(solution)/shard_map/ppermute | solution.py:403
  8.7 6.2 %copy-start = (f32[3,1,128,8,193]{2,4,0,3,1:T(8,128)}, f32[3,1,128,8,193]{2,4,0,3,1:T(8,128)S(1)}, u32[]{:S(2)}) copy-start(f32[3,1,128,8,193]{2,4,0,3,1:T(8,128)S(1)} %copy.37) | copy-start | bytes 7114756
  8.8 11.0 %collective-permute-start.5 = (f32[3,193,128]{2,1,0:T(8,128)S(1)}, f32[3,193,128]{2,1,0:T(8,128)S(1)}, u32[]{:S(2)}, u32[]{:S(2)}) collective-permute-start(f32[3,193,128]{2,1,0:T(8,128)S(1)} %get-tuple-element.38), channel_id=1, source_target_pairs={{1,0},{2,1},{3,2},{4,3},{5,4},{6,5},{7,6},{8,7},{9,8},{10,9},{11,1... | collective-permute-start | bytes 889352 | tf_op jit(solution)/shard_map/ppermute | solution.py:481
  10.4 9.4 %collective-permute-start.4 = (f32[3,193,128]{2,1,0:T(8,128)S(1)}, f32[3,193,128]{2,1,0:T(8,128)S(1)}, u32[]{:S(2)}, u32[]{:S(2)}) collective-permute-start(f32[3,193,128]{2,1,0:T(8,128)S(1)} %get-tuple-element.39), channel_id=1, source_target_pairs={{0,1},{1,2},{2,3},{3,4},{4,5},{5,6},{6,7},{7,8},{8,9},{9,10},{10,1... | collective-permute-start | bytes 889352 | tf_op jit(solution)/shard_map/ppermute | solution.py:480
  16.1 14.3 %collective-permute-start.3 = (f32[2,193,128]{2,1,0:T(8,128)S(1)}, f32[2,193,128]{2,1,0:T(8,128)S(1)}, u32[]{:S(2)}, u32[]{:S(2)}) collective-permute-start(f32[2,193,128]{2,1,0:T(8,128)S(1)} %fusion.7), channel_id=1, source_target_pairs={{0,64},{16,80},{32,96},{48,112},{64,0},{80,16},{96,32},{112,48},{1... | collective-permute-start | bytes 592904 | tf_op jit(solution)/shard_map/ppermute | solution.py:413
  30.4 15.7 %copy-start.13 = (f32[2,193,128]{2,1,0:T(8,128)}, f32[2,193,128]{2,1,0:T(8,128)S(1)}, u32[]{:S(2)}) copy-start(f32[2,193,128]{2,1,0:T(8,128)S(1)} %add.106.refs_0_) | copy-start | bytes 592900
  30.4 11.1 %collective-permute-start.8 = (f32[2,193,128]{2,1,0:T(8,128)S(1)}, f32[2,193,128]{2,1,0:T(8,128)S(1)}, u32[]{:S(2)}, u32[]{:S(2)}) collective-permute-start(f32[2,193,128]{2,1,0:T(8,128)S(1)} %add.106.refs_0_), channel_id=1, source_target_pairs={{0,48},{16,0},{32,16},{48,32},{64,112},{80,64},{96,80},{112,96},{1... | collective-permute-start | bytes 592904 | tf_op jit(solution)/shard_map/ppermute | solution.py:403
  33.3 8.2 %collective-permute-start.7 = (f32[2,193,128]{2,1,0:T(8,128)S(1)}, f32[2,193,128]{2,1,0:T(8,128)S(1)}, u32[]{:S(2)}, u32[]{:S(2)}) collective-permute-start(f32[2,193,128]{2,1,0:T(8,128)S(1)} %add.106.refs_0_), channel_id=1, source_target_pairs={{0,32},{16,48},{32,0},{48,16},{64,96},{80,112},{96,64},{112,80},{1... | collective-permute-start | bytes 592904 | tf_op jit(solution)/shard_map/ppermute | solution.py:403
  33.5 12.5 %collective-permute-start.6 = (f32[2,193,128]{2,1,0:T(8,128)S(1)}, f32[2,193,128]{2,1,0:T(8,128)S(1)}, u32[]{:S(2)}, u32[]{:S(2)}) collective-permute-start(f32[2,193,128]{2,1,0:T(8,128)S(1)} %add.106.refs_0_), channel_id=1, source_target_pairs={{0,16},{16,32},{32,48},{48,0},{64,80},{80,96},{96,112},{112,64},{1... | collective-permute-start | bytes 592904 | tf_op jit(solution)/shard_map/ppermute | solution.py:403
  51.6 36.2 %all-to-all-start = ((f32[8,3,193,128]{3,2,1,0:T(8,128)}), f32[8,3,193,128]{3,2,1,0:T(8,128)S(1)}, u32[]{:S(2)}, u32[]{:S(2)}) async-start(f32[8,3,193,128]{3,2,1,0:T(8,128)} %get-tuple-element.29), calls=%async_computation | async-start | bytes 4915200 | tf_op jit(solution)/shard_map/all_to_all | solution.py:500
  55.4 32.4 %copy-start.3 = (f32[128,256]{1,0:T(8,128)S(1)}, f32[128,256]{1,0:T(8,128)}, u32[]{:S(2)}) copy-start(f32[128,256]{1,0:T(8,128)} %constant.102.clone.x_ref) | copy-start | bytes 393220
  88.8 17.9 %copy-start.19 = (f32[193]{0:T(256)S(1)}, f32[193]{0:T(256)}, u32[]{:S(2)}) copy-start(f32[193]{0:T(256)} %param.27) | copy-start | bytes 2320
  88.8 18.5 %copy-start.20 = (f32[128]{0:T(128)S(1)}, f32[128]{0:T(128)}, u32[]{:S(2)}) copy-start(f32[128]{0:T(128)} %constant.103.clone) | copy-start | bytes 1540
  88.8 19.8 %copy-start.21 = (f32[128]{0:T(128)S(1)}, f32[128]{0:T(128)}, u32[]{:S(2)}) copy-start(f32[128]{0:T(128)} %constant.104.clone) | copy-start | bytes 1540
  93.8 30.6 %copy-start.2 = (f32[256,128]{1,0:T(8,128)S(1)}, f32[256,128]{1,0:T(8,128)}, u32[]{:S(2)}) copy-start(f32[256,128]{1,0:T(8,128)} %constant.108.clone.b_ref) | copy-start | bytes 393220
  93.8 30.6 %copy-start.4 = (f32[128,128]{1,0:T(8,128)S(1)}, f32[128,128]{1,0:T(8,128)}, u32[]{:S(2)}) copy-start(f32[128,128]{1,0:T(8,128)} %constant.107.clone.g_ref) | copy-start | bytes 196612
  93.8 30.6 %copy-start.5 = (f32[128,128]{1,0:T(8,128)S(1)}, f32[128,128]{1,0:T(8,128)}, u32[]{:S(2)}) copy-start(f32[128,128]{1,0:T(8,128)} %constant.106.clone.f_ref) | copy-start | bytes 196612
  93.8 30.6 %all-to-all-start.1 = ((f32[128,2,8,128]{3,2,1,0:T(8,128)}), f32[128,2,8,128]{3,2,1,0:T(8,128)S(1)}, u32[]{:S(2)}, u32[]{:S(2)}) async-start(f32[128,2,8,128]{3,2,1,0:T(8,128)} %bitcast.22), calls=%async_computation.1 | async-start | bytes 2097152 | tf_op jit(solution)/shard_map/all_to_all | solution.py:519
  128.6 7.4 %copy-start.11 = (f32[193,193]{1,0:T(8,128)S(1)}, f32[193,193]{1,0:T(8,128)}, u32[]{:S(2)}) copy-start(f32[193,193]{1,0:T(8,128)} %param.24) | copy-start | bytes 446992
  128.6 7.4 %copy-start.12 = (f32[193,193]{1,0:T(8,128)S(1)}, f32[193,193]{1,0:T(8,128)}, u32[]{:S(2)}) copy-start(f32[193,193]{1,0:T(8,128)} %param.26) | copy-start | bytes 446992
  128.6 67.6 %all-to-all-start.2 = ((f32[128,3,3,8,128]{4,3,2,1,0:T(8,128)}), f32[128,3,3,8,128]{4,3,2,1,0:T(8,128)}, u32[]{:S(2)}, u32[]{:S(2)}) async-start(f32[128,3,3,8,128]{4,3,2,1,0:T(8,128)} %get-tuple-element.31), calls=%async_computation.2 | async-start | bytes 9437184 | tf_op jit(solution)/shard_map/all_to_all | solution.py:545
  (10 other events, 25.9 us)

commit v7 on v5

--- a/solution.py
+++ b/solution.py
@@ -142,6 +142,19 @@
     return jnp.asarray(np.concatenate([high, high, low], axis=0))
 
 
+def paired_three(table):
+    table = np.asarray(table, np.float32)
+    high = table.astype(jnp.bfloat16)
+    low = (table - high.astype(np.float32)).astype(jnp.bfloat16)
+    column = np.concatenate([high, high, low], axis=0)
+    empty = np.zeros_like(column)
+    return jnp.asarray(
+        np.concatenate(
+            [np.concatenate([column, empty], axis=1), np.concatenate([empty, column], axis=1)]
+        )
+    )
+
+
 def split_three(table, axis):
     high = lax.reduce_precision(table, 8, 7)
     low = (table - high).astype(jnp.bfloat16)
@@ -167,20 +180,24 @@
 
 def plane_kernel(n_ref, s_ref, v_ref, m_ref, x_ref, o_ref, t_ref):
     k = pl.program_id(0)
-    count = pl.num_programs(0)
+    steps = pl.num_programs(0)
+    count = steps * n_ref.shape[0]
     size_y, size_x = s_ref.shape
 
     @pl.when(k == 0)
     def _():
         t_ref[...] = jnp.zeros_like(t_ref)
 
-    for start in range(0, size_y, 64):
-        part = pl.ds(start, min(64, size_y - start))
-        moved = [n_ref[0, c, part, :] for c in range(3)]
+    for start in range(0, size_y, 32):
+        part = pl.ds(start, min(32, size_y - start))
+        moved = [[n_ref[f, c, part, :] for c in range(3)] for f in range(n_ref.shape[0])]
         for p, (i, j) in enumerate(PAIRS):
-            t_ref[p, part, :] += moved[i] * moved[j]
-
-    @pl.when(k == count - 1)
+            value = moved[0][i] * moved[0][j]
+            for own in moved[1:]:
+                value += own[i] * own[j]
+            t_ref[p, part, :] += value
+
+    @pl.when(k == steps - 1)
     def _():
         for start in range(0, size_y, 64):
             part = pl.ds(start, min(64, size_y - start))
@@ -230,9 +247,9 @@
     whole = pl.BlockSpec(memory_space=pltpu.VMEM)
     message = pl.pallas_call(
         plane_kernel,
-        grid=(count,),
+        grid=(2,),
         in_specs=[
-            pl.BlockSpec((1, 3, size_y, size_x), lambda k: (k, 0, 0, 0)),
+            pl.BlockSpec((count // 2, 3, size_y, size_x), lambda k: (k, 0, 0, 0)),
             whole,
             whole,
             whole,
@@ -306,7 +323,7 @@
     )(spectra, damping, last_damping, forward, forward_slope, inverse, slab_inverse)
 
 
-def slab_kernel(r_ref, l_ref, t_ref, c_ref, x_ref, v_ref, g_ref):
+def slab_kernel(r_ref, l_ref, t_ref, c_ref, x_ref, b_ref, v_ref, g_ref):
     i = pl.program_id(0)
     rows = r_ref.shape[0]
     _, size_y, slab, size_x = v_ref.shape
@@ -350,15 +367,15 @@
             out_v[place, :] = both[:size_y, :size_x]
             out_g[0, place, :] = both[:size_y, size_x:]
             both = jnp.dot(
-                three_of(jnp.concatenate([value_z[half:], slope_z], axis=0), 1),
-                x_ref[:, :size_x],
+                jnp.concatenate([three_of(value_z[half:], 1), three_of(slope_z, 1)], axis=1),
+                b_ref[...],
                 preferred_element_type=jnp.float32,
             )
-            out_g[1, place, :] = both[:size_y]
-            out_g[2, place, :] = both[half : half + size_y]
-
-
-def slab_values(rows, last, wall_table, last_column, table_x, size_y):
+            out_g[1, place, :] = both[:size_y, :size_x]
+            out_g[2, place, :] = both[:size_y, size_x:]
+
+
+def slab_values(rows, last, wall_table, last_column, table_x, table_pair, size_y):
     count = rows.shape[0]
     slab, size_x = rows.shape[3], table_x.shape[1] // 2
     whole = pl.BlockSpec(memory_space=pltpu.VMEM)
@@ -368,6 +385,7 @@
         grid=(3,),
         in_specs=[
             pl.BlockSpec((count, 1, 3, slab, 128), lambda i: (0, i, 0, 0, 0)),
+            whole,
             whole,
             whole,
             whole,
@@ -382,7 +400,7 @@
             jax.ShapeDtypeStruct((9, size_y, slab, size_x), jnp.float32),
         ),
         compiler_params=pltpu.CompilerParams(vmem_limit_bytes=60 * 1024 * 1024),
-    )(rows, last, wall_table, last_column, table_x)
+    )(rows, last, wall_table, last_column, table_x, table_pair)
 
 
 def summed(planes, beside):
@@ -504,6 +522,7 @@
         split_three(wall_table.at[:, size_y - 1].set(0.0), 1),
         wall_table[:, size_y - 1 : size_y],
         stacked_three(np.concatenate([rows_x, (rows_x.T @ slope_rows_x).T], axis=1)),
+        paired_three(rows_x),
         size_y,
     )
     return (

time: 204 us -> 204 us (level)
  no operation moved by 1% of the time
where the time goes in v7:
time: 204 us; the launch traced here: 203 us
  waiting for transfers between devices  110 us (54%)
  starting transfers between devices  35.2 us (17%)
  Pallas kernels  31.8 us (16%)
  local copies, waits for them, and re-layouts  13.2 us (6%)
  other arithmetic  10.2 us (5%)
  matrix products  2.05 us (1%)
    all_to_all x1, waiting for transfers between devices, on_device(): rows = lax.all_to_all(back, BOTH, 0, 0, tiled=True)  54.5 us
    all_to_all x1, waiting for transfers between devices, on_device(): moved = lax.all_to_all(new_fields, 'sample', 0, 0, tiled=True)  27.2 us
    all_to_all x1, waiting for transfers between devices, on_device(): spectra = lax.all_to_all(message, BOTH, 0, 0, tiled=True)  14.3 us
    ppermute x6, waiting for transfers between devices, shifted(): return lax.ppermute(values, 'sample', pairs)  13.5 us
    pallas_call x1, Pallas kernels, slab_values(): pl.pallas_call(slab_kernel, grid=(3,), in_specs=[pl.BlockSpec((count, 1,...  12.2 us
    pallas_call x1, Pallas kernels, spring_free(): pl.pallas_call(functools.partial(free_kernel, scales), grid=(steps,), in_...  11.2 us
    ppermute x6, starting transfers between devices, shifted(): return lax.ppermute(values, 'sample', pairs)  9.2 us
    all_to_all x1, starting transfers between devices, on_device(): spectra = lax.all_to_all(message, BOTH, 0, 0, tiled=True)  8.7 us
  transfers between devices with their start and end apart: 12, of which 7 were waited for; matrix products, arithmetic and copies ran while one was open for 8% of the time, Pallas kernels for 6%

profile of v7, /device:TPU:5, one launch (start us, length us, event | category | flops | bytes accessed | tf_op | source)
XLA Modules:
  0.0 203.1 jit_solution(18161619422936817312)
XLA Ops:
  0.6 2.1 %multiply_reduce_fusion = f32[8,193,128]{2,1,0:T(8,128)S(1)} fusion(f32[3,1,128,8,193]{2,3,4,1,0:T(8,128)} %param.21), kind=kLoop, calls=%fused_computation.2 | loop fusion | flops 988160 | bytes 3162112 | tf_op jit(solution)/shard_map/reduce_sum | solution.py:465
  4.4 2.6 %collective-permute-start.1 = (f32[2,193,128]{2,1,0:T(8,128)S(1)}, f32[2,193,128]{2,1,0:T(8,128)S(1)}, u32[]{:S(2)}, u32[]{:S(2)}) collective-permute-start(f32[2,193,128]{2,1,0:T(8,128)S(1)} %get-tuple-element.33), channel_id=1, source_target_pairs={{0,32},{16,48},{32,0},{48,16},{64,96},{80,112},{96,64},{112,80},{1... | collective-permute-start | bytes 592904 | tf_op jit(solution)/shard_map/ppermute | solution.py:415
  8.6 1.6 collective-permute-start.5
  10.2 1.6 collective-permute-start.4
  12.5 3.4 %collective-permute-done.1 = f32[2,193,128]{2,1,0:T(8,128)S(1)} collective-permute-done((f32[2,193,128]{2,1,0:T(8,128)S(1)}, f32[2,193,128]{2,1,0:T(8,128)S(1)}, u32[]{:S(2)}, u32[]{:S(2)}) %collective-permute-start.1) | collective-permute-done | bytes 197664 | tf_op jit(solution)/shard_map/ppermute | solution.py:415
  15.9 3.7 %collective-permute-start.3 = (f32[2,193,128]{2,1,0:T(8,128)S(1)}, f32[2,193,128]{2,1,0:T(8,128)S(1)}, u32[]{:S(2)}, u32[]{:S(2)}) collective-permute-start(f32[2,193,128]{2,1,0:T(8,128)S(1)} %fusion.7), channel_id=1, source_target_pairs={{0,64},{16,80},{32,96},{48,112},{64,0},{80,16},{96,32},{112,48},{1... | collective-permute-start | bytes 592904 | tf_op jit(solution)/shard_map/ppermute | solution.py:424
  20.4 11.2 %shard_map.202 = f32[8,3,193,128]{3,2,1,0:T(8,128)} custom-call(f32[8,3,193,128]{3,2,1,0:T(8,128)} %bitcast.75, f32[8,3,193,128]{3,2,1,0:T(8,128)} %bitcast.76, f32[3,193,8,128]{3,2,1,0:T(8,128)} %bitcast.82, f32[3,193,8,128]{3,2,1,0:T(8,128)} %bitcast.81, f32[9,193,8,128]{3,2,1,0:T(8,128)} %bitcast.78, f32[3,193,128]{2,1,0:T(8,128)} %copy-done.18, ...), custom_call_target="tpu_custom_call" | custom-call | flops 3000000000 | bytes 18000000 | tf_op jit(solution)/shard_map/pallas_call | solution.py:120
  31.7 2.9 %collective-permute-start.6 = (f32[2,193,128]{2,1,0:T(8,128)S(1)}, f32[2,193,128]{2,1,0:T(8,128)S(1)}, u32[]{:S(2)}, u32[]{:S(2)}) collective-permute-start(f32[2,193,128]{2,1,0:T(8,128)S(1)} %add.112), channel_id=1, source_target_pairs={{0,48},{16,0},{32,16},{48,32},{64,112},{80,64},{96,80},{112,96},{1... | collective-permute-start | bytes 592904 | tf_op jit(solution)/shard_map/ppermute | solution.py:415
  35.9 2.2 %collective-permute-done.6 = f32[2,193,128]{2,1,0:T(8,128)S(1)} collective-permute-done((f32[2,193,128]{2,1,0:T(8,128)S(1)}, f32[2,193,128]{2,1,0:T(8,128)S(1)}, u32[]{:S(2)}, u32[]{:S(2)}) %collective-permute-start.6) | collective-permute-done | bytes 197664 | tf_op jit(solution)/shard_map/ppermute | solution.py:415
  38.1 5.2 %collective-permute-done.7 = f32[2,193,128]{2,1,0:T(8,128)S(1)} collective-permute-done((f32[2,193,128]{2,1,0:T(8,128)S(1)}, f32[2,193,128]{2,1,0:T(8,128)S(1)}, u32[]{:S(2)}, u32[]{:S(2)}) %collective-permute-start.7) | collective-permute-done | bytes 197664 | tf_op jit(solution)/shard_map/ppermute | solution.py:415
  43.3 2.7 %collective-permute-done.8 = f32[2,193,128]{2,1,0:T(8,128)S(1)} collective-permute-done((f32[2,193,128]{2,1,0:T(8,128)S(1)}, f32[2,193,128]{2,1,0:T(8,128)S(1)}, u32[]{:S(2)}, u32[]{:S(2)}) %collective-permute-start.8) | collective-permute-done | bytes 197664 | tf_op jit(solution)/shard_map/ppermute | solution.py:415
  48.8 2.0 %multiply_subtract_fusion = f32[8,3,193,128]{3,2,1,0:T(8,128)} fusion(f32[8,3,193,128]{3,2,1,0:T(8,128)S(1)} %copy-done.10, f32[8,193,128]{2,1,0:T(8,128)S(1)} %broadcast_multiply_fusion, f32[3,1,128,8,193]{2,3,4,1,0:T(8,128)S(1)} %copy-done.9), kind=kLoop, calls=%fused_computation.1 | loop fusion | flops 1185792 | bytes 7905280 | tf_op jit(solution)/shard_map/sub | solution.py:467
  50.8 3.8 %all-to-all-start = ((f32[8,3,193,128]{3,2,1,0:T(8,128)}), f32[8,3,193,128]{3,2,1,0:T(8,128)S(1)}, u32[]{:S(2)}, u32[]{:S(2)}) async-start(f32[8,3,193,128]{3,2,1,0:T(8,128)} %multiply_subtract_fusion), calls=%async_computation | async-start | bytes 4915200 | tf_op jit(solution)/shard_map/all_to_all | solution.py:468
  54.6 1.9 constant_dynamic-slice_fusion
  59.7 27.2 %all-to-all-done.n_ref = f32[8,3,193,128]{3,2,1,0:T(8,128)S(1)} async-done(((f32[8,3,193,128]{3,2,1,0:T(8,128)}), f32[8,3,193,128]{3,2,1,0:T(8,128)S(1)}, u32[]{:S(2)}, u32[]{:S(2)}) %all-to-all-start) | async-done | bytes 2371616 | tf_op jit(solution)/shard_map/all_to_all | solution.py:468
  87.9 4.8 %shard_map.203 = f32[2048,128]{1,0:T(8,128)} custom-call(f32[8,3,193,128]{3,2,1,0:T(8,128)S(1)} %all-to-all-done.n_ref, f32[193,128]{1,0:T(8,128)S(1)} %dynamic-slice_bitcast_fusion.s_ref, f32[3,256,128]{2,1,0:T(8,128)S(1)} %copy-done, bf16[512,768]{1,0:T(8,128)(2,1)S(1)} %pad_maximum_fusion.m_ref, f32[128,256]{1,0:T(8,128)S(1)} %copy-done.2), custom_call_target="tpu_custom_call" | custom-call | tf_op jit(solution)/shard_map/pallas_call | solution.py:248
  92.7 8.7 %all-to-all-start.1 = ((f32[128,2,8,128]{3,2,1,0:T(8,128)}), f32[128,2,8,128]{3,2,1,0:T(8,128)S(1)}, u32[]{:S(2)}, u32[]{:S(2)}) async-start(f32[128,2,8,128]{3,2,1,0:T(8,128)} %bitcast.26), calls=%async_computation.1 | async-start | bytes 2097152 | tf_op jit(solution)/shard_map/all_to_all | solution.py:487
  104.8 14.3 %all-to-all-done.1.in_ref = f32[128,2,8,128]{3,2,1,0:T(8,128)S(1)} async-done(((f32[128,2,8,128]{3,2,1,0:T(8,128)}), f32[128,2,8,128]{3,2,1,0:T(8,128)S(1)}, u32[]{:S(2)}, u32[]{:S(2)}) %all-to-all-start.1) | async-done | bytes 1048608 | tf_op jit(solution)/shard_map/all_to_all | solution.py:487
  119.2 3.6 %shard_map.204 = (f32[128,3,3,8,128]{4,3,2,1,0:T(8,128)}, f32[6,8,128]{2,1,0:T(8,128)S(1)}) custom-call(f32[128,2,8,128]{3,2,1,0:T(8,128)S(1)} %all-to-all-done.1.in_ref, f32[128,256]{1,0:T(8,128)S(1)} %multiply_add_fusion.d_ref, f32[128,128]{1,0:T(8,128)S(1)} %multiply_add_fusion.1.e_ref, f32[128,128]{1,0:T(8,128)S(1)} %copy-done.4, ...), custom_call_target="tpu_custom_call" | custom-call | tf_op jit(solution)/shard_map/pallas_call | solution.py:310
  123.4 6.7 %all-to-all-start.2 = ((f32[128,3,3,8,128]{4,3,2,1,0:T(8,128)}), f32[128,3,3,8,128]{4,3,2,1,0:T(8,128)}, u32[]{:S(2)}, u32[]{:S(2)}) async-start(f32[128,3,3,8,128]{4,3,2,1,0:T(8,128)} %get-tuple-element.23), calls=%async_computation.2 | async-start | bytes 9437184 | tf_op jit(solution)/shard_map/all_to_all | solution.py:513
  131.1 1.6 fusion.10
  134.6 1.8 copy.27
  136.4 54.5 %all-to-all-done.2.r_ref = f32[128,3,3,8,128]{4,3,2,1,0:T(8,128)} async-done(((f32[128,3,3,8,128]{4,3,2,1,0:T(8,128)}), f32[128,3,3,8,128]{4,3,2,1,0:T(8,128)}, u32[]{:S(2)}, u32[]{:S(2)}) %all-to-all-start.2) | async-done | bytes 4718624 | tf_op jit(solution)/shard_map/all_to_all | solution.py:513
  190.9 12.2 %shard_map.205 = (f32[3,193,8,128]{3,2,1,0:T(8,128)}, f32[9,193,8,128]{3,2,1,0:T(8,128)}) custom-call(f32[128,3,3,8,128]{4,3,2,1,0:T(8,128)} %all-to-all-done.2.r_ref, f32[6,8,128]{2,1,0:T(8,128)} %copy-done.5, bf16[416,768]{1,0:T(8,128)(2,1)} %pad_maximum_fusion.1.t_ref, f32[416,1]{1,0:T(8,128)} %get-tuple-element.37.c_ref, ...), custom_call_target="tpu_custom_call" | custom-call | tf_op jit(solution)/shard_map/pallas_call | solution.py:383
  (89 shorter events, 19.8 us)
Async XLA Ops:
  2.8 5.3 %copy-start.8 = (f32[3,1,128,8,193]{2,3,4,1,0:T(8,128)S(1)}, f32[3,1,128,8,193]{2,3,4,1,0:T(8,128)}, u32[]{:S(2)}) copy-start(f32[3,1,128,8,193]{2,3,4,1,0:T(8,128)} %param.21) | copy-start | bytes 7114756
  3.0 9.5 %collective-permute-start = (f32[2,193,128]{2,1,0:T(8,128)S(1)}, f32[2,193,128]{2,1,0:T(8,128)S(1)}, u32[]{:S(2)}, u32[]{:S(2)}) collective-permute-start(f32[2,193,128]{2,1,0:T(8,128)S(1)} %get-tuple-element.32), channel_id=1, source_target_pairs={{0,16},{16,32},{32,48},{48,0},{64,80},{80,96},{96,112},{112,64},{1... | collective-permute-start | bytes 592904 | tf_op jit(solution)/shard_map/ppermute | solution.py:415
  4.4 11.5 %collective-permute-start.1 = (f32[2,193,128]{2,1,0:T(8,128)S(1)}, f32[2,193,128]{2,1,0:T(8,128)S(1)}, u32[]{:S(2)}, u32[]{:S(2)}) collective-permute-start(f32[2,193,128]{2,1,0:T(8,128)S(1)} %get-tuple-element.33), channel_id=1, source_target_pairs={{0,32},{16,48},{32,0},{48,16},{64,96},{80,112},{96,64},{112,80},{1... | collective-permute-start | bytes 592904 | tf_op jit(solution)/shard_map/ppermute | solution.py:415
  7.0 4.8 %copy-start.14 = (f32[193,193]{1,0:T(8,128)S(1)}, f32[193,193]{1,0:T(8,128)}, u32[]{:S(2)}) copy-start(f32[193,193]{1,0:T(8,128)} %param.25) | copy-start | bytes 446992
  7.0 8.9 %collective-permute-start.2 = (f32[2,193,128]{2,1,0:T(8,128)S(1)}, f32[2,193,128]{2,1,0:T(8,128)S(1)}, u32[]{:S(2)}, u32[]{:S(2)}) collective-permute-start(f32[2,193,128]{2,1,0:T(8,128)S(1)} %get-tuple-element.34), channel_id=1, source_target_pairs={{0,48},{16,0},{32,16},{48,32},{64,112},{80,64},{96,80},{112,96},{1... | collective-permute-start | bytes 592904 | tf_op jit(solution)/shard_map/ppermute | solution.py:415
  8.5 11.1 %copy-start.6 = (f32[3,1,128,8,193]{2,4,0,3,1:T(8,128)}, f32[3,1,128,8,193]{2,4,0,3,1:T(8,128)S(1)}, u32[]{:S(2)}) copy-start(f32[3,1,128,8,193]{2,4,0,3,1:T(8,128)S(1)} %copy.40) | copy-start | bytes 7114756
  8.6 11.0 %collective-permute-start.5 = (f32[3,193,128]{2,1,0:T(8,128)S(1)}, f32[3,193,128]{2,1,0:T(8,128)S(1)}, u32[]{:S(2)}, u32[]{:S(2)}) collective-permute-start(f32[3,193,128]{2,1,0:T(8,128)S(1)} %get-tuple-element.30), channel_id=1, source_target_pairs={{1,0},{2,1},{3,2},{4,3},{5,4},{6,5},{7,6},{8,7},{9,8},{10,9},{11,1... | collective-permute-start | bytes 889352 | tf_op jit(solution)/shard_map/ppermute | solution.py:452
  10.2 9.4 %collective-permute-start.4 = (f32[3,193,128]{2,1,0:T(8,128)S(1)}, f32[3,193,128]{2,1,0:T(8,128)S(1)}, u32[]{:S(2)}, u32[]{:S(2)}) collective-permute-start(f32[3,193,128]{2,1,0:T(8,128)S(1)} %get-tuple-element.31), channel_id=1, source_target_pairs={{0,1},{1,2},{2,3},{3,4},{4,5},{5,6},{6,7},{7,8},{8,9},{9,10},{10,1... | collective-permute-start | bytes 889352 | tf_op jit(solution)/shard_map/ppermute | solution.py:451
  15.9 15.7 %collective-permute-start.3 = (f32[2,193,128]{2,1,0:T(8,128)S(1)}, f32[2,193,128]{2,1,0:T(8,128)S(1)}, u32[]{:S(2)}, u32[]{:S(2)}) collective-permute-start(f32[2,193,128]{2,1,0:T(8,128)S(1)} %fusion.7), channel_id=1, source_target_pairs={{0,64},{16,80},{32,96},{48,112},{64,0},{80,16},{96,32},{112,48},{1... | collective-permute-start | bytes 592904 | tf_op jit(solution)/shard_map/ppermute | solution.py:424
  31.7 6.3 %collective-permute-start.6 = (f32[2,193,128]{2,1,0:T(8,128)S(1)}, f32[2,193,128]{2,1,0:T(8,128)S(1)}, u32[]{:S(2)}, u32[]{:S(2)}) collective-permute-start(f32[2,193,128]{2,1,0:T(8,128)S(1)} %add.112), channel_id=1, source_target_pairs={{0,48},{16,0},{32,16},{48,32},{64,112},{80,64},{96,80},{112,96},{1... | collective-permute-start | bytes 592904 | tf_op jit(solution)/shard_map/ppermute | solution.py:415
  34.6 11.5 %collective-permute-start.8 = (f32[2,193,128]{2,1,0:T(8,128)S(1)}, f32[2,193,128]{2,1,0:T(8,128)S(1)}, u32[]{:S(2)}, u32[]{:S(2)}) collective-permute-start(f32[2,193,128]{2,1,0:T(8,128)S(1)} %add.112), channel_id=1, source_target_pairs={{0,16},{16,32},{32,48},{48,0},{64,80},{80,96},{96,112},{112,64},{1... | collective-permute-start | bytes 592904 | tf_op jit(solution)/shard_map/ppermute | solution.py:415
  34.6 8.7 %collective-permute-start.7 = (f32[2,193,128]{2,1,0:T(8,128)S(1)}, f32[2,193,128]{2,1,0:T(8,128)S(1)}, u32[]{:S(2)}, u32[]{:S(2)}) collective-permute-start(f32[2,193,128]{2,1,0:T(8,128)S(1)} %add.112), channel_id=1, source_target_pairs={{0,32},{16,48},{32,0},{48,16},{64,96},{80,112},{96,64},{112,80},{1... | collective-permute-start | bytes 592904 | tf_op jit(solution)/shard_map/ppermute | solution.py:415
  50.8 36.1 %all-to-all-start = ((f32[8,3,193,128]{3,2,1,0:T(8,128)}), f32[8,3,193,128]{3,2,1,0:T(8,128)S(1)}, u32[]{:S(2)}, u32[]{:S(2)}) async-start(f32[8,3,193,128]{3,2,1,0:T(8,128)} %multiply_subtract_fusion), calls=%async_computation | async-start | bytes 4915200 | tf_op jit(solution)/shard_map/all_to_all | solution.py:468
  56.9 30.0 %copy-start.2 = (f32[128,256]{1,0:T(8,128)S(1)}, f32[128,256]{1,0:T(8,128)}, u32[]{:S(2)}) copy-start(f32[128,256]{1,0:T(8,128)} %constant.119.clone.x_ref) | copy-start | bytes 393220
  92.7 8.8 %copy-start.19 = (f32[193]{0:T(256)S(1)}, f32[193]{0:T(256)}, u32[]{:S(2)}) copy-start(f32[193]{0:T(256)} %param.28) | copy-start | bytes 2320
  92.7 9.3 %copy-start.20 = (f32[128]{0:T(128)S(1)}, f32[128]{0:T(128)}, u32[]{:S(2)}) copy-start(f32[128]{0:T(128)} %constant.120.clone) | copy-start | bytes 1540
  92.7 10.6 %copy-start.21 = (f32[128]{0:T(128)S(1)}, f32[128]{0:T(128)}, u32[]{:S(2)}) copy-start(f32[128]{0:T(128)} %constant.121.clone) | copy-start | bytes 1540
  92.7 26.4 %copy-start.1 = (f32[256,128]{1,0:T(8,128)S(1)}, f32[256,128]{1,0:T(8,128)}, u32[]{:S(2)}) copy-start(f32[256,128]{1,0:T(8,128)} %constant.125.clone.b_ref) | copy-start | bytes 393220
  92.7 26.4 %copy-start.3 = (f32[128,128]{1,0:T(8,128)S(1)}, f32[128,128]{1,0:T(8,128)}, u32[]{:S(2)}) copy-start(f32[128,128]{1,0:T(8,128)} %constant.124.clone.g_ref) | copy-start | bytes 196612
  92.7 26.4 %copy-start.4 = (f32[128,128]{1,0:T(8,128)S(1)}, f32[128,128]{1,0:T(8,128)}, u32[]{:S(2)}) copy-start(f32[128,128]{1,0:T(8,128)} %constant.123.clone.f_ref) | copy-start | bytes 196612
  92.7 26.4 %all-to-all-start.1 = ((f32[128,2,8,128]{3,2,1,0:T(8,128)}), f32[128,2,8,128]{3,2,1,0:T(8,128)S(1)}, u32[]{:S(2)}, u32[]{:S(2)}) async-start(f32[128,2,8,128]{3,2,1,0:T(8,128)} %bitcast.26), calls=%async_computation.1 | async-start | bytes 2097152 | tf_op jit(solution)/shard_map/all_to_all | solution.py:487
  123.4 7.3 %copy-start.15 = (f32[193,193]{1,0:T(8,128)S(1)}, f32[193,193]{1,0:T(8,128)}, u32[]{:S(2)}) copy-start(f32[193,193]{1,0:T(8,128)} %param.25) | copy-start | bytes 446992
  123.4 7.3 %copy-start.16 = (f32[193,193]{1,0:T(8,128)S(1)}, f32[193,193]{1,0:T(8,128)}, u32[]{:S(2)}) copy-start(f32[193,193]{1,0:T(8,128)} %param.27) | copy-start | bytes 446992
  123.4 67.6 %all-to-all-start.2 = ((f32[128,3,3,8,128]{4,3,2,1,0:T(8,128)}), f32[128,3,3,8,128]{4,3,2,1,0:T(8,128)}, u32[]{:S(2)}, u32[]{:S(2)}) async-start(f32[128,3,3,8,128]{4,3,2,1,0:T(8,128)} %get-tuple-element.23), calls=%async_computation.2 | async-start | bytes 9437184 | tf_op jit(solution)/shard_map/all_to_all | solution.py:513
  (10 other events, 16.8 us)

commit v8 on v6

--- a/solution.py
+++ b/solution.py
@@ -148,6 +148,19 @@
     return jnp.asarray(np.concatenate([high, high, low], axis=0))
 
 
+def paired_three(table):
+    table = np.asarray(table, np.float32)
+    high = table.astype(jnp.bfloat16)
+    low = (table - high.astype(np.float32)).astype(jnp.bfloat16)
+    column = np.concatenate([high, high, low], axis=0)
+    empty = np.zeros_like(column)
+    return jnp.asarray(
+        np.concatenate(
+            [np.concatenate([column, empty], axis=1), np.concatenate([empty, column], axis=1)]
+        )
+    )
+
+
 def split_three(table, axis):
     high = lax.reduce_precision(table, 8, 7)
     low = (table - high).astype(jnp.bfloat16)
@@ -173,20 +186,24 @@
 
 def plane_kernel(n_ref, s_ref, v_ref, m_ref, x_ref, o_ref, t_ref):
     k = pl.program_id(0)
-    count = pl.num_programs(0)
+    steps = pl.num_programs(0)
+    count = steps * n_ref.shape[0]
     size_y, size_x = s_ref.shape
 
     @pl.when(k == 0)
     def _():
         t_ref[...] = jnp.zeros_like(t_ref)
 
-    for start in range(0, size_y, 64):
-        part = pl.ds(start, min(64, size_y - start))
-        moved = [n_ref[0, c, part, :] for c in range(3)]
+    for start in range(0, size_y, 32):
+        part = pl.ds(start, min(32, size_y - start))
+        moved = [[n_ref[f, c, part, :] for c in range(3)] for f in range(n_ref.shape[0])]
         for p, (i, j) in enumerate(PAIRS):
-            t_ref[p, part, :] += moved[i] * moved[j]
-
-    @pl.when(k == count - 1)
+            value = moved[0][i] * moved[0][j]
+            for own in moved[1:]:
+                value += own[i] * own[j]
+            t_ref[p, part, :] += value
+
+    @pl.when(k == steps - 1)
     def _():
         for start in range(0, size_y, 64):
             part = pl.ds(start, min(64, size_y - start))
@@ -236,9 +253,9 @@
     whole = pl.BlockSpec(memory_space=pltpu.VMEM)
     message = pl.pallas_call(
         plane_kernel,
-        grid=(count,),
+        grid=(2,),
         in_specs=[
-            pl.BlockSpec((1, 3, size_y, size_x), lambda k: (k, 0, 0, 0)),
+            pl.BlockSpec((count // 2, 3, size_y, size_x), lambda k: (k, 0, 0, 0)),
             whole,
             whole,
             whole,
@@ -312,7 +329,7 @@
     )(spectra, damping, last_damping, forward, forward_slope, inverse, slab_inverse)
 
 
-def slab_kernel(r_ref, l_ref, t_ref, c_ref, x_ref, v_ref, g_ref):
+def slab_kernel(r_ref, l_ref, t_ref, c_ref, x_ref, b_ref, v_ref, g_ref):
     i = pl.program_id(0)
     rows = r_ref.shape[0]
     _, size_y, slab, size_x = v_ref.shape
@@ -356,15 +373,15 @@
             out_v[place, :] = both[:size_y, :size_x]
             out_g[0, place, :] = both[:size_y, size_x:]
             both = jnp.dot(
-                three_of(jnp.concatenate([value_z[half:], slope_z], axis=0), 1),
-                x_ref[:, :size_x],
+                jnp.concatenate([three_of(value_z[half:], 1), three_of(slope_z, 1)], axis=1),
+                b_ref[...],
                 preferred_element_type=jnp.float32,
             )
-            out_g[1, place, :] = both[:size_y]
-            out_g[2, place, :] = both[half : half + size_y]
-
-
-def slab_values(rows, last, wall_table, last_column, table_x, size_y):
+            out_g[1, place, :] = both[:size_y, :size_x]
+            out_g[2, place, :] = both[:size_y, size_x:]
+
+
+def slab_values(rows, last, wall_table, last_column, table_x, table_pair, size_y):
     count = rows.shape[0]
     slab, size_x = rows.shape[3], table_x.shape[1] // 2
     whole = pl.BlockSpec(memory_space=pltpu.VMEM)
@@ -374,6 +391,7 @@
         grid=(3,),
         in_specs=[
             pl.BlockSpec((count, 1, 3, slab, 128), lambda i: (0, i, 0, 0, 0)),
+            whole,
             whole,
             whole,
             whole,
@@ -388,7 +406,7 @@
             jax.ShapeDtypeStruct((9, size_y, slab, size_x), jnp.float32),
         ),
         compiler_params=pltpu.CompilerParams(vmem_limit_bytes=60 * 1024 * 1024),
-    )(rows, last, wall_table, last_column, table_x)
+    )(rows, last, wall_table, last_column, table_x, table_pair)
 
 
 def summed(planes, early, rest):
@@ -412,50 +430,10 @@
     pairs = [(i, (i + ring) % count) for i in range(count)]
     total = total + lax.ppermute(total, "sample", pairs)
     total, beside = lax.optimization_barrier((total, rest(early)))
-    return place, [total] + [shifted(total, k) for k in range(1, ring)], beside
-
-
-def finish_kernel(relax, samples, at_ref, *refs):
-    *quarters, a_ref, f_ref, o_ref, s_ref = refs
-    for k, quarter in enumerate(quarters):
-
-        @pl.when(pl.program_id(0) == k)
-        def _(quarter=quarter):
-            for j in range(quarter.shape[0]):
-                spring = 1.0 / (1.0 - quarter[j] / samples / EXTENSIBILITY)
-                s_ref[j] = spring
-                scale = relax * spring
-                for c in range(3):
-                    o_ref[j, c] = a_ref[j, c] - scale * f_ref[j, c]
-
-
-def finished(place, quarters, free, planes, relax, samples):
-    slab, _, size_y, size_x = planes.shape
-    ring = len(quarters)
-    part = slab // ring
-    whole = pl.BlockSpec(memory_space=pltpu.VMEM)
-
-    def quarter(k, at):
-        return lax.rem(at[0] + ring - k, ring)
-
-    each = pl.BlockSpec((part, 3, size_y, size_x), lambda k, at: (quarter(k, at), 0, 0, 0))
-    return pl.pallas_call(
-        functools.partial(finish_kernel, relax, samples),
-        grid_spec=pltpu.PrefetchScalarGridSpec(
-            num_scalar_prefetch=1,
-            grid=(ring,),
-            in_specs=[whole] * ring + [each, each],
-            out_specs=(
-                each,
-                pl.BlockSpec((part, size_y, size_x), lambda k, at: (quarter(k, at), 0, 0)),
-            ),
-        ),
-        out_shape=(
-            pltpu.HBM(planes.shape, jnp.float32),
-            jax.ShapeDtypeStruct((slab, size_y, size_x), jnp.float32),
-        ),
-        compiler_params=pltpu.CompilerParams(vmem_limit_bytes=60 * 1024 * 1024),
-    )(jnp.reshape(place, (1,)).astype(jnp.int32), *quarters, free, planes)
+    parts = [shifted(total, k) for k in range(ring - 1, 0, -1)] + [total]
+    start = (ring - 1 - place) % ring
+    gathered = lax.dynamic_slice_in_dim(jnp.stack(parts + parts), start, ring, axis=0)
+    return gathered.reshape(planes.shape), beside
 
 
 def on_device(
@@ -480,7 +458,6 @@
     below = lax.ppermute(field[-1], "span", ahead)
     above = lax.ppermute(field[0], "span", back)
     speed = jnp.transpose(velocity, (0, 3, 2, 1))
-
     def rest(slope):
         return spring_free(
             field,
@@ -495,8 +472,9 @@
         )
 
     slope = wall_slope(field, wall_derivative)
-    place, quarters, free = summed(jnp.sum(field * field, axis=1), slope, rest)
-    new_fields, slab_spring = finished(place, quarters, free, field, relax, samples)
+    total_square, free = summed(jnp.sum(field * field, axis=1), slope, rest)
+    slab_spring = 1.0 / (1.0 - total_square / samples / EXTENSIBILITY)
+    new_fields = free - relax * slab_spring[:, None] * field
     moved = lax.all_to_all(new_fields, "sample", 0, 0, tiled=True)
 
     own_velocity = lax.dynamic_index_in_dim(
@@ -554,6 +532,7 @@
         split_three(wall_table.at[:, size_y - 1].set(0.0), 1),
         wall_table[:, size_y - 1 : size_y],
         stacked_three(np.concatenate([rows_x, (rows_x.T @ slope_rows_x).T], axis=1)),
+        paired_three(rows_x),
         size_y,
     )
     return (

time: 209 us -> 202 us (0.967)
  Pallas kernels: 38.8 us -> 33.3 us
  starting transfers between devices: 38.8 us -> 35.2 us
  other arithmetic: 7.31 us -> 9.52 us
    pallas_call x2 -> x1, Pallas kernels: 9.9 us -> 4.76 us  [own_plane(): pl.pallas_call(plane_kernel, grid=(2,), in_specs=[pl.BlockSpec((count //...]
    all_to_all x1, starting transfers between devices: 12.9 us -> 8.7 us  [on_device(): spectra = lax.all_to_all(message, BOTH, 0, 0, tiled=True)]
    unnamed x46 -> x51, local copies, waits for them, and re-layouts: 5.42 us -> 6.99 us
  transfers between devices with their start and end apart: 12 -> 12, of which waited for: 6 -> 7; matrix products, arithmetic and copies ran while one was open for 8% -> 7% of each run, Pallas kernels for 6% -> 6%
where the time goes in v8:
time: 202 us; the launch traced here: 201 us
  waiting for transfers between devices  107 us (53%)
  starting transfers between devices  35.2 us (17%)
  Pallas kernels  33.3 us (16%)
  local copies, waits for them, and re-layouts  12.6 us (6%)
  other arithmetic  9.52 us (5%)
  matrix products  2.05 us (1%)
    all_to_all x1, waiting for transfers between devices, on_device(): rows = lax.all_to_all(back, BOTH, 0, 0, tiled=True)  54.5 us
    all_to_all x1, waiting for transfers between devices, on_device(): moved = lax.all_to_all(new_fields, 'sample', 0, 0, tiled=True)  27.2 us
    all_to_all x1, waiting for transfers between devices, on_device(): spectra = lax.all_to_all(message, BOTH, 0, 0, tiled=True)  14.3 us
    pallas_call x1, Pallas kernels, slab_values(): pl.pallas_call(slab_kernel, grid=(3,), in_specs=[pl.BlockSpec((count, 1,...  12.2 us
    ppermute x6, waiting for transfers between devices, shifted(): return lax.ppermute(values, 'sample', pairs)  11.2 us
    pallas_call x1, Pallas kernels, spring_free(): pl.pallas_call(functools.partial(free_kernel, scales), grid=(-(-size_y //...  9.75 us
    ppermute x6, starting transfers between devices, shifted(): return lax.ppermute(values, 'sample', pairs)  9.2 us
    all_to_all x1, starting transfers between devices, on_device(): spectra = lax.all_to_all(message, BOTH, 0, 0, tiled=True)  8.7 us
  transfers between devices with their start and end apart: 12, of which 7 were waited for; matrix products, arithmetic and copies ran while one was open for 7% of the time, Pallas kernels for 6%

profile of v8, /device:TPU:5, one launch (start us, length us, event | category | flops | bytes accessed | tf_op | source)
XLA Modules:
  0.0 200.9 jit_solution(17885105574493038221)
XLA Ops:
  0.6 2.2 %multiply_reduce_fusion = f32[8,193,128]{2,1,0:T(8,128)S(1)} fusion(f32[3,1,128,8,193]{2,3,4,1,0:T(8,128)} %param.21), kind=kLoop, calls=%fused_computation.2 | loop fusion | flops 988160 | bytes 3162112 | tf_op jit(solution)/shard_map/reduce_sum | solution.py:475
  4.4 2.6 %collective-permute-start.1 = (f32[2,193,128]{2,1,0:T(8,128)S(1)}, f32[2,193,128]{2,1,0:T(8,128)S(1)}, u32[]{:S(2)}, u32[]{:S(2)}) collective-permute-start(f32[2,193,128]{2,1,0:T(8,128)S(1)} %get-tuple-element.37), channel_id=1, source_target_pairs={{0,32},{16,48},{32,0},{48,16},{64,96},{80,112},{96,64},{112,80},{1... | collective-permute-start | bytes 592904 | tf_op jit(solution)/shard_map/ppermute | solution.py:421
  8.6 1.6 collective-permute-start.5
  10.2 1.6 collective-permute-start.4
  11.8 3.0 %shard_map.202.s_ref = f32[8,3,193,128]{3,2,1,0:T(8,128)} custom-call(f32[8,3,193,128]{3,2,1,0:T(8,128)S(1)} %bitcast.75, bf16[193,193]{1,0:T(8,128)(2,1)S(1)} %get-tuple-element.46.d_ref, bf16[193,193]{1,0:T(8,128)(2,1)S(1)} %get-tuple-element.45.e_ref), custom_call_target="tpu_custom_call" | custom-call | flops 1000000000 | bytes 6000000 | tf_op jit(solution)/shard_map/pallas_call | solution.py:71
  15.9 3.7 %collective-permute-start.3 = (f32[2,193,128]{2,1,0:T(8,128)S(1)}, f32[2,193,128]{2,1,0:T(8,128)S(1)}, u32[]{:S(2)}, u32[]{:S(2)}) collective-permute-start(f32[2,193,128]{2,1,0:T(8,128)S(1)} %fusion.7), channel_id=1, source_target_pairs={{0,64},{16,80},{32,96},{48,112},{64,0},{80,16},{96,32},{112,48},{1... | collective-permute-start | bytes 592904 | tf_op jit(solution)/shard_map/ppermute | solution.py:431
  20.4 9.7 %shard_map.203 = f32[8,3,193,128]{3,2,1,0:T(8,128)} custom-call(f32[8,3,193,128]{3,2,1,0:T(8,128)} %bitcast.76, f32[8,3,193,128]{3,2,1,0:T(8,128)} %shard_map.202.s_ref, f32[3,193,8,128]{3,2,1,0:T(8,128)} %bitcast.82, f32[3,193,8,128]{3,2,1,0:T(8,128)} %bitcast.81, f32[9,193,8,128]{3,2,1,0:T(8,128)} %bitcast.78, f32[3,193,128]{2,1,0:T(8,128)} %copy-done.17, ...), custom_call_target="tpu_custom_call" | custom-call | flops 100000000 | bytes 19000000 | tf_op jit(solution)/shard_map/pallas_call | solution.py:127
  30.2 2.9 %collective-permute-start.6 = (f32[2,193,128]{2,1,0:T(8,128)S(1)}, f32[2,193,128]{2,1,0:T(8,128)S(1)}, u32[]{:S(2)}, u32[]{:S(2)}) collective-permute-start(f32[2,193,128]{2,1,0:T(8,128)S(1)} %add.112), channel_id=1, source_target_pairs={{0,48},{16,0},{32,16},{48,32},{64,112},{80,64},{96,80},{112,96},{1... | collective-permute-start | bytes 592904 | tf_op jit(solution)/shard_map/ppermute | solution.py:421
  34.4 2.2 %collective-permute-done.6 = f32[2,193,128]{2,1,0:T(8,128)S(1)} collective-permute-done((f32[2,193,128]{2,1,0:T(8,128)S(1)}, f32[2,193,128]{2,1,0:T(8,128)S(1)}, u32[]{:S(2)}, u32[]{:S(2)}) %collective-permute-start.6) | collective-permute-done | bytes 197664 | tf_op jit(solution)/shard_map/ppermute | solution.py:421
  36.6 5.2 %collective-permute-done.7 = f32[2,193,128]{2,1,0:T(8,128)S(1)} collective-permute-done((f32[2,193,128]{2,1,0:T(8,128)S(1)}, f32[2,193,128]{2,1,0:T(8,128)S(1)}, u32[]{:S(2)}, u32[]{:S(2)}) %collective-permute-start.7) | collective-permute-done | bytes 197664 | tf_op jit(solution)/shard_map/ppermute | solution.py:421
  41.8 2.7 %collective-permute-done.8 = f32[2,193,128]{2,1,0:T(8,128)S(1)} collective-permute-done((f32[2,193,128]{2,1,0:T(8,128)S(1)}, f32[2,193,128]{2,1,0:T(8,128)S(1)}, u32[]{:S(2)}, u32[]{:S(2)}) %collective-permute-start.8) | collective-permute-done | bytes 197664 | tf_op jit(solution)/shard_map/ppermute | solution.py:421
  46.7 2.0 multiply_subtract_fusion
  48.7 3.8 %all-to-all-start = ((f32[8,3,193,128]{3,2,1,0:T(8,128)}), f32[8,3,193,128]{3,2,1,0:T(8,128)S(1)}, u32[]{:S(2)}, u32[]{:S(2)}) async-start(f32[8,3,193,128]{3,2,1,0:T(8,128)} %multiply_subtract_fusion), calls=%async_computation | async-start | bytes 4915200 | tf_op jit(solution)/shard_map/all_to_all | solution.py:478
  52.5 1.9 constant_dynamic-slice_fusion
  57.6 27.2 %all-to-all-done.n_ref = f32[8,3,193,128]{3,2,1,0:T(8,128)S(1)} async-done(((f32[8,3,193,128]{3,2,1,0:T(8,128)}), f32[8,3,193,128]{3,2,1,0:T(8,128)S(1)}, u32[]{:S(2)}, u32[]{:S(2)}) %all-to-all-start) | async-done | bytes 2371616 | tf_op jit(solution)/shard_map/all_to_all | solution.py:478
  85.8 4.8 %shard_map.204 = f32[2048,128]{1,0:T(8,128)} custom-call(f32[8,3,193,128]{3,2,1,0:T(8,128)S(1)} %all-to-all-done.n_ref, f32[193,128]{1,0:T(8,128)S(1)} %dynamic-slice_bitcast_fusion.s_ref, f32[3,256,128]{2,1,0:T(8,128)S(1)} %copy-done.1, bf16[512,768]{1,0:T(8,128)(2,1)S(1)} %pad_maximum_fusion.m_ref, f32[128,256]{1,0:T(8,128)S(1)} %copy-done.3), custom_call_target="tpu_custom_call" | custom-call | tf_op jit(solution)/shard_map/pallas_call | solution.py:254
  90.6 8.7 %all-to-all-start.1 = ((f32[128,2,8,128]{3,2,1,0:T(8,128)}), f32[128,2,8,128]{3,2,1,0:T(8,128)S(1)}, u32[]{:S(2)}, u32[]{:S(2)}) async-start(f32[128,2,8,128]{3,2,1,0:T(8,128)} %bitcast.26), calls=%async_computation.1 | async-start | bytes 2097152 | tf_op jit(solution)/shard_map/all_to_all | solution.py:497
  102.7 14.3 %all-to-all-done.1.in_ref = f32[128,2,8,128]{3,2,1,0:T(8,128)S(1)} async-done(((f32[128,2,8,128]{3,2,1,0:T(8,128)}), f32[128,2,8,128]{3,2,1,0:T(8,128)S(1)}, u32[]{:S(2)}, u32[]{:S(2)}) %all-to-all-start.1) | async-done | bytes 1048608 | tf_op jit(solution)/shard_map/all_to_all | solution.py:497
  117.0 3.6 %shard_map.205 = (f32[128,3,3,8,128]{4,3,2,1,0:T(8,128)}, f32[6,8,128]{2,1,0:T(8,128)S(1)}) custom-call(f32[128,2,8,128]{3,2,1,0:T(8,128)S(1)} %all-to-all-done.1.in_ref, f32[128,256]{1,0:T(8,128)S(1)} %multiply_add_fusion.d_ref, f32[128,128]{1,0:T(8,128)S(1)} %multiply_add_fusion.1.e_ref, f32[128,128]{1,0:T(8,128)S(1)} %copy-done.5, ...), custom_call_target="tpu_custom_call" | custom-call | tf_op jit(solution)/shard_map/pallas_call | solution.py:316
  121.2 6.7 %all-to-all-start.2 = ((f32[128,3,3,8,128]{4,3,2,1,0:T(8,128)}), f32[128,3,3,8,128]{4,3,2,1,0:T(8,128)}, u32[]{:S(2)}, u32[]{:S(2)}) async-start(f32[128,3,3,8,128]{4,3,2,1,0:T(8,128)} %get-tuple-element.27), calls=%async_computation.2 | async-start | bytes 9437184 | tf_op jit(solution)/shard_map/all_to_all | solution.py:523
  129.0 1.6 fusion.10
  132.4 1.8 copy.27
  134.3 54.5 %all-to-all-done.2.r_ref = f32[128,3,3,8,128]{4,3,2,1,0:T(8,128)} async-done(((f32[128,3,3,8,128]{4,3,2,1,0:T(8,128)}), f32[128,3,3,8,128]{4,3,2,1,0:T(8,128)}, u32[]{:S(2)}, u32[]{:S(2)}) %all-to-all-start.2) | async-done | bytes 4718624 | tf_op jit(solution)/shard_map/all_to_all | solution.py:523
  188.8 12.2 %shard_map.206 = (f32[3,193,8,128]{3,2,1,0:T(8,128)}, f32[9,193,8,128]{3,2,1,0:T(8,128)}) custom-call(f32[128,3,3,8,128]{4,3,2,1,0:T(8,128)} %all-to-all-done.2.r_ref, f32[6,8,128]{2,1,0:T(8,128)} %copy-done.6, bf16[416,768]{1,0:T(8,128)(2,1)} %pad_maximum_fusion.1.t_ref, f32[416,1]{1,0:T(8,128)} %get-tuple-element.41.c_ref, ...), custom_call_target="tpu_custom_call" | custom-call | tf_op jit(solution)/shard_map/pallas_call | solution.py:389
  (88 shorter events, 19.5 us)
Async XLA Ops:
  2.8 5.3 %copy-start.8 = (f32[3,1,128,8,193]{2,3,4,1,0:T(8,128)S(1)}, f32[3,1,128,8,193]{2,3,4,1,0:T(8,128)}, u32[]{:S(2)}) copy-start(f32[3,1,128,8,193]{2,3,4,1,0:T(8,128)} %param.21) | copy-start | bytes 7114756
  3.0 11.8 %collective-permute-start = (f32[2,193,128]{2,1,0:T(8,128)S(1)}, f32[2,193,128]{2,1,0:T(8,128)S(1)}, u32[]{:S(2)}, u32[]{:S(2)}) collective-permute-start(f32[2,193,128]{2,1,0:T(8,128)S(1)} %get-tuple-element.36), channel_id=1, source_target_pairs={{0,16},{16,32},{32,48},{48,0},{64,80},{80,96},{96,112},{112,64},{1... | collective-permute-start | bytes 592904 | tf_op jit(solution)/shard_map/ppermute | solution.py:421
  4.4 11.5 %collective-permute-start.1 = (f32[2,193,128]{2,1,0:T(8,128)S(1)}, f32[2,193,128]{2,1,0:T(8,128)S(1)}, u32[]{:S(2)}, u32[]{:S(2)}) collective-permute-start(f32[2,193,128]{2,1,0:T(8,128)S(1)} %get-tuple-element.37), channel_id=1, source_target_pairs={{0,32},{16,48},{32,0},{48,16},{64,96},{80,112},{96,64},{112,80},{1... | collective-permute-start | bytes 592904 | tf_op jit(solution)/shard_map/ppermute | solution.py:421
  7.0 4.8 %copy-start.13 = (f32[193,193]{1,0:T(8,128)S(1)}, f32[193,193]{1,0:T(8,128)}, u32[]{:S(2)}) copy-start(f32[193,193]{1,0:T(8,128)} %param.25) | copy-start | bytes 446992
  7.0 8.9 %collective-permute-start.2 = (f32[2,193,128]{2,1,0:T(8,128)S(1)}, f32[2,193,128]{2,1,0:T(8,128)S(1)}, u32[]{:S(2)}, u32[]{:S(2)}) collective-permute-start(f32[2,193,128]{2,1,0:T(8,128)S(1)} %get-tuple-element.38), channel_id=1, source_target_pairs={{0,48},{16,0},{32,16},{48,32},{64,112},{80,64},{96,80},{112,96},{1... | collective-permute-start | bytes 592904 | tf_op jit(solution)/shard_map/ppermute | solution.py:421
  8.6 6.3 %copy-start = (f32[3,1,128,8,193]{2,4,0,3,1:T(8,128)}, f32[3,1,128,8,193]{2,4,0,3,1:T(8,128)S(1)}, u32[]{:S(2)}) copy-start(f32[3,1,128,8,193]{2,4,0,3,1:T(8,128)S(1)} %copy.40) | copy-start | bytes 7114756
  8.6 11.0 %collective-permute-start.5 = (f32[3,193,128]{2,1,0:T(8,128)S(1)}, f32[3,193,128]{2,1,0:T(8,128)S(1)}, u32[]{:S(2)}, u32[]{:S(2)}) collective-permute-start(f32[3,193,128]{2,1,0:T(8,128)S(1)} %get-tuple-element.34), channel_id=1, source_target_pairs={{1,0},{2,1},{3,2},{4,3},{5,4},{6,5},{7,6},{8,7},{9,8},{10,9},{11,1... | collective-permute-start | bytes 889352 | tf_op jit(solution)/shard_map/ppermute | solution.py:459
  10.2 9.4 %collective-permute-start.4 = (f32[3,193,128]{2,1,0:T(8,128)S(1)}, f32[3,193,128]{2,1,0:T(8,128)S(1)}, u32[]{:S(2)}, u32[]{:S(2)}) collective-permute-start(f32[3,193,128]{2,1,0:T(8,128)S(1)} %get-tuple-element.35), channel_id=1, source_target_pairs={{0,1},{1,2},{2,3},{3,4},{4,5},{5,6},{6,7},{7,8},{8,9},{9,10},{10,1... | collective-permute-start | bytes 889352 | tf_op jit(solution)/shard_map/ppermute | solution.py:458
  15.9 14.2 %collective-permute-start.3 = (f32[2,193,128]{2,1,0:T(8,128)S(1)}, f32[2,193,128]{2,1,0:T(8,128)S(1)}, u32[]{:S(2)}, u32[]{:S(2)}) collective-permute-start(f32[2,193,128]{2,1,0:T(8,128)S(1)} %fusion.7), channel_id=1, source_target_pairs={{0,64},{16,80},{32,96},{48,112},{64,0},{80,16},{96,32},{112,48},{1... | collective-permute-start | bytes 592904 | tf_op jit(solution)/shard_map/ppermute | solution.py:431
  30.2 6.3 %collective-permute-start.6 = (f32[2,193,128]{2,1,0:T(8,128)S(1)}, f32[2,193,128]{2,1,0:T(8,128)S(1)}, u32[]{:S(2)}, u32[]{:S(2)}) collective-permute-start(f32[2,193,128]{2,1,0:T(8,128)S(1)} %add.112), channel_id=1, source_target_pairs={{0,48},{16,0},{32,16},{48,32},{64,112},{80,64},{96,80},{112,96},{1... | collective-permute-start | bytes 592904 | tf_op jit(solution)/shard_map/ppermute | solution.py:421
  33.1 11.5 %collective-permute-start.8 = (f32[2,193,128]{2,1,0:T(8,128)S(1)}, f32[2,193,128]{2,1,0:T(8,128)S(1)}, u32[]{:S(2)}, u32[]{:S(2)}) collective-permute-start(f32[2,193,128]{2,1,0:T(8,128)S(1)} %add.112), channel_id=1, source_target_pairs={{0,16},{16,32},{32,48},{48,0},{64,80},{80,96},{96,112},{112,64},{1... | collective-permute-start | bytes 592904 | tf_op jit(solution)/shard_map/ppermute | solution.py:421
  33.1 8.7 %collective-permute-start.7 = (f32[2,193,128]{2,1,0:T(8,128)S(1)}, f32[2,193,128]{2,1,0:T(8,128)S(1)}, u32[]{:S(2)}, u32[]{:S(2)}) collective-permute-start(f32[2,193,128]{2,1,0:T(8,128)S(1)} %add.112), channel_id=1, source_target_pairs={{0,32},{16,48},{32,0},{48,16},{64,96},{80,112},{96,64},{112,80},{1... | collective-permute-start | bytes 592904 | tf_op jit(solution)/shard_map/ppermute | solution.py:421
  48.7 36.1 %all-to-all-start = ((f32[8,3,193,128]{3,2,1,0:T(8,128)}), f32[8,3,193,128]{3,2,1,0:T(8,128)S(1)}, u32[]{:S(2)}, u32[]{:S(2)}) async-start(f32[8,3,193,128]{3,2,1,0:T(8,128)} %multiply_subtract_fusion), calls=%async_computation | async-start | bytes 4915200 | tf_op jit(solution)/shard_map/all_to_all | solution.py:478
  54.8 30.0 %copy-start.3 = (f32[128,256]{1,0:T(8,128)S(1)}, f32[128,256]{1,0:T(8,128)}, u32[]{:S(2)}) copy-start(f32[128,256]{1,0:T(8,128)} %constant.119.clone.x_ref) | copy-start | bytes 393220
  90.5 8.8 %copy-start.18 = (f32[193]{0:T(256)S(1)}, f32[193]{0:T(256)}, u32[]{:S(2)}) copy-start(f32[193]{0:T(256)} %param.28) | copy-start | bytes 2320
  90.5 9.3 %copy-start.19 = (f32[128]{0:T(128)S(1)}, f32[128]{0:T(128)}, u32[]{:S(2)}) copy-start(f32[128]{0:T(128)} %constant.120.clone) | copy-start | bytes 1540
  90.5 10.6 %copy-start.20 = (f32[128]{0:T(128)S(1)}, f32[128]{0:T(128)}, u32[]{:S(2)}) copy-start(f32[128]{0:T(128)} %constant.121.clone) | copy-start | bytes 1540
  90.5 26.4 %copy-start.2 = (f32[256,128]{1,0:T(8,128)S(1)}, f32[256,128]{1,0:T(8,128)}, u32[]{:S(2)}) copy-start(f32[256,128]{1,0:T(8,128)} %constant.125.clone.b_ref) | copy-start | bytes 393220
  90.6 26.4 %copy-start.4 = (f32[128,128]{1,0:T(8,128)S(1)}, f32[128,128]{1,0:T(8,128)}, u32[]{:S(2)}) copy-start(f32[128,128]{1,0:T(8,128)} %constant.124.clone.g_ref) | copy-start | bytes 196612
  90.6 26.4 %copy-start.5 = (f32[128,128]{1,0:T(8,128)S(1)}, f32[128,128]{1,0:T(8,128)}, u32[]{:S(2)}) copy-start(f32[128,128]{1,0:T(8,128)} %constant.123.clone.f_ref) | copy-start | bytes 196612
  90.6 26.4 %all-to-all-start.1 = ((f32[128,2,8,128]{3,2,1,0:T(8,128)}), f32[128,2,8,128]{3,2,1,0:T(8,128)S(1)}, u32[]{:S(2)}, u32[]{:S(2)}) async-start(f32[128,2,8,128]{3,2,1,0:T(8,128)} %bitcast.26), calls=%async_computation.1 | async-start | bytes 2097152 | tf_op jit(solution)/shard_map/all_to_all | solution.py:497
  121.2 7.3 %copy-start.14 = (f32[193,193]{1,0:T(8,128)S(1)}, f32[193,193]{1,0:T(8,128)}, u32[]{:S(2)}) copy-start(f32[193,193]{1,0:T(8,128)} %param.25) | copy-start | bytes 446992
  121.2 7.4 %copy-start.15 = (f32[193,193]{1,0:T(8,128)S(1)}, f32[193,193]{1,0:T(8,128)}, u32[]{:S(2)}) copy-start(f32[193,193]{1,0:T(8,128)} %param.27) | copy-start | bytes 446992
  121.2 67.6 %all-to-all-start.2 = ((f32[128,3,3,8,128]{4,3,2,1,0:T(8,128)}), f32[128,3,3,8,128]{4,3,2,1,0:T(8,128)}, u32[]{:S(2)}, u32[]{:S(2)}) async-start(f32[128,3,3,8,128]{4,3,2,1,0:T(8,128)} %get-tuple-element.27), calls=%async_computation.2 | async-start | bytes 9437184 | tf_op jit(solution)/shard_map/all_to_all | solution.py:523
  (9 other events, 14.2 us)
